TPU v7x, 1024 devices: a whole 4x4x32 slice. The times are simulated.
1024 devices in a mesh: dp: 8 (over x, core), expert: 32 (over y, z_lo), tensor: 4 (over z_hi).
Axes of the slice: x: 4, y: 4, z: 32 (z_hi: 4, z_lo: 8; z = z_hi * 8 + z_lo), core: 2. Of those that a mesh axis runs over, the one named last changes fastest.
Arguments:
- cotangent: bfloat16 [14336, 4096], P(('dp', 'expert', 'tensor')), may hold values from -6 to 6
- probs: float32 [14336, 2], P(('dp', 'expert', 'tensor')), may hold values from 0.1 to 1
- expert_ids: int32 [14336, 2], P(('dp', 'expert')), may hold values from 0 to 15, all different within a row; in each aligned block of 56 rows (0 to 55, 56 to 111, ...) at most 8 rows name the same one
- saved_hidden: bfloat16 [2048, 51200], P('dp', ('expert', 'tensor')), may hold values from -0.29882812 to 0.29882812
- down_weight: bfloat16 [4096, 51200], P(None, ('expert', 'tensor')), may hold values from -0.09375 to 0.09375
Outputs:
- hidden_grad: bfloat16 [2048, 51200], P('dp', ('expert', 'tensor'))
- weight_grad: bfloat16 [4096, 51200], P('dp', ('expert', 'tensor'))
- prob_grad: float32 [14336, 2], P(('dp', 'expert', 'tensor'))
Inputs may be any that keep to these rules, and one draw needn't show every extreme that they name: `expert_ids`: in each aligned block of 56 rows (one token group) no expert is named by more than 8 rows, a bound that some block reaches; the two ids of a row differ.
All inputs are finite; a program needn't handle non-finite values.
Results may differ from a plain program's by a relative error of at most 0.017.
Values may be sent and summed in bfloat16 or wider, within the bound.
No kernel may reach another device: no remote copies, remote signals or barrier semaphores. Data moves between devices by JAX's collectives and lax.ppermute only.
A program may use at most 32 MiB of HBM per device.

v0:
```python
import jax
import jax.numpy as jnp
from jax import lax
from jax.sharding import PartitionSpec as P


def assign_slots(flat_ids, experts):
    expert_range = jnp.arange(experts, dtype=jnp.int32)
    onehot = (flat_ids[:, None] == expert_range[None, :]).astype(jnp.int32)
    earlier = jnp.cumsum(onehot, axis=0) - onehot
    return jnp.sum(earlier * onehot, axis=1)


def build_buffer(gathered, flat_ids, slot_ids, n_expert, per_device):
    row_index = jnp.arange(n_expert * per_device, dtype=jnp.int32)
    destination = row_index // per_device
    offset = row_index % per_device
    wanted_expert = destination // 2
    selector = (
        (flat_ids[None, :] == wanted_expert[:, None]) & (slot_ids[None, :] == offset[:, None])
    ).astype(jnp.bfloat16)
    filled = jnp.dot(selector, gathered, preferred_element_type=jnp.float32).astype(jnp.bfloat16)
    return filled.reshape(n_expert, per_device, gathered.shape[1])


def shards(cotangent, probs, expert_ids, saved_hidden, down_weight):
    n_expert = lax.axis_size("expert")
    own_tokens = cotangent.shape[0]
    model_width = cotangent.shape[1]
    hidden_cols = saved_hidden.shape[1]
    capacity = saved_hidden.shape[0] // n_expert
    experts = n_expert // 2
    scaled = (probs[:, :, None] * cotangent.astype(jnp.float32)[:, None, :]).astype(jnp.bfloat16)
    scaled = scaled.reshape(own_tokens * 2, model_width)
    gathered = lax.all_gather(scaled, "tensor", axis=0, tiled=True)
    flat_ids = expert_ids.reshape(-1)
    slot_ids = assign_slots(flat_ids, experts)
    buffer = build_buffer(gathered, flat_ids, slot_ids, n_expert, capacity)
    slot_rows = lax.all_to_all(buffer, "expert", split_axis=0, concat_axis=0, tiled=True)
    slot_rows, product = (
        slot_rows,
        jnp.einsum("jkd,df->jkf", slot_rows, down_weight, preferred_element_type=jnp.float32),
    )
    rows_flat = slot_rows.reshape(-1, model_width)
    product_flat = product.reshape(-1, hidden_cols)
    hidden_grad = product_flat.astype(jnp.bfloat16)
    partial_value = jnp.sum(saved_hidden.astype(jnp.float32) * product_flat, axis=1).reshape(
        n_expert, capacity
    )
    weight_grad = lax.psum_scatter(
        lax.dot_general(
            rows_flat, saved_hidden, (((0,), (0,)), ((), ())), preferred_element_type=jnp.float32
        ).astype(jnp.bfloat16),
        "dp",
        scatter_dimension=0,
        tiled=True,
    )
    returned = lax.all_to_all(partial_value, "expert", split_axis=0, concat_axis=0, tiled=True)
    summed = lax.psum(returned, "tensor")
    lookup = jnp.sum(summed.reshape(experts, 2, capacity), axis=1)
    start_row = lax.axis_index("tensor") * (own_tokens * 2)
    own_ids = lax.dynamic_slice_in_dim(flat_ids, start_row, own_tokens * 2)
    own_slots = lax.dynamic_slice_in_dim(slot_ids, start_row, own_tokens * 2)
    matches = (own_ids[:, None] == jnp.arange(experts, dtype=jnp.int32)[None, :]).astype(
        jnp.float32
    )
    chosen = jnp.dot(matches, lookup, precision=lax.Precision.HIGHEST)
    slot_match = (own_slots[:, None] == jnp.arange(capacity, dtype=jnp.int32)[None, :]).astype(
        jnp.float32
    )
    values = jnp.sum(chosen * slot_match, axis=1).reshape(own_tokens, 2)
    prob_grad = values / probs
    return (hidden_grad, weight_grad, prob_grad)


def solution(mesh):
    in_specs = (
        P(("dp", "expert", "tensor"), None),
        P(("dp", "expert", "tensor"), None),
        P(("dp", "expert"), None),
        P("dp", ("expert", "tensor")),
        P(None, ("expert", "tensor")),
    )
    out_specs = (
        P("dp", ("expert", "tensor")),
        P("dp", ("expert", "tensor")),
        P(("dp", "expert", "tensor"), None),
    )
    return jax.shard_map(shards, mesh=mesh, in_specs=in_specs, out_specs=out_specs, check_vma=False)
```

profile of v0, /device:TPU:6, one launch (start us, length us, event | category | flops | bytes accessed | tf_op | source)
XLA Modules:
  0.0 296.8 jit_solution(9148596051642771054)
XLA Ops:
  7.2 0.0 copy-start
  7.2 0.0 reduce-scatter.2.cloned.1.call-start
  7.2 0.9 copy.21
  8.2 0.1 mul.31
  8.2 0.8 copy.20
  9.0 0.1 eq.34
  9.1 0.1 fusion.16
  9.2 0.2 reduce_window_sum.11
  9.4 0.2 select_reduce_fusion
  9.6 1.9 mul.33
  11.4 2.1 mul.34
  13.6 1.1 fusion.8
  14.7 96.9 %all-gather = bf16[4,28,4096]{2,1,0:T(8,128)(2,1)} all-gather(bf16[1,28,4096]{2,1,0:T(8,128)(2,1)S(1)} %fusion.8), channel_id=1, replica_groups=mesh['dp'=8,'expert'=32,'tensor'=4] {'tensor'}, dimensions={0}, use_global_device_ids=true | all-gather | bytes 1146880 | tf_op jit(solution)/shard_map/all_gather | solution.py:35
  111.6 2.4 reshape.81
  114.0 1.9 fusion
  115.9 0.0 copy-start.2
  115.9 104.1 %all_to_all.17 = bf16[32,8,4096]{2,1,0:T(8,128)(2,1)S(1)} all-to-all(bf16[32,8,4096]{2,1,0:T(8,128)(2,1)S(1)} %fusion), channel_id=1, replica_groups=mesh['dp'=8,'expert'=32,'tensor'=4] {'expert'}, dimensions={0} | all-to-all | bytes 4194304 | tf_op jit(solution)/shard_map/all_to_all | solution.py:39
  220.0 0.0 copy-start.1
  220.0 1.3 copy-done.1
  221.4 0.0 copy-done.2
  221.4 2.7 convolution_convert_fusion
  224.1 0.0 reduce-scatter.2.cloned.1.call-update
  224.1 0.0 copy-done
  224.1 3.7 %fusion.4 = f32[256,400]{1,0:T(8,128)} fusion(bf16[32,8,4096]{2,1,0:T(8,128)(2,1)} %copy-done.1, bf16[4096,400]{0,1:T(8,128)(2,1)S(1)} %copy-done), kind=kOutput, calls=%fused_computation.6 | convolution fusion | flops 838860800 | bytes 5783552 | tf_op jit(solution)/shard_map/jkd,df->jkf/dot_general | solution.py:42
  227.8 2.0 copy.22
  229.8 1.9 multiply_reduce_fusion
  231.6 0.7 all_to_all.12
  232.3 8.9 %all-to-all-start.1 = ((f32[32,1,8]{2,1,0:T(1,128)}), f32[32,1,8]{2,1,0:T(1,128)S(1)}, u32[]{:S(2)}, u32[]{:S(2)}) async-start(f32[32,1,8]{2,1,0:T(1,128)} %bitcast.5), calls=%async_computation.2 | async-start | bytes 32768 | tf_op jit(solution)/shard_map/all_to_all | solution.py:58
  241.2 0.1 dynamic_slice.7
  241.3 0.1 dynamic_slice.6
  241.3 12.3 %all-to-all-done.1 = f32[32,1,8]{2,1,0:T(1,128)S(1)} async-done(((f32[32,1,8]{2,1,0:T(1,128)}), f32[32,1,8]{2,1,0:T(1,128)S(1)}, u32[]{:S(2)}, u32[]{:S(2)}) %all-to-all-start.1) | async-done | bytes 1056 | tf_op jit(solution)/shard_map/all_to_all | solution.py:58
  253.7 35.3 %psum.7 = f32[16,2,8]{2,1,0:T(2,128)S(1)} all-reduce(f32[16,2,8]{2,1,0:T(2,128)S(1)} %bitcast.20), channel_id=1, replica_groups=mesh['dp'=8,'expert'=32,'tensor'=4] {'tensor'}, use_global_device_ids=true, to_apply=%region_4.5 | all-reduce | flops 256 | bytes 2048 | tf_op jit(solution)/shard_map/psum | solution.py:59
  289.0 0.2 fusion.7
  289.2 0.1 reshape.78
  289.3 0.7 copy.26
  290.0 0.0 reduce-scatter.2.cloned.1.call-done
  (3 shorter events, 0.1 us)
Async XLA Ops:
  7.2 217.0 %copy-start = (bf16[4096,400]{0,1:T(8,128)(2,1)S(1)}, bf16[4096,400]{0,1:T(8,128)(2,1)}, u32[]{:S(2)}) copy-start(bf16[4096,400]{0,1:T(8,128)(2,1)} %param.9) | copy-start | bytes 9830404
  7.2 282.8 %reduce-scatter.2.cloned.1.call-start = ((), (), s32[]{:S(2)}) async-start(), calls=%async_computation.3 | async-start | bytes 3686400 | tf_op jit(solution)/shard_map/reduce_scatter | solution.py:50
  115.9 105.5 %copy-start.2 = (bf16[256,400]{0,1:T(8,128)(2,1)S(1)}, bf16[256,400]{0,1:T(8,128)(2,1)}, u32[]{:S(2)}) copy-start(bf16[256,400]{0,1:T(8,128)(2,1)} %param.8) | copy-start | bytes 614404
  220.0 1.4 copy-start.1
  232.3 21.4 %all-to-all-start.1 = ((f32[32,1,8]{2,1,0:T(1,128)}), f32[32,1,8]{2,1,0:T(1,128)S(1)}, u32[]{:S(2)}, u32[]{:S(2)}) async-start(f32[32,1,8]{2,1,0:T(1,128)} %bitcast.5), calls=%async_computation.2 | async-start | bytes 32768 | tf_op jit(solution)/shard_map/all_to_all | solution.py:58
Sparse Core Ops, SparseCore 0:
  224.2 41.8 reduce-scatter.1
where the time goes:
time: 297 us
  blocking collectives  236 us (79%)
  between operations  14.1 us (5%)
  local copies, waits for them, and re-layouts  13.2 us (4%)
  waiting for transfers between devices  12.3 us (4%)
  starting transfers between devices  8.93 us (3%)
  matrix products  8.51 us (3%)
  other arithmetic  3.46 us (1%)
    all_to_all x1, blocking collectives, shards(): lax.all_to_all(buffer, 'expert', split_axis=0, concat_axis=0, tiled=True)  104 us
    all_gather x1, blocking collectives, shards(): gathered = lax.all_gather(scaled, 'tensor', axis=0, tiled=True)  96.9 us
    psum x1, blocking collectives, shards(): summed = lax.psum(returned, 'tensor')  35.3 us
    all_to_all x1, waiting for transfers between devices, shards(): lax.all_to_all(partial_value, 'expert', split_axis=0, concat_axis=0, tile...  12.3 us
    all_to_all x1, starting transfers between devices, shards(): lax.all_to_all(partial_value, 'expert', split_axis=0, concat_axis=0, tile...  8.89 us
    unnamed x10, local copies, waits for them, and re-layouts  6.08 us
  transfers between devices with their start and end apart: 2, of which 1 were waited for; matrix products, arithmetic and copies ran while one was open for 3% of the time, Pallas kernels for 0%

commit v1 on v0

v1 whole, which is shorter than its diff:
```python
import functools

import jax
import jax.numpy as jnp
from jax import lax
from jax.experimental import pallas as pl
from jax.experimental.pallas import tpu as pltpu
from jax.sharding import Mesh, PartitionSpec as P

PAD = 16
LANES = 128


def split3(value):
    high = value.astype(jnp.bfloat16)
    rest = value - high.astype(jnp.float32)
    middle = rest.astype(jnp.bfloat16)
    low = (rest - middle.astype(jnp.float32)).astype(jnp.bfloat16)
    return high, middle, low


def pack_kernel(cot_ref, probs_ref, out_ref):
    own_tokens = cot_ref.shape[0]
    place = lax.axis_index("tensor") * PAD
    lane = lax.broadcasted_iota(jnp.int32, (own_tokens, LANES), 1)
    token = lax.broadcasted_iota(jnp.int32, (own_tokens, LANES), 0)
    here = lane == token + place
    probs = probs_ref[...]
    out_ref[:own_tokens, :] = cot_ref[...]
    out_ref[own_tokens:, :] = jnp.zeros((PAD - own_tokens, cot_ref.shape[1]), jnp.bfloat16)
    rows = []
    for k in range(2):
        spread = jnp.sum(jnp.where(here, probs[:, k : k + 1], 0.0), axis=0, keepdims=True)
        rows.append(jnp.concatenate(split3(spread), axis=1))
    out_ref[own_tokens:, : 3 * LANES] = jnp.concatenate(rows, axis=0)


def fill_kernel(own_tokens, experts, capacity, gathered_ref, ids_ref, out_ref):
    members = gathered_ref.shape[0]
    group = members * own_tokens
    span = members * PAD
    lane = lax.broadcasted_iota(jnp.int32, (group, LANES), 1)
    token = lax.broadcasted_iota(jnp.int32, (group, LANES), 0)
    here = lane == token + (PAD - own_tokens) * (token // own_tokens)
    ids = ids_ref[...]
    lane_row = lax.broadcasted_iota(jnp.int32, (1, LANES), 1)
    real = (lane_row < span) & (lane_row % PAD < own_tokens)
    spread = [
        jnp.where(
            real, jnp.sum(jnp.where(here, ids[:, k : k + 1], 0), axis=0, keepdims=True), -1
        )
        for k in range(2)
    ]
    expert = lax.broadcasted_iota(jnp.int32, (experts, LANES), 0)
    named = [(spread[k] == expert).astype(jnp.float32) for k in range(2)]
    earlier_lane = lax.broadcasted_iota(jnp.int32, (LANES, LANES), 0)
    later_lane = lax.broadcasted_iota(jnp.int32, (LANES, LANES), 1)
    before = (earlier_lane < later_lane).astype(jnp.bfloat16)
    earlier = jnp.dot(
        (named[0] + named[1]).astype(jnp.bfloat16), before, preferred_element_type=jnp.float32
    )
    row = lax.broadcasted_iota(jnp.int32, (experts * capacity, LANES), 0)
    selector = jnp.zeros((experts * capacity, LANES), jnp.float32)
    weight = jnp.zeros((experts * capacity, LANES), jnp.float32)
    for k in range(2):
        count = earlier if k == 0 else earlier + named[0]
        slot = jnp.sum(count * named[k], axis=0, keepdims=True).astype(jnp.int32)
        key = jnp.where(spread[k] >= 0, spread[k] * capacity + slot, -1)
        parts = gathered_ref[:, own_tokens + k : own_tokens + k + 1, : 3 * LANES]
        parts = jnp.sum(parts.astype(jnp.float32), axis=0)
        prob = parts[:, :LANES] + parts[:, LANES : 2 * LANES] + parts[:, 2 * LANES :]
        match = row == key
        selector = jnp.where(match, 1.0, selector)
        weight = jnp.where(match, prob, weight)
    scale = jnp.sum(weight, axis=1, keepdims=True)
    picked = selector[:, :span].astype(jnp.bfloat16)
    step = 512
    for start in range(0, gathered_ref.shape[2], step):
        block = gathered_ref[:, :, start : start + step].reshape(span, step)
        rows = jnp.dot(picked, block, preferred_element_type=jnp.float32)
        out_ref[:, start : start + step] = (rows * scale).astype(jnp.bfloat16)


def assign_slots(flat_ids, experts):
    expert_range = jnp.arange(experts, dtype=jnp.int32)
    onehot = (flat_ids[:, None] == expert_range[None, :]).astype(jnp.int32)
    earlier = jnp.cumsum(onehot, axis=0) - onehot
    return jnp.sum(earlier * onehot, axis=1)


def shards(cotangent, probs, expert_ids, saved_hidden, down_weight):
    n_y, n_q, n_par = lax.axis_size("y"), lax.axis_size("zq"), lax.axis_size("par")
    members = lax.axis_size("tensor")
    n_expert = n_y * n_q * n_par
    experts = n_y * n_q
    own_tokens, model_width = cotangent.shape
    hidden_cols = saved_hidden.shape[1]
    capacity = saved_hidden.shape[0] // n_expert

    packed = pl.pallas_call(
        pack_kernel,
        out_shape=jax.ShapeDtypeStruct((PAD, model_width), jnp.bfloat16),
        compiler_params=pltpu.CompilerParams(vmem_limit_bytes=8 << 20),
    )(cotangent, probs)
    gathered = lax.all_gather(packed, "tensor", axis=0)
    buffer = pl.pallas_call(
        functools.partial(fill_kernel, own_tokens, experts, capacity),
        out_shape=jax.ShapeDtypeStruct((experts * capacity, model_width), jnp.bfloat16),
        compiler_params=pltpu.CompilerParams(vmem_limit_bytes=24 << 20),
    )(gathered, expert_ids)
    buffer = buffer.reshape(experts, capacity, model_width)
    own = lax.all_to_all(buffer, ("y", "zq"), split_axis=0, concat_axis=0, tiled=True)
    other = lax.ppermute(own, "par", [(0, 1), (1, 0)])
    is_even = lax.axis_index("par") == 0
    even = jnp.where(is_even, own, other)
    odd = jnp.where(is_even, other, own)
    rows = jnp.stack([even, odd], axis=1).reshape(n_expert * capacity, model_width)

    weight_grad = lax.psum_scatter(
        lax.dot_general(
            rows, saved_hidden, (((0,), (0,)), ((), ())), preferred_element_type=jnp.float32
        ).astype(jnp.bfloat16),
        "dp",
        scatter_dimension=0,
        tiled=True,
    )
    product = jnp.dot(rows, down_weight, preferred_element_type=jnp.float32)
    hidden_grad = product.astype(jnp.bfloat16)
    partial_value = jnp.sum(saved_hidden.astype(jnp.float32) * product, axis=1).reshape(
        n_expert, capacity
    )
    returned = lax.all_to_all(
        partial_value, ("y", "zq", "par"), split_axis=0, concat_axis=0, tiled=True
    )
    summed = lax.psum(returned, "tensor")
    lookup = jnp.sum(summed.reshape(experts, n_par, capacity), axis=1)
    flat_ids = expert_ids.reshape(-1)
    slot_ids = assign_slots(flat_ids, experts)
    start_row = lax.axis_index("tensor") * (own_tokens * 2)
    own_ids = lax.dynamic_slice_in_dim(flat_ids, start_row, own_tokens * 2)
    own_slots = lax.dynamic_slice_in_dim(slot_ids, start_row, own_tokens * 2)
    matches = (own_ids[:, None] == jnp.arange(experts, dtype=jnp.int32)[None, :]).astype(
        jnp.float32
    )
    chosen = jnp.dot(matches, lookup, precision=lax.Precision.HIGHEST)
    slot_match = (own_slots[:, None] == jnp.arange(capacity, dtype=jnp.int32)[None, :]).astype(
        jnp.float32
    )
    values = jnp.sum(chosen * slot_match, axis=1).reshape(own_tokens, 2)
    prob_grad = values / probs
    return (hidden_grad, weight_grad, prob_grad)


def solution(mesh):
    n_dp, n_expert, n_tensor = mesh.devices.shape
    fine = Mesh(
        mesh.devices.reshape(n_dp, 4, n_expert // 8, 2, n_tensor), ("dp", "y", "zq", "par", "tensor")
    )
    expert = ("y", "zq", "par")
    in_specs = (
        P(("dp",) + expert + ("tensor",), None),
        P(("dp",) + expert + ("tensor",), None),
        P(("dp",) + expert, None),
        P("dp", expert + ("tensor",)),
        P(None, expert + ("tensor",)),
    )
    out_specs = (
        P("dp", expert + ("tensor",)),
        P("dp", expert + ("tensor",)),
        P(("dp",) + expert + ("tensor",), None),
    )
    return jax.shard_map(shards, mesh=fine, in_specs=in_specs, out_specs=out_specs, check_vma=False)
```

time: 297 us -> 231 us (0.78)
  blocking collectives: 236 us -> 154 us
  waiting for transfers between devices: 12.3 us -> 35.2 us
  local copies, waits for them, and re-layouts: 13.2 us -> 5.68 us
    all_to_all x1, blocking collectives: 104 us -> 52.3 us  [shards(): lax.all_to_all(buffer, ('y', 'zq'), split_axis=0, concat_axis=0, tiled=True)]
    all_gather x1, blocking collectives: 96.9 us -> 66.6 us  [shards(): gathered = lax.all_gather(packed, 'tensor', axis=0)]
    ppermute x0 -> x1, waiting for transfers between devices: none -> 23.8 us  [shards(): other = lax.ppermute(own, 'par', [(0, 1), (1, 0)])]
    mul x3 -> x0, local copies, waits for them, and re-layouts: 4.08 us -> none  [shards(): probs[:, :, None] * cotangent.astype(jnp.float32)[:, None, :]]
    dot_general x3 -> x2, matrix products: 8.31 us -> 6.04 us  [the longest x1 3.32 us: shards(): product = jnp.dot(rows, down_weight, preferred_element_type=jnp.float32)]
    unnamed x10 -> x11, local copies, waits for them, and re-layouts: 6.08 us -> 4.63 us
  transfers between devices with their start and end apart: 2 -> 3, of which waited for: 1 -> 2; matrix products, arithmetic and copies ran while one was open for 3% -> 3% of each run, Pallas kernels for 0% -> 0%
where the time goes in v1:
time: 231 us; the launch traced here: 230 us
  blocking collectives  154 us (67%)
  waiting for transfers between devices  35.2 us (15%)
  between operations  14.1 us (6%)
  starting transfers between devices  8.86 us (4%)
  matrix products  6.24 us (3%)
  local copies, waits for them, and re-layouts  5.68 us (2%)
  other arithmetic  5.2 us (2%)
    all_gather x1, blocking collectives, shards(): gathered = lax.all_gather(packed, 'tensor', axis=0)  66.6 us
    all_to_all x1, blocking collectives, shards(): lax.all_to_all(buffer, ('y', 'zq'), split_axis=0, concat_axis=0, tiled=True)  52.3 us
    psum x1, blocking collectives, shards(): summed = lax.psum(returned, 'tensor')  35.1 us
    ppermute x1, waiting for transfers between devices, shards(): other = lax.ppermute(own, 'par', [(0, 1), (1, 0)])  23.8 us
    all_to_all x1, waiting for transfers between devices, shards(): lax.all_to_all(partial_value, ('y', 'zq', 'par'), split_axis=0, concat_ax...  11.3 us
    all_to_all x1, starting transfers between devices, shards(): lax.all_to_all(partial_value, ('y', 'zq', 'par'), split_axis=0, concat_ax...  6.91 us
    unnamed x11, local copies, waits for them, and re-layouts  4.63 us
  transfers between devices with their start and end apart: 3, of which 2 were waited for; matrix products, arithmetic and copies ran while one was open for 3% of the time, Pallas kernels for 0%

profile of v1, /device:TPU:6, one launch (start us, length us, event | category | flops | bytes accessed | tf_op | source)
XLA Modules:
  0.0 230.0 jit_solution(17027916765861326597)
XLA Ops:
  7.2 0.0 copy-start
  7.2 0.0 reduce-scatter.2.cloned.1.call-start
  7.2 0.9 copy.19.probs_ref
  8.1 0.8 copy.20.ids_ref
  8.9 0.0 copy-start.1
  8.9 0.9 copy-done.1
  9.8 0.1 shard_map.76
  9.9 66.6 %all-gather = bf16[64,4096]{1,0:T(8,128)(2,1)S(1)} all-gather(bf16[16,4096]{1,0:T(8,128)(2,1)S(1)} %shard_map.76), channel_id=2, replica_groups=mesh['dp'=8,'y'=4,'zq'=4,'par'=2,'tensor'=4] {'tensor'}, dimensions={0}, use_global_device_ids=true | all-gather | bytes 655360 | tf_op jit(solution)/shard_map/all_gather | solution.py:105
  76.6 0.6 shard_map.77
  77.2 52.3 %all_to_all.17 = bf16[16,8,4096]{2,1,0:T(8,128)(2,1)} all-to-all(bf16[16,8,4096]{2,1,0:T(8,128)(2,1)S(1)} %bitcast.16), channel_id=1, replica_groups=mesh['dp'=8,'y'=4,'zq'=4,'par'=2,'tensor'=4] {'y','zq'}, dimensions={0} | all-to-all | bytes 2097152 | tf_op jit(solution)/shard_map/all_to_all | solution.py:112
  129.6 1.9 collective-permute-start
  131.5 23.8 %collective-permute-done = bf16[16,8,4096]{2,1,0:T(8,128)(2,1)} collective-permute-done((bf16[16,8,4096]{2,1,0:T(8,128)(2,1)}, bf16[16,8,4096]{2,1,0:T(8,128)(2,1)}, u32[]{:S(2)}, u32[]{:S(2)}) %collective-permute-start) | collective-permute-done | bytes 1048608 | tf_op jit(solution)/shard_map/ppermute | solution.py:113
  155.3 1.7 select_bitcast_fusion.1
  157.0 0.0 copy-start.3
  157.0 0.2 pad_maximum_fusion
  157.2 0.0 copy-start.2
  157.2 1.3 copy-done.2
  158.6 0.0 copy-done.3
  158.6 2.7 %convolution_convert_fusion = bf16[4096,400]{0,1:T(8,128)(2,1)} fusion(bf16[256,400]{0,1:T(8,128)(2,1)S(1)} %copy-done.3, bf16[256,4096]{1,0:T(8,128)(2,1)S(1)} %bitcast.18), kind=kOutput, calls=%fused_computation | convolution fusion | flops 840499200 | bytes 5578752 | tf_op jit(solution)/shard_map/dot_general | solution.py:120
  161.3 0.0 reduce-scatter.2.cloned.1.call-update
  161.3 0.1 eq.45
  161.4 0.7 fusion.1
  162.1 1.6 reduce_window_sum.11
  163.7 0.0 copy-done
  163.7 3.3 %multiply_reduce_fusion = (f32[256]{0:T(256)S(1)}, bf16[256,400]{0,1:T(8,128)(2,1)}) fusion(bf16[256,400]{0,1:T(8,128)(2,1)S(1)} %copy-done.3, bf16[256,4096]{1,0:T(8,128)(2,1)} %bitcast.19, bf16[4096,400]{0,1:T(8,128)(2,1)S(1)} %copy-done), kind=kOutput, calls=%fused_computation.6 | convolution fusion | flops 839270144 | bytes 5784576 | tf_op jit(solution)/shard_map/dot_general | solution.py:127
  167.0 0.7 all_to_all.12
  167.7 6.9 %all-to-all-start.1 = ((f32[32,1,8]{2,1,0:T(1,128)}), f32[32,1,8]{2,1,0:T(1,128)S(1)}, u32[]{:S(2)}, u32[]{:S(2)}) async-start(f32[32,1,8]{2,1,0:T(1,128)} %bitcast.6), calls=%async_computation.2 | async-start | bytes 32768 | tf_op jit(solution)/shard_map/all_to_all | solution.py:132
  174.6 1.0 select_reduce_fusion
  175.7 0.1 dynamic_slice.7
  175.7 0.1 dynamic_slice.6
  175.8 11.3 %all-to-all-done.1 = f32[32,1,8]{2,1,0:T(1,128)S(1)} async-done(((f32[32,1,8]{2,1,0:T(1,128)}), f32[32,1,8]{2,1,0:T(1,128)S(1)}, u32[]{:S(2)}, u32[]{:S(2)}) %all-to-all-start.1) | async-done | bytes 1056 | tf_op jit(solution)/shard_map/all_to_all | solution.py:132
  187.1 35.1 %psum.7 = f32[16,2,8]{2,1,0:T(2,128)S(1)} all-reduce(f32[16,2,8]{2,1,0:T(2,128)S(1)} %bitcast.20), channel_id=1, replica_groups=mesh['dp'=8,'y'=4,'zq'=4,'par'=2,'tensor'=4] {'tensor'}, use_global_device_ids=true, to_apply=%region_4.5 | all-reduce | flops 256 | bytes 2048 | tf_op jit(solution)/shard_map/psum | solution.py:135
  222.2 0.2 fusion
  222.4 0.1 reshape.29
  222.5 0.7 copy.25
  223.2 0.0 reduce-scatter.2.cloned.1.call-done
  (2 shorter events, 0.0 us)
Async XLA Ops:
  7.2 156.5 %copy-start = (bf16[4096,400]{0,1:T(8,128)(2,1)S(1)}, bf16[4096,400]{0,1:T(8,128)(2,1)}, u32[]{:S(2)}) copy-start(bf16[4096,400]{0,1:T(8,128)(2,1)} %param.9) | copy-start | bytes 9830404
  7.2 216.0 %reduce-scatter.2.cloned.1.call-start = ((), (), s32[]{:S(2)}) async-start(), calls=%async_computation.3 | async-start | bytes 3686400 | tf_op jit(solution)/shard_map/reduce_scatter | solution.py:119
  8.9 0.9 copy-start.1
  129.6 25.8 %collective-permute-start = (bf16[16,8,4096]{2,1,0:T(8,128)(2,1)}, bf16[16,8,4096]{2,1,0:T(8,128)(2,1)}, u32[]{:S(2)}, u32[]{:S(2)}) collective-permute-start(bf16[16,8,4096]{2,1,0:T(8,128)(2,1)} %all_to_all.17), channel_id=1, source_target_pairs={{0,4},{4,0},{1,5},{5,1},{2,6},{6,2},{3,7},{7,3},{8,12},{12,8},{9,1... | collective-permute-start | bytes 3145736 | tf_op jit(solution)/shard_map/ppermute | solution.py:113
  157.0 1.6 copy-start.3
  157.2 1.4 copy-start.2
  167.7 19.4 %all-to-all-start.1 = ((f32[32,1,8]{2,1,0:T(1,128)}), f32[32,1,8]{2,1,0:T(1,128)S(1)}, u32[]{:S(2)}, u32[]{:S(2)}) async-start(f32[32,1,8]{2,1,0:T(1,128)} %bitcast.6), calls=%async_computation.2 | async-start | bytes 32768 | tf_op jit(solution)/shard_map/all_to_all | solution.py:132
Sparse Core Ops, SparseCore 0:
  161.4 41.5 reduce-scatter.1

commit v2 on v1

--- a/solution.py
+++ b/solution.py
@@ -88,6 +88,21 @@
     return jnp.sum(earlier * onehot, axis=1)
 
 
+def windows(n_dp, n_y, n_q, n_par, n_tensor):
+    groups = []
+    for dp in range(n_dp):
+        for par in range(n_par):
+            for run in range(n_tensor):
+                group = []
+                for y in range(n_y):
+                    for q in range(n_q):
+                        wraps = dp % 2 == 1 and q < n_q // 2
+                        at = (run + 1) % n_tensor if wraps else run
+                        group.append((((dp * n_y + y) * n_q + q) * n_par + par) * n_tensor + at)
+                groups.append(group)
+    return groups
+
+
 def shards(cotangent, probs, expert_ids, saved_hidden, down_weight):
     n_y, n_q, n_par = lax.axis_size("y"), lax.axis_size("zq"), lax.axis_size("par")
     members = lax.axis_size("tensor")
@@ -109,8 +124,20 @@
         compiler_params=pltpu.CompilerParams(vmem_limit_bytes=24 << 20),
     )(gathered, expert_ids)
     buffer = buffer.reshape(experts, capacity, model_width)
-    own = lax.all_to_all(buffer, ("y", "zq"), split_axis=0, concat_axis=0, tiled=True)
+    own = lax.all_to_all(
+        buffer,
+        ("dp", "y", "zq", "par", "tensor"),
+        split_axis=0,
+        concat_axis=0,
+        axis_index_groups=windows(lax.axis_size("dp"), n_y, n_q, n_par, members),
+        tiled=True,
+    )
     other = lax.ppermute(own, "par", [(0, 1), (1, 0)])
+    flat_ids = expert_ids.reshape(-1)
+    keys = flat_ids * capacity + assign_slots(flat_ids, experts)
+    start_row = lax.axis_index("tensor") * (own_tokens * 2)
+    own_keys = lax.dynamic_slice_in_dim(keys, start_row, own_tokens * 2)
+    own, other, own_keys = lax.optimization_barrier((own, other, own_keys))
     is_even = lax.axis_index("par") == 0
     even = jnp.where(is_even, own, other)
     odd = jnp.where(is_even, other, own)
@@ -132,21 +159,10 @@
     returned = lax.all_to_all(
         partial_value, ("y", "zq", "par"), split_axis=0, concat_axis=0, tiled=True
     )
-    summed = lax.psum(returned, "tensor")
-    lookup = jnp.sum(summed.reshape(experts, n_par, capacity), axis=1)
-    flat_ids = expert_ids.reshape(-1)
-    slot_ids = assign_slots(flat_ids, experts)
-    start_row = lax.axis_index("tensor") * (own_tokens * 2)
-    own_ids = lax.dynamic_slice_in_dim(flat_ids, start_row, own_tokens * 2)
-    own_slots = lax.dynamic_slice_in_dim(slot_ids, start_row, own_tokens * 2)
-    matches = (own_ids[:, None] == jnp.arange(experts, dtype=jnp.int32)[None, :]).astype(
-        jnp.float32
-    )
-    chosen = jnp.dot(matches, lookup, precision=lax.Precision.HIGHEST)
-    slot_match = (own_slots[:, None] == jnp.arange(capacity, dtype=jnp.int32)[None, :]).astype(
-        jnp.float32
-    )
-    values = jnp.sum(chosen * slot_match, axis=1).reshape(own_tokens, 2)
+    returned = jnp.sum(returned.reshape(experts, n_par, capacity), axis=1)
+    lookup = lax.psum(returned, "tensor").reshape(1, experts * capacity)
+    chosen = own_keys[:, None] == jnp.arange(experts * capacity, dtype=jnp.int32)[None, :]
+    values = jnp.sum(jnp.where(chosen, lookup, 0.0), axis=1).reshape(own_tokens, 2)
     prob_grad = values / probs
     return (hidden_grad, weight_grad, prob_grad)
 

time: 231 us -> 201 us (0.87)
  waiting for transfers between devices: 35.2 us -> 20.8 us
  blocking collectives: 154 us -> 144 us
  other arithmetic: 5.2 us -> 2.51 us
    psum x1, blocking collectives: 35.1 us -> 20.9 us  [shards(): lookup = lax.psum(returned, 'tensor').reshape(1, experts * capacity)]
    all_to_all x1 -> x0, waiting for transfers between devices: 11.3 us -> none  [shards(): lax.all_to_all(partial_value, ('y', 'zq', 'par'), split_axis=0, concat_ax...]
    all_to_all x1 -> x0, starting transfers between devices: 6.91 us -> none  [shards(): lax.all_to_all(partial_value, ('y', 'zq', 'par'), split_axis=0, concat_ax...]
    ppermute x1, starting transfers between devices: 1.91 us -> 6.9 us  [shards(): other = lax.ppermute(own, 'par', [(0, 1), (1, 0)])]
    all_to_all x1 -> x2, blocking collectives: 52.3 us -> 56.1 us  [the longest x1 37.7 us: shards(): lax.all_to_all(buffer, ('dp', 'y', 'zq', 'par', 'tensor'), split_axis=0,...]
    ppermute x1, waiting for transfers between devices: 23.8 us -> 20.7 us  [shards(): other = lax.ppermute(own, 'par', [(0, 1), (1, 0)])]
  transfers between devices with their start and end apart: 3 -> 2, of which waited for: 2 -> 1; matrix products, arithmetic and copies ran while one was open for 3% -> 2% of each run, Pallas kernels for 0% -> 0%
where the time goes in v2:
time: 201 us; the launch traced here: 200 us
  blocking collectives  144 us (72%)
  waiting for transfers between devices  20.8 us (10%)
  between operations  14.1 us (7%)
  starting transfers between devices  6.94 us (3%)
  matrix products  6.04 us (3%)
  local copies, waits for them, and re-layouts  5.08 us (3%)
  other arithmetic  2.51 us (1%)
    all_gather x1, blocking collectives, shards(): gathered = lax.all_gather(packed, 'tensor', axis=0)  66.6 us
    all_to_all x1, blocking collectives, shards(): lax.all_to_all(buffer, ('dp', 'y', 'zq', 'par', 'tensor'), split_axis=0,...  37.7 us
    psum x1, blocking collectives, shards(): lookup = lax.psum(returned, 'tensor').reshape(1, experts * capacity)  20.9 us
    ppermute x1, waiting for transfers between devices, shards(): other = lax.ppermute(own, 'par', [(0, 1), (1, 0)])  20.7 us
    all_to_all x1, blocking collectives, shards(): lax.all_to_all(partial_value, ('y', 'zq', 'par'), split_axis=0, concat_ax...  18.3 us
    ppermute x1, starting transfers between devices, shards(): other = lax.ppermute(own, 'par', [(0, 1), (1, 0)])  6.9 us
    unnamed x11, local copies, waits for them, and re-layouts  4.63 us
  transfers between devices with their start and end apart: 2, of which 1 were waited for; matrix products, arithmetic and copies ran while one was open for 2% of the time, Pallas kernels for 0%

profile of v2, /device:TPU:6, one launch (start us, length us, event | category | flops | bytes accessed | tf_op | source)
XLA Modules:
  0.0 199.8 jit_solution(3675353795380415304)
XLA Ops:
  7.2 0.0 copy-start
  7.2 0.0 reduce-scatter.2.cloned.1.call-start
  7.2 0.9 copy.26.probs_ref
  8.1 0.8 copy.27.ids_ref
  8.9 0.0 copy-start.1
  8.9 0.9 copy-done.1
  9.8 0.1 shard_map.76
  9.9 66.6 %all-gather = bf16[64,4096]{1,0:T(8,128)(2,1)S(1)} all-gather(bf16[16,4096]{1,0:T(8,128)(2,1)S(1)} %shard_map.76), channel_id=2, replica_groups=mesh['dp'=8,'y'=4,'zq'=4,'par'=2,'tensor'=4] {'tensor'}, dimensions={0}, use_global_device_ids=true | all-gather | bytes 655360 | tf_op jit(solution)/shard_map/all_gather | solution.py:120
  76.6 0.6 shard_map.77
  77.2 37.7 %all_to_all.14 = bf16[16,8,4096]{2,1,0:T(8,128)(2,1)} all-to-all(bf16[16,8,4096]{2,1,0:T(8,128)(2,1)S(1)} %bitcast.15), channel_id=1, replica_groups={{0,8,16,24,32,40,48,56,64,72,80,88,96,104,112,120},{1,9,17,25,33,41,49,..., dimensions={0} | all-to-all | bytes 2097152 | tf_op jit(solution)/shard_map/all_to_all | solution.py:127
  115.0 6.9 %collective-permute-start = (bf16[16,8,4096]{2,1,0:T(8,128)(2,1)}, bf16[16,8,4096]{2,1,0:T(8,128)(2,1)}, u32[]{:S(2)}, u32[]{:S(2)}) collective-permute-start(bf16[16,8,4096]{2,1,0:T(8,128)(2,1)} %all_to_all.14), channel_id=1, source_target_pairs={{0,4},{4,0},{1,5},{5,1},{2,6},{6,2},{3,7},{7,3},{8,12},{12,8},{9,1... | collective-permute-start | bytes 3145736 | tf_op jit(solution)/shard_map/ppermute | solution.py:135
  121.9 0.1 reshape.31
  122.0 0.1 fusion
  122.1 0.2 reduce_window_sum.11
  122.3 0.2 select_reduce_fusion
  122.4 0.1 dynamic_slice.3
  122.5 20.7 %collective-permute-done = bf16[16,8,4096]{2,1,0:T(8,128)(2,1)} collective-permute-done((bf16[16,8,4096]{2,1,0:T(8,128)(2,1)}, bf16[16,8,4096]{2,1,0:T(8,128)(2,1)}, u32[]{:S(2)}, u32[]{:S(2)}) %collective-permute-start) | collective-permute-done | bytes 1048608 | tf_op jit(solution)/shard_map/ppermute | solution.py:135
  143.3 1.7 select_bitcast_fusion.1
  144.9 0.0 copy-start.3
  145.0 0.2 pad_maximum_fusion
  145.2 0.0 copy-start.2
  145.2 1.3 copy-done.2
  146.5 0.0 copy-done.3
  146.5 2.7 %convolution_convert_fusion = bf16[4096,400]{0,1:T(8,128)(2,1)} fusion(bf16[256,400]{0,1:T(8,128)(2,1)S(1)} %copy-done.3, bf16[256,4096]{1,0:T(8,128)(2,1)S(1)} %bitcast.17), kind=kOutput, calls=%fused_computation | convolution fusion | flops 840499200 | bytes 5578752 | tf_op jit(solution)/shard_map/dot_general | solution.py:147
  149.2 0.0 reduce-scatter.2.cloned.1.call-update
  149.2 0.0 copy-done
  149.3 3.3 %multiply_reduce_fusion = (f32[256]{0:T(256)S(1)}, bf16[256,400]{0,1:T(8,128)(2,1)}) fusion(bf16[256,400]{0,1:T(8,128)(2,1)S(1)} %copy-done.3, bf16[256,4096]{1,0:T(8,128)(2,1)} %bitcast.18, bf16[4096,400]{0,1:T(8,128)(2,1)S(1)} %copy-done), kind=kOutput, calls=%fused_computation.4 | convolution fusion | flops 839270144 | bytes 5784576 | tf_op jit(solution)/shard_map/dot_general | solution.py:154
  152.6 0.1 all_to_all.10
  152.7 18.3 %all_to_all.15 = f32[32,1,8]{2,1,0:T(1,128)S(1)} all-to-all(f32[32,1,8]{2,1,0:T(1,128)S(1)} %bitcast.20), channel_id=1, replica_groups=mesh['dp'=8,'y'=4,'zq'=4,'par'=2,'tensor'=4] {'y','zq','par'}, dimensions={0} | all-to-all | bytes 2048 | tf_op jit(solution)/shard_map/all_to_all | solution.py:159
  171.0 0.1 broadcast_in_dim.17
  171.1 20.9 %psum.7 = f32[128]{0:T(128)S(1)} all-reduce(f32[128]{0:T(128)S(1)} %broadcast_in_dim.17), channel_id=1, replica_groups=mesh['dp'=8,'y'=4,'zq'=4,'par'=2,'tensor'=4] {'tensor'}, use_global_device_ids=true, to_apply=%region_5.6 | all-reduce | flops 128 | bytes 1024 | tf_op jit(solution)/shard_map/psum | solution.py:163
  192.0 0.2 select_reduce_fusion.1
  192.2 0.1 reshape.34
  192.3 0.7 copy.32
  193.0 0.0 reduce-scatter.2.cloned.1.call-done
  (3 shorter events, 0.0 us)
Async XLA Ops:
  7.2 142.1 %copy-start = (bf16[4096,400]{0,1:T(8,128)(2,1)S(1)}, bf16[4096,400]{0,1:T(8,128)(2,1)}, u32[]{:S(2)}) copy-start(bf16[4096,400]{0,1:T(8,128)(2,1)} %param.9) | copy-start | bytes 9830404
  7.2 185.8 %reduce-scatter.2.cloned.1.call-start = ((), (), s32[]{:S(2)}) async-start(), calls=%async_computation.3 | async-start | bytes 3686400 | tf_op jit(solution)/shard_map/reduce_scatter | solution.py:146
  8.9 0.9 copy-start.1
  115.0 28.3 %collective-permute-start = (bf16[16,8,4096]{2,1,0:T(8,128)(2,1)}, bf16[16,8,4096]{2,1,0:T(8,128)(2,1)}, u32[]{:S(2)}, u32[]{:S(2)}) collective-permute-start(bf16[16,8,4096]{2,1,0:T(8,128)(2,1)} %all_to_all.14), channel_id=1, source_target_pairs={{0,4},{4,0},{1,5},{5,1},{2,6},{6,2},{3,7},{7,3},{8,12},{12,8},{9,1... | collective-permute-start | bytes 3145736 | tf_op jit(solution)/shard_map/ppermute | solution.py:135
  144.9 1.6 copy-start.3
  145.2 1.4 copy-start.2
Sparse Core Ops, SparseCore 0:
  149.4 40.1 reduce-scatter.1

commit v3 on v2

--- a/solution.py
+++ b/solution.py
@@ -112,6 +112,23 @@
     hidden_cols = saved_hidden.shape[1]
     capacity = saved_hidden.shape[0] // n_expert
 
+    n_dp = lax.axis_size("dp")
+    swap = [(0, 1), (1, 0)]
+    is_even = lax.axis_index("par") == 0
+
+    hidden = saved_hidden.reshape(experts, n_par, capacity, hidden_cols)
+    hidden_mine = jnp.where(is_even, hidden[:, 0], hidden[:, 1])
+    hidden_mine = hidden_mine.reshape(experts * capacity, hidden_cols)
+    hidden_send = jnp.where(is_even, hidden[:, 1], hidden[:, 0])
+    hidden_send = hidden_send.reshape(experts * capacity, hidden_cols)
+    hidden_theirs = lax.ppermute(hidden_send, "par", swap)
+    hidden_all = lax.all_gather(jnp.stack([hidden_mine, hidden_theirs]), "dp", axis=0)
+    chunk = model_width // n_dp
+    weight_send = lax.dynamic_slice_in_dim(down_weight, lax.axis_index("dp") * chunk, chunk)
+    weight_theirs = lax.all_gather(
+        lax.ppermute(weight_send, "par", swap), "dp", axis=0, tiled=True
+    )
+
     packed = pl.pallas_call(
         pack_kernel,
         out_shape=jax.ShapeDtypeStruct((PAD, model_width), jnp.bfloat16),
@@ -124,42 +141,48 @@
         compiler_params=pltpu.CompilerParams(vmem_limit_bytes=24 << 20),
     )(gathered, expert_ids)
     buffer = buffer.reshape(experts, capacity, model_width)
-    own = lax.all_to_all(
-        buffer,
-        ("dp", "y", "zq", "par", "tensor"),
-        split_axis=0,
-        concat_axis=0,
-        axis_index_groups=windows(lax.axis_size("dp"), n_y, n_q, n_par, members),
-        tiled=True,
-    )
-    other = lax.ppermute(own, "par", [(0, 1), (1, 0)])
+    groups = windows(n_dp, n_y, n_q, n_par, members)
+    every = ("dp", "y", "zq", "par", "tensor")
+    rows = lax.all_to_all(
+        buffer, every, split_axis=0, concat_axis=0, axis_index_groups=groups, tiled=True
+    ).reshape(experts * capacity, model_width)
+
     flat_ids = expert_ids.reshape(-1)
     keys = flat_ids * capacity + assign_slots(flat_ids, experts)
     start_row = lax.axis_index("tensor") * (own_tokens * 2)
     own_keys = lax.dynamic_slice_in_dim(keys, start_row, own_tokens * 2)
-    own, other, own_keys = lax.optimization_barrier((own, other, own_keys))
-    is_even = lax.axis_index("par") == 0
-    even = jnp.where(is_even, own, other)
-    odd = jnp.where(is_even, other, own)
-    rows = jnp.stack([even, odd], axis=1).reshape(n_expert * capacity, model_width)
-
-    weight_grad = lax.psum_scatter(
-        lax.dot_general(
-            rows, saved_hidden, (((0,), (0,)), ((), ())), preferred_element_type=jnp.float32
-        ).astype(jnp.bfloat16),
-        "dp",
-        scatter_dimension=0,
-        tiled=True,
-    )
+
     product = jnp.dot(rows, down_weight, preferred_element_type=jnp.float32)
-    hidden_grad = product.astype(jnp.bfloat16)
-    partial_value = jnp.sum(saved_hidden.astype(jnp.float32) * product, axis=1).reshape(
-        n_expert, capacity
-    )
+    product_theirs = jnp.dot(rows, weight_theirs, preferred_element_type=jnp.float32)
+    partial_value = jnp.sum(
+        hidden_mine.astype(jnp.float32) * product
+        + hidden_theirs.astype(jnp.float32) * product_theirs,
+        axis=1,
+    ).reshape(experts, capacity)
+    swapped = lax.ppermute(product_theirs.astype(jnp.bfloat16), "par", swap)
+
+    by_feature = rows.reshape(experts * capacity, n_dp, model_width // n_dp).transpose(1, 0, 2)
+    replica_rows = lax.all_to_all(by_feature, "dp", split_axis=0, concat_axis=0, tiled=True)
+    contract = (((0, 1), (0, 1)), ((), ()))
+    term_theirs = lax.dot_general(
+        replica_rows, hidden_all[:, 1], contract, preferred_element_type=jnp.float32
+    ).astype(jnp.bfloat16)
+    term_mine = lax.dot_general(
+        replica_rows, hidden_all[:, 0], contract, preferred_element_type=jnp.float32
+    )
+    term_theirs, partial_value = lax.optimization_barrier((term_theirs, partial_value))
+    term_swapped = lax.ppermute(term_theirs, "par", swap)
+    weight_grad = (term_mine + term_swapped.astype(jnp.float32)).astype(jnp.bfloat16)
+
+    mine = product.astype(jnp.bfloat16).reshape(experts, capacity, hidden_cols)
+    swapped = swapped.reshape(experts, capacity, hidden_cols)
+    even = jnp.where(is_even, mine, swapped)
+    odd = jnp.where(is_even, swapped, mine)
+    hidden_grad = jnp.stack([even, odd], axis=1).reshape(n_expert * capacity, hidden_cols)
+
     returned = lax.all_to_all(
-        partial_value, ("y", "zq", "par"), split_axis=0, concat_axis=0, tiled=True
-    )
-    returned = jnp.sum(returned.reshape(experts, n_par, capacity), axis=1)
+        partial_value, every, split_axis=0, concat_axis=0, axis_index_groups=groups, tiled=True
+    )
     lookup = lax.psum(returned, "tensor").reshape(1, experts * capacity)
     chosen = own_keys[:, None] == jnp.arange(experts * capacity, dtype=jnp.int32)[None, :]
     values = jnp.sum(jnp.where(chosen, lookup, 0.0), axis=1).reshape(own_tokens, 2)

time: 201 us -> 259 us (1.29)
  blocking collectives: 144 us -> 87.3 us
  waiting for transfers between devices: 20.8 us -> 72.5 us
  starting transfers between devices: 6.94 us -> 42 us
  local copies, waits for them, and re-layouts: 5.08 us -> 18.8 us
  other arithmetic: 2.51 us -> 9.86 us
  matrix products: 6.04 us -> 11.9 us
    all_to_all x2 -> x0, blocking collectives: 56.1 us -> none  [the longest x1 37.7 us: shards(): lax.all_to_all(buffer, ('dp', 'y', 'zq', 'par', 'tensor'), split_axis=0,...]
    all_gather x0 -> x2, waiting for transfers between devices: none -> 41.4 us  [the longest x1 41.4 us: shards(): lax.all_gather(jnp.stack([hidden_mine, hidden_theirs]), 'dp', axis=0)]
    all_to_all x0 -> x3, starting transfers between devices: none -> 26.4 us  [the longest x1 11.6 us: shards(): lax.all_to_all(partial_value, every, split_axis=0, concat_axis=0, axis_in...]
    all_to_all x0 -> x3, waiting for transfers between devices: none -> 15.2 us  [the longest x1 10.9 us: shards(): lax.all_to_all(partial_value, every, split_axis=0, concat_axis=0, axis_in...]
    ppermute x1 -> x4, starting transfers between devices: 6.9 us -> 15.6 us  [the longest x1 7.76 us: shards(): swapped = lax.ppermute(product_theirs.astype(jnp.bfloat16), 'par', swap)]
    dot_general x1 -> x3, matrix products: 2.71 us -> 9.64 us  [the longest x1 3.92 us: shards(): jnp.dot(rows, weight_theirs, preferred_element_type=jnp.float32)]
    all_gather x1, blocking collectives: 66.6 us -> 60.9 us  [shards(): gathered = lax.all_gather(packed, 'tensor', axis=0)]
    ppermute x1 -> x4, waiting for transfers between devices: 20.7 us -> 15.2 us  [the longest x1 15.2 us: shards(): hidden_theirs = lax.ppermute(hidden_send, 'par', swap)]
  transfers between devices with their start and end apart: 2 -> 9, of which waited for: 1 -> 4; matrix products, arithmetic and copies ran while one was open for 2% -> 13% of each run, Pallas kernels for 0% -> 0%
where the time goes in v3:
time: 259 us; the launch traced here: 257 us
  blocking collectives  87.3 us (34%)
  waiting for transfers between devices  72.5 us (28%)
  starting transfers between devices  42 us (16%)
  local copies, waits for them, and re-layouts  18.8 us (7%)
  between operations  14.3 us (6%)
  matrix products  11.9 us (5%)
  other arithmetic  9.86 us (4%)
    all_gather x1, blocking collectives, shards(): gathered = lax.all_gather(packed, 'tensor', axis=0)  60.9 us
    all_gather x1, waiting for transfers between devices, shards(): lax.all_gather(jnp.stack([hidden_mine, hidden_theirs]), 'dp', axis=0)  41.4 us
    psum x1, blocking collectives, shards(): lookup = lax.psum(returned, 'tensor').reshape(1, experts * capacity)  26.3 us
    ppermute x1, waiting for transfers between devices, shards(): hidden_theirs = lax.ppermute(hidden_send, 'par', swap)  15.2 us
    all_to_all x1, starting transfers between devices, shards(): lax.all_to_all(partial_value, every, split_axis=0, concat_axis=0, axis_in...  11.6 us
    all_to_all x1, waiting for transfers between devices, shards(): lax.all_to_all(partial_value, every, split_axis=0, concat_axis=0, axis_in...  10.9 us
    all_to_all x1, starting transfers between devices, shards(): lax.all_to_all(buffer, every, split_axis=0, concat_axis=0, axis_index_gro...  9.9 us
    unnamed x18, local copies, waits for them, and re-layouts  9.32 us
  transfers between devices with their start and end apart: 9, of which 4 were waited for; matrix products, arithmetic and copies ran while one was open for 13% of the time, Pallas kernels for 0%

profile of v3, /device:TPU:6, one launch (start us, length us, event | category | flops | bytes accessed | tf_op | source)
XLA Modules:
  0.0 257.3 jit_solution(10867143550099813402)
XLA Ops:
  7.2 0.0 copy-start
  7.2 0.0 copy-start.5
  7.2 1.9 copy-done
  9.1 0.8 constant_dynamic-slice_fusion
  9.9 3.8 %collective-permute-start = (bf16[512,400]{0,1:T(8,128)(2,1)}, bf16[512,400]{0,1:T(8,128)(2,1)}, u32[]{:S(2)}, u32[]{:S(2)}) collective-permute-start(bf16[512,400]{0,1:T(8,128)(2,1)} %constant_dynamic-slice_fusion), channel_id=1, source_target_pairs={{0,4},{4,0},{1,5},{5,1},{2,6},{6,2},{3,7},{7,3},{8,12},{12,8},{9,1... | collective-permute-start | bytes 1228808 | tf_op jit(solution)/shard_map/ppermute | solution.py:129
  13.7 0.8 copy.72.probs_ref
  14.5 0.8 copy.73.ids_ref
  15.2 0.9 copy-done.2
  16.1 0.1 shard_map.76
  16.2 60.9 %all-gather = bf16[64,4096]{1,0:T(8,128)(2,1)S(1)} all-gather(bf16[16,4096]{1,0:T(8,128)(2,1)S(1)} %shard_map.76), channel_id=2, replica_groups=mesh['dp'=8,'y'=4,'zq'=4,'par'=2,'tensor'=4] {'tensor'}, dimensions={0}, use_global_device_ids=true | all-gather | bytes 655360 | tf_op jit(solution)/shard_map/all_gather | solution.py:137
  77.2 0.6 shard_map.77
  77.8 0.0 copy-start.1
  77.8 1.0 copy-done.1
  78.8 9.9 %all-to-all-start = ((bf16[16,8,4096]{2,1,0:T(8,128)(2,1)}), bf16[16,8,4096]{2,1,0:T(8,128)(2,1)}, u32[]{:S(2)}, u32[]{:S(2)}) async-start(bf16[16,8,4096]{2,1,0:T(8,128)(2,1)} %bitcast.53), calls=%async_computation | async-start | bytes 2097152 | tf_op jit(solution)/shard_map/all_to_all | solution.py:146
  88.7 0.0 all-gather.5.cloned.1.call-start
  88.8 0.0 collective-permute-done
  88.8 0.7 all-gather.5.cloned.1.call-update
  89.5 0.0 all-gather.7.cloned.1.call-start
  89.5 0.0 copy-done.5
  89.5 0.8 copy.78
  90.4 1.8 bitcast_convert_fusion
  92.2 1.7 copy.79
  93.8 1.9 collective-permute-start.2
  95.7 0.8 copy.80
  96.5 15.2 %collective-permute-done.2 = bf16[128,400]{0,1:T(8,128)(2,1)S(1)} collective-permute-done((bf16[128,400]{0,1:T(8,128)(2,1)}, bf16[128,400]{0,1:T(8,128)(2,1)S(1)}, u32[]{:S(2)}, u32[]{:S(2)}) %collective-permute-start.2) | collective-permute-done | bytes 102432 | tf_op jit(solution)/shard_map/ppermute | solution.py:124
  111.7 1.6 pad_maximum_fusion.1
  113.4 0.0 all-gather.7.cloned.1.call-update
  113.4 0.0 copy-done.4
  113.4 0.1 reshape.109
  113.5 0.7 fusion.5
  114.2 1.6 reduce_window_sum.11
  115.8 4.3 %all-to-all-done = bf16[16,8,4096]{2,1,0:T(8,128)(2,1)} async-done(((bf16[16,8,4096]{2,1,0:T(8,128)(2,1)}), bf16[16,8,4096]{2,1,0:T(8,128)(2,1)}, u32[]{:S(2)}, u32[]{:S(2)}) %all-to-all-start) | async-done | bytes 1048608 | tf_op jit(solution)/shard_map/all_to_all | solution.py:146
  120.1 1.6 copy.94
  121.7 1.3 copy.96
  123.0 4.9 %all-to-all-start.1 = ((bf16[8,128,512]{2,1,0:T(8,128)(2,1)}), bf16[8,128,512]{2,1,0:T(8,128)(2,1)}, u32[]{:S(2)}, u32[]{:S(2)}) async-start(bf16[8,128,512]{2,1,0:T(8,128)(2,1)} %bitcast.55), calls=%async_computation.1 | async-start | bytes 2097152 | tf_op jit(solution)/shard_map/all_to_all | solution.py:165
  127.9 1.0 select_reduce_fusion
  128.9 0.0 copy-done.3
  128.9 0.8 copy.83
  129.8 0.7 dynamic_slice.7
  130.4 2.2 fusion.3
  132.7 0.0 all-gather.5.cloned.1.call-done
  132.7 3.9 %add_reduce_fusion = (f32[128]{0:T(128)S(1)}, bf16[128,400]{0,1:T(8,128)(2,1)}) fusion(bf16[128,400]{0,1:T(8,128)(2,1)} %copy-done.4, f32[128,400]{0,1:T(8,128)} %copy.83, f32[128,400]{0,1:T(8,128)S(1)} %fusion.3, bf16[4096,400]{0,1:T(8,128)(2,1)} %all-gather.5.cloned.1.call-done, bf16[16,8,4096]{2,1,0:T(8,128)(2,1)} %all-to-all-done), kind=kOutput, calls=%fused_computation.13 | convolution fusion | flops 419737472 | bytes 4940288 | tf_op jit(solution)/shard_map/dot_general | solution.py:156
  136.6 7.8 %collective-permute-start.1 = (bf16[128,400]{0,1:T(8,128)(2,1)}, bf16[128,400]{0,1:T(8,128)(2,1)}, u32[]{:S(2)}, u32[]{:S(2)}) collective-permute-start(bf16[128,400]{0,1:T(8,128)(2,1)} %get-tuple-element.28), channel_id=1, source_target_pairs={{0,4},{4,0},{1,5},{5,1},{2,6},{6,2},{3,7},{7,3},{8,12},{12,8},{9,1... | collective-permute-start | bytes 307208 | tf_op jit(solution)/shard_map/ppermute | solution.py:162
  144.4 0.7 reshape.108
  145.1 41.4 %all-gather.7.cloned.1.call-done = bf16[16,128,400]{1,2,0:T(8,128)(2,1)} async-done(((bf16[2,128,400]{1,2,0:T(8,128)(2,1)}), bf16[16,128,400]{1,2,0:T(8,128)(2,1)}) %all-gather.7.cloned.1.call-update) | async-done | bytes 1638416 | tf_op jit(solution)/shard_map/all_gather | solution.py:125
  186.5 0.0 all-to-all-done.1
  186.5 2.8 %fusion = bf16[512,400]{0,1:T(8,128)(2,1)} fusion(bf16[8,128,512]{2,1,0:T(8,128)(2,1)} %all-to-all-done.1, bf16[8,2,128,400]{2,3,1,0:T(8,128)(2,1)} %bitcast.62), kind=kOutput, calls=%fused_computation.2 | convolution fusion | flops 419635200 | bytes 2277376 | tf_op jit(solution)/shard_map/dot_general | solution.py:167
  189.3 2.1 collective-permute-start.3
  191.4 0.0 collective-permute-done.1
  191.4 1.6 broadcast_select_fusion.2
  193.0 1.0 copy.75
  194.0 1.0 copy.74
  195.0 11.6 %all-to-all-start.2 = ((f32[16,1,8]{2,1,0:T(1,128)}), f32[16,1,8]{2,1,0:T(1,128)S(1)}, u32[]{:S(2)}, u32[]{:S(2)}) async-start(f32[16,1,8]{2,1,0:T(1,128)} %bitcast.19), calls=%async_computation.2 | async-start | bytes 16384 | tf_op jit(solution)/shard_map/all_to_all | solution.py:183
  206.6 0.8 copy.88
  207.4 10.9 %all-to-all-done.2 = f32[16,1,8]{2,1,0:T(1,128)S(1)} async-done(((f32[16,1,8]{2,1,0:T(1,128)}), f32[16,1,8]{2,1,0:T(1,128)S(1)}, u32[]{:S(2)}, u32[]{:S(2)}) %all-to-all-start.2) | async-done | bytes 544 | tf_op jit(solution)/shard_map/all_to_all | solution.py:183
  218.3 0.5 broadcast.40
  218.9 0.7 reduce.3
  219.5 0.1 broadcast_in_dim.17
  219.6 26.3 %psum.7 = f32[128]{0:T(128)S(1)} all-reduce(f32[128]{0:T(128)S(1)} %broadcast_in_dim.17), channel_id=1, replica_groups=mesh['dp'=8,'y'=4,'zq'=4,'par'=2,'tensor'=4] {'tensor'}, use_global_device_ids=true, to_apply=%region_3.4 | all-reduce | flops 128 | bytes 1024 | tf_op jit(solution)/shard_map/psum | solution.py:186
  246.0 0.9 select_reduce_fusion.1
  246.8 0.1 reshape.110
  246.9 0.7 copy.89
  247.6 0.0 collective-permute-done.3
  247.6 2.9 %add_convert_fusion = bf16[512,400]{0,1:T(8,128)(2,1)} fusion(bf16[512,400]{0,1:T(8,128)(2,1)} %collective-permute-done.3, bf16[8,128,512]{2,1,0:T(8,128)(2,1)} %all-to-all-done.1, bf16[8,2,128,400]{2,3,1,0:T(8,128)(2,1)} %bitcast.63), kind=kOutput, calls=%fused_computation.10 | convolution fusion | flops 420044800 | bytes 2686976 | tf_op jit(solution)/shard_map/dot_general | solution.py:170
  (7 shorter events, 0.1 us)
Async XLA Ops:
  7.2 1.9 copy-start
  7.2 82.4 %copy-start.5 = (bf16[256,400]{0,1:T(8,128)(2,1)S(1)}, bf16[256,400]{0,1:T(8,128)(2,1)}, u32[]{:S(2)}) copy-start(bf16[256,400]{0,1:T(8,128)(2,1)} %param.8) | copy-start | bytes 614404
  9.9 78.9 %collective-permute-start = (bf16[512,400]{0,1:T(8,128)(2,1)}, bf16[512,400]{0,1:T(8,128)(2,1)}, u32[]{:S(2)}, u32[]{:S(2)}) collective-permute-start(bf16[512,400]{0,1:T(8,128)(2,1)} %constant_dynamic-slice_fusion), channel_id=1, source_target_pairs={{0,4},{4,0},{1,5},{5,1},{2,6},{6,2},{3,7},{7,3},{8,12},{12,8},{9,1... | collective-permute-start | bytes 1228808 | tf_op jit(solution)/shard_map/ppermute | solution.py:129
  15.2 0.9 copy-start.2
  77.8 1.0 copy-start.1
  78.8 41.2 %all-to-all-start = ((bf16[16,8,4096]{2,1,0:T(8,128)(2,1)}), bf16[16,8,4096]{2,1,0:T(8,128)(2,1)}, u32[]{:S(2)}, u32[]{:S(2)}) async-start(bf16[16,8,4096]{2,1,0:T(8,128)(2,1)} %bitcast.53), calls=%async_computation | async-start | bytes 2097152 | tf_op jit(solution)/shard_map/all_to_all | solution.py:146
  88.7 43.9 %all-gather.5.cloned.1.call-start = ((), (), s32[]{:S(2)}) async-start(), calls=%async_computation.3 | async-start | bytes 3686400 | tf_op jit(solution)/shard_map/all_gather | solution.py:128
  89.5 97.0 %all-gather.7.cloned.1.call-start = ((), (), s32[]{:S(2)}) async-start(), calls=%async_computation.4 | async-start | bytes 1843200 | tf_op jit(solution)/shard_map/all_gather | solution.py:125
  93.8 17.9 %collective-permute-start.2 = (bf16[128,400]{0,1:T(8,128)(2,1)}, bf16[128,400]{0,1:T(8,128)(2,1)S(1)}, u32[]{:S(2)}, u32[]{:S(2)}) collective-permute-start(bf16[128,400]{0,1:T(8,128)(2,1)} %copy.79), channel_id=1, source_target_pairs={{0,4},{4,0},{1,5},{5,1},{2,6},{6,2},{3,7},{7,3},{8,12},{12,8},{9,1... | collective-permute-start | bytes 307208 | tf_op jit(solution)/shard_map/ppermute | solution.py:124
  111.7 1.7 copy-start.4
  113.5 15.4 %copy-start.3 = (f32[128,400]{1,0:T(8,128)S(1)}, f32[128,400]{1,0:T(8,128)}, u32[]{:S(2)}) copy-start(f32[128,400]{1,0:T(8,128)} %get-tuple-element.24) | copy-start | bytes 614404
  123.0 63.5 %all-to-all-start.1 = ((bf16[8,128,512]{2,1,0:T(8,128)(2,1)}), bf16[8,128,512]{2,1,0:T(8,128)(2,1)}, u32[]{:S(2)}, u32[]{:S(2)}) async-start(bf16[8,128,512]{2,1,0:T(8,128)(2,1)} %bitcast.55), calls=%async_computation.1 | async-start | bytes 2097152 | tf_op jit(solution)/shard_map/all_to_all | solution.py:165
  136.6 54.8 %collective-permute-start.1 = (bf16[128,400]{0,1:T(8,128)(2,1)}, bf16[128,400]{0,1:T(8,128)(2,1)}, u32[]{:S(2)}, u32[]{:S(2)}) collective-permute-start(bf16[128,400]{0,1:T(8,128)(2,1)} %get-tuple-element.28), channel_id=1, source_target_pairs={{0,4},{4,0},{1,5},{5,1},{2,6},{6,2},{3,7},{7,3},{8,12},{12,8},{9,1... | collective-permute-start | bytes 307208 | tf_op jit(solution)/shard_map/ppermute | solution.py:162
  189.3 58.3 %collective-permute-start.3 = (bf16[512,400]{0,1:T(8,128)(2,1)}, bf16[512,400]{0,1:T(8,128)(2,1)}, u32[]{:S(2)}, u32[]{:S(2)}) collective-permute-start(bf16[512,400]{0,1:T(8,128)(2,1)} %fusion), channel_id=1, source_target_pairs={{0,4},{4,0},{1,5},{5,1},{2,6},{6,2},{3,7},{7,3},{8,12},{12,8},{9,1... | collective-permute-start | bytes 1228808 | tf_op jit(solution)/shard_map/ppermute | solution.py:174
  195.0 23.4 %all-to-all-start.2 = ((f32[16,1,8]{2,1,0:T(1,128)}), f32[16,1,8]{2,1,0:T(1,128)S(1)}, u32[]{:S(2)}, u32[]{:S(2)}) async-start(f32[16,1,8]{2,1,0:T(1,128)} %bitcast.19), calls=%async_computation.2 | async-start | bytes 16384 | tf_op jit(solution)/shard_map/all_to_all | solution.py:183
Sparse Core Ops, SparseCore 0:
  92.3 37.8 all-gather.4
  133.4 52.9 all-gather.6

commit v4 on v3

--- a/solution.py
+++ b/solution.py
@@ -81,6 +81,106 @@
         out_ref[:, start : start + step] = (rows * scale).astype(jnp.bfloat16)
 
 
+def parity_order(rows, capacity, from_natural):
+    lanes = rows // 2
+    axes = (0, 1) if from_natural else (1, 0)
+    natural = lax.broadcasted_iota(jnp.int32, (rows, rows), axes[0])
+    ordered = lax.broadcasted_iota(jnp.int32, (rows, rows), axes[1])
+    here = lax.axis_index("par")
+    parity = jnp.where(ordered < lanes, here, 1 - here)
+    within = ordered % lanes
+    source = (within // capacity) * (2 * capacity) + parity * capacity + within % capacity
+    return (natural == source).astype(jnp.bfloat16)
+
+
+def sort_kernel(capacity, hidden_ref, mine_ref, send_ref):
+    rows = hidden_ref.shape[1]
+    order = parity_order(rows, capacity, True)
+    moved = jnp.dot(hidden_ref[...], order, preferred_element_type=jnp.float32)
+    moved = moved.astype(jnp.bfloat16)
+    mine_ref[...] = moved[:, : rows // 2]
+    send_ref[...] = moved[:, rows // 2 :]
+
+
+def unsort_kernel(capacity, mine_ref, theirs_ref, out_ref):
+    rows = out_ref.shape[1]
+    order = parity_order(rows, capacity, False)
+    both = jnp.concatenate([mine_ref[...], theirs_ref[...]], axis=1)
+    out_ref[...] = jnp.dot(both, order, preferred_element_type=jnp.float32).astype(jnp.bfloat16)
+
+
+def product_kernel(
+    capacity,
+    rows_ref,
+    weight_ref,
+    weight_theirs_ref,
+    hidden_ref,
+    hidden_theirs_ref,
+    mine_ref,
+    theirs_ref,
+    partial_ref,
+    by_feature_ref,
+    total,
+):
+    step = pl.program_id(0)
+
+    @pl.when(step == 0)
+    def _():
+        total[...] = jnp.zeros_like(total)
+
+    rows = rows_ref[...]
+    by_feature_ref[0] = rows
+    contract = (((1,), (1,)), ((), ()))
+    total[0] += lax.dot_general(
+        weight_ref[...], rows, contract, preferred_element_type=jnp.float32
+    )
+    total[1] += lax.dot_general(
+        weight_theirs_ref[0], rows, contract, preferred_element_type=jnp.float32
+    )
+
+    @pl.when(step == pl.num_programs(0) - 1)
+    def _():
+        mine, theirs = total[0], total[1]
+        mine_ref[...] = mine.astype(jnp.bfloat16)
+        theirs_ref[...] = theirs.astype(jnp.bfloat16)
+        summed = jnp.sum(
+            hidden_ref[...].astype(jnp.float32) * mine
+            + hidden_theirs_ref[...].astype(jnp.float32) * theirs,
+            axis=0,
+            keepdims=True,
+        )
+        lanes = summed.shape[1]
+        experts = partial_ref.shape[0]
+        of_expert = lax.broadcasted_iota(jnp.int32, (experts, lanes), 1) // capacity
+        expert = lax.broadcasted_iota(jnp.int32, (experts, lanes), 0)
+        spread = jnp.where(of_expert == expert, summed, 0.0)
+        at = lax.broadcasted_iota(jnp.int32, (lanes, LANES), 0) % capacity
+        slot = lax.broadcasted_iota(jnp.int32, (lanes, LANES), 1)
+        partial_ref[...] = jnp.dot(
+            spread,
+            (at == slot).astype(jnp.float32),
+            precision=lax.Precision.HIGHEST,
+            preferred_element_type=jnp.float32,
+        )
+
+
+def term_kernel(hidden_ref, rows_ref, mine_ref, theirs_ref, total):
+    step = pl.program_id(0)
+
+    @pl.when(step == 0)
+    def _():
+        total[...] = jnp.zeros_like(total)
+
+    rows = rows_ref[0]
+    for half in range(2):
+        total[half] += jnp.dot(hidden_ref[0, half], rows, preferred_element_type=jnp.float32)
+
+    @pl.when(step == pl.num_programs(0) - 1)
+    def _():
+        mine_ref[...] = total[0]
+        theirs_ref[...] = total[1].astype(jnp.bfloat16)
+
+
 def assign_slots(flat_ids, experts):
     expert_range = jnp.arange(experts, dtype=jnp.int32)
     onehot = (flat_ids[:, None] == expert_range[None, :]).astype(jnp.int32)
@@ -113,79 +213,115 @@
     capacity = saved_hidden.shape[0] // n_expert
 
     n_dp = lax.axis_size("dp")
+    chunk = model_width // n_dp
+    half = experts * capacity
     swap = [(0, 1), (1, 0)]
-    is_even = lax.axis_index("par") == 0
-
-    hidden = saved_hidden.reshape(experts, n_par, capacity, hidden_cols)
-    hidden_mine = jnp.where(is_even, hidden[:, 0], hidden[:, 1])
-    hidden_mine = hidden_mine.reshape(experts * capacity, hidden_cols)
-    hidden_send = jnp.where(is_even, hidden[:, 1], hidden[:, 0])
-    hidden_send = hidden_send.reshape(experts * capacity, hidden_cols)
+    large = pltpu.CompilerParams(vmem_limit_bytes=56 << 20)
+    small = pltpu.CompilerParams(vmem_limit_bytes=16 << 20)
+
+    weight = down_weight.T
+    weight_send = lax.dynamic_slice_in_dim(weight, lax.axis_index("dp") * chunk, chunk, axis=1)
+    weight_swapped = lax.ppermute(weight_send, "par", swap)
+    hidden_mine, hidden_send = pl.pallas_call(
+        functools.partial(sort_kernel, capacity),
+        out_shape=[jax.ShapeDtypeStruct((hidden_cols, half), jnp.bfloat16)] * 2,
+        compiler_params=small,
+    )(saved_hidden.T)
     hidden_theirs = lax.ppermute(hidden_send, "par", swap)
-    hidden_all = lax.all_gather(jnp.stack([hidden_mine, hidden_theirs]), "dp", axis=0)
-    chunk = model_width // n_dp
-    weight_send = lax.dynamic_slice_in_dim(down_weight, lax.axis_index("dp") * chunk, chunk)
-    weight_theirs = lax.all_gather(
-        lax.ppermute(weight_send, "par", swap), "dp", axis=0, tiled=True
-    )
-
     packed = pl.pallas_call(
         pack_kernel,
         out_shape=jax.ShapeDtypeStruct((PAD, model_width), jnp.bfloat16),
-        compiler_params=pltpu.CompilerParams(vmem_limit_bytes=8 << 20),
+        compiler_params=small,
     )(cotangent, probs)
+    packed, weight_swapped, hidden_theirs = lax.optimization_barrier(
+        (packed, weight_swapped, hidden_theirs)
+    )
+    weight_theirs = lax.all_gather(weight_swapped, "dp", axis=0)
+    hidden_all = lax.all_gather(jnp.stack([hidden_mine, hidden_theirs]), "dp", axis=0)
+
     gathered = lax.all_gather(packed, "tensor", axis=0)
     buffer = pl.pallas_call(
         functools.partial(fill_kernel, own_tokens, experts, capacity),
-        out_shape=jax.ShapeDtypeStruct((experts * capacity, model_width), jnp.bfloat16),
+        out_shape=jax.ShapeDtypeStruct((half, model_width), jnp.bfloat16),
         compiler_params=pltpu.CompilerParams(vmem_limit_bytes=24 << 20),
     )(gathered, expert_ids)
+    buffer, weight_theirs = lax.optimization_barrier((buffer, weight_theirs))
     buffer = buffer.reshape(experts, capacity, model_width)
     groups = windows(n_dp, n_y, n_q, n_par, members)
     every = ("dp", "y", "zq", "par", "tensor")
     rows = lax.all_to_all(
         buffer, every, split_axis=0, concat_axis=0, axis_index_groups=groups, tiled=True
-    ).reshape(experts * capacity, model_width)
+    ).reshape(half, model_width)
 
     flat_ids = expert_ids.reshape(-1)
     keys = flat_ids * capacity + assign_slots(flat_ids, experts)
     start_row = lax.axis_index("tensor") * (own_tokens * 2)
     own_keys = lax.dynamic_slice_in_dim(keys, start_row, own_tokens * 2)
-
-    product = jnp.dot(rows, down_weight, preferred_element_type=jnp.float32)
-    product_theirs = jnp.dot(rows, weight_theirs, preferred_element_type=jnp.float32)
-    partial_value = jnp.sum(
-        hidden_mine.astype(jnp.float32) * product
-        + hidden_theirs.astype(jnp.float32) * product_theirs,
-        axis=1,
-    ).reshape(experts, capacity)
-    swapped = lax.ppermute(product_theirs.astype(jnp.bfloat16), "par", swap)
-
-    by_feature = rows.reshape(experts * capacity, n_dp, model_width // n_dp).transpose(1, 0, 2)
+    rows, own_keys = lax.optimization_barrier((rows, own_keys))
+
+    whole = pl.BlockSpec((hidden_cols, half), lambda i: (0, 0))
+    product, product_theirs, partial_value, by_feature = pl.pallas_call(
+        functools.partial(product_kernel, capacity),
+        grid=(n_dp,),
+        in_specs=[
+            pl.BlockSpec((half, chunk), lambda i: (0, i)),
+            pl.BlockSpec((hidden_cols, chunk), lambda i: (0, i)),
+            pl.BlockSpec((1, hidden_cols, chunk), lambda i: (i, 0, 0)),
+            whole,
+            whole,
+        ],
+        out_specs=[
+            whole,
+            whole,
+            pl.BlockSpec((experts, LANES), lambda i: (0, 0)),
+            pl.BlockSpec((1, half, chunk), lambda i: (i, 0, 0)),
+        ],
+        out_shape=[
+            jax.ShapeDtypeStruct((hidden_cols, half), jnp.bfloat16),
+            jax.ShapeDtypeStruct((hidden_cols, half), jnp.bfloat16),
+            jax.ShapeDtypeStruct((experts, LANES), jnp.float32),
+            jax.ShapeDtypeStruct((n_dp, half, chunk), jnp.bfloat16),
+        ],
+        scratch_shapes=[pltpu.VMEM((2, hidden_cols, half), jnp.float32)],
+        compiler_params=large,
+    )(rows, weight, weight_theirs, hidden_mine, hidden_theirs)
+
     replica_rows = lax.all_to_all(by_feature, "dp", split_axis=0, concat_axis=0, tiled=True)
-    contract = (((0, 1), (0, 1)), ((), ()))
-    term_theirs = lax.dot_general(
-        replica_rows, hidden_all[:, 1], contract, preferred_element_type=jnp.float32
-    ).astype(jnp.bfloat16)
-    term_mine = lax.dot_general(
-        replica_rows, hidden_all[:, 0], contract, preferred_element_type=jnp.float32
-    )
-    term_theirs, partial_value = lax.optimization_barrier((term_theirs, partial_value))
+    partial_value = lax.psum(partial_value, "tensor")
+    product_swapped = lax.ppermute(product_theirs, "par", swap)
+    square = pl.BlockSpec((hidden_cols, chunk), lambda i: (0, 0))
+    term, term_theirs = pl.pallas_call(
+        term_kernel,
+        grid=(n_dp,),
+        in_specs=[
+            pl.BlockSpec((1, 2, hidden_cols, half), lambda i: (i, 0, 0, 0)),
+            pl.BlockSpec((1, half, chunk), lambda i: (i, 0, 0)),
+        ],
+        out_specs=[square, square],
+        out_shape=[
+            jax.ShapeDtypeStruct((hidden_cols, chunk), jnp.float32),
+            jax.ShapeDtypeStruct((hidden_cols, chunk), jnp.bfloat16),
+        ],
+        scratch_shapes=[pltpu.VMEM((2, hidden_cols, chunk), jnp.float32)],
+        compiler_params=large,
+    )(hidden_all, replica_rows)
+    hidden_grad = pl.pallas_call(
+        functools.partial(unsort_kernel, capacity),
+        out_shape=jax.ShapeDtypeStruct((hidden_cols, 2 * half), jnp.bfloat16),
+        compiler_params=small,
+    )(product, product_swapped)
+    partial_value, term_theirs = lax.optimization_barrier((partial_value, term_theirs))
     term_swapped = lax.ppermute(term_theirs, "par", swap)
-    weight_grad = (term_mine + term_swapped.astype(jnp.float32)).astype(jnp.bfloat16)
-
-    mine = product.astype(jnp.bfloat16).reshape(experts, capacity, hidden_cols)
-    swapped = swapped.reshape(experts, capacity, hidden_cols)
-    even = jnp.where(is_even, mine, swapped)
-    odd = jnp.where(is_even, swapped, mine)
-    hidden_grad = jnp.stack([even, odd], axis=1).reshape(n_expert * capacity, hidden_cols)
-
-    returned = lax.all_to_all(
+    lookup = lax.all_to_all(
         partial_value, every, split_axis=0, concat_axis=0, axis_index_groups=groups, tiled=True
     )
-    lookup = lax.psum(returned, "tensor").reshape(1, experts * capacity)
-    chosen = own_keys[:, None] == jnp.arange(experts * capacity, dtype=jnp.int32)[None, :]
-    values = jnp.sum(jnp.where(chosen, lookup, 0.0), axis=1).reshape(own_tokens, 2)
+    weight_grad = (term + term_swapped.astype(jnp.float32)).astype(jnp.bfloat16).T
+    hidden_grad = hidden_grad.T
+
+    expert = lax.broadcasted_iota(jnp.int32, (1, experts, LANES), 1)
+    slot = lax.broadcasted_iota(jnp.int32, (1, experts, LANES), 2)
+    chosen = (own_keys[:, None, None] == expert * capacity + slot) & (slot < capacity)
+    values = jnp.sum(jnp.where(chosen, lookup[None], 0.0), axis=(1, 2)).reshape(own_tokens, 2)
     prob_grad = values / probs
     return (hidden_grad, weight_grad, prob_grad)
 

time: 259 us -> 211 us (0.81)
  waiting for transfers between devices: 72.5 us -> 47.5 us
  Pallas kernels: 0.74 us -> 18.6 us
  matrix products: 11.9 us -> 0 us
  local copies, waits for them, and re-layouts: 18.8 us -> 8.11 us
  starting transfers between devices: 42 us -> 33.4 us
  other arithmetic: 9.86 us -> 3.68 us
  blocking collectives: 87.3 us -> 84.2 us
    all_gather x1, waiting for transfers between devices: 41.4 us -> 0.01 us  [shards(): lax.all_gather(jnp.stack([hidden_mine, hidden_theirs]), 'dp', axis=0)]
    all_to_all x1, waiting for transfers between devices: 4.25 us -> 29.9 us  [shards(): lax.all_to_all(buffer, every, split_axis=0, concat_axis=0, axis_index_gro...]
    pallas_call x0 -> x4, Pallas kernels: none -> 16.8 us  [the longest x1 8.49 us: shards(): pl.pallas_call(functools.partial(product_kernel, capacity), grid=(n_dp,),...]
    dot_general x4 -> x0, matrix products: 11.9 us -> none  [the longest x1 3.92 us: shards(): jnp.dot(rows, weight_theirs, preferred_element_type=jnp.float32)]
    ppermute x1, waiting for transfers between devices: 15.2 us -> 6.67 us  [shards(): hidden_theirs = lax.ppermute(hidden_send, 'par', swap)]
    all_to_all x1, starting transfers between devices: 11.6 us -> 4.45 us  [shards(): lax.all_to_all(partial_value, every, split_axis=0, concat_axis=0, axis_in...]
    ppermute x2, starting transfers between devices: 11.6 us -> 5.74 us  [the longest x1 3.83 us: shards(): weight_swapped = lax.ppermute(weight_send, 'par', swap)]
    select_n x4 -> x0, local copies, waits for them, and re-layouts: 4.4 us -> none  [the longest x1 1.65 us: shards(): hidden_send = jnp.where(is_even, hidden[:, 1], hidden[:, 0])]
  transfers between devices with their start and end apart: 9 -> 9, of which waited for: 4 -> 4; matrix products, arithmetic and copies ran while one was open for 13% -> 2% of each run, Pallas kernels for 0% -> 5%
where the time goes in v4:
time: 211 us; the launch traced here: 210 us
  blocking collectives  84.2 us (40%)
  waiting for transfers between devices  47.5 us (23%)
  starting transfers between devices  33.4 us (16%)
  Pallas kernels  18.6 us (9%)
  between operations  14.2 us (7%)
  local copies, waits for them, and re-layouts  8.11 us (4%)
  other arithmetic  3.68 us (2%)
    all_gather x1, blocking collectives, shards(): gathered = lax.all_gather(packed, 'tensor', axis=0)  60.4 us
    all_to_all x1, waiting for transfers between devices, shards(): lax.all_to_all(buffer, every, split_axis=0, concat_axis=0, axis_index_gro...  29.9 us
    psum x1, blocking collectives, shards(): partial_value = lax.psum(partial_value, 'tensor')  23.8 us
    all_to_all x1, starting transfers between devices, shards(): lax.all_to_all(buffer, every, split_axis=0, concat_axis=0, axis_index_gro...  9.92 us
    pallas_call x1, Pallas kernels, shards(): pl.pallas_call(functools.partial(product_kernel, capacity), grid=(n_dp,),...  8.49 us
    pallas_call x1, Pallas kernels, shards(): pl.pallas_call(term_kernel, grid=(n_dp,), in_specs=[pl.BlockSpec((1, 2, h...  7.2 us
    all_to_all x1, waiting for transfers between devices, shards(): lax.all_to_all(partial_value, every, split_axis=0, concat_axis=0, axis_in...  7.02 us
    unnamed x21, local copies, waits for them, and re-layouts  6.79 us
  transfers between devices with their start and end apart: 9, of which 4 were waited for; matrix products, arithmetic and copies ran while one was open for 2% of the time, Pallas kernels for 5%

profile of v4, /device:TPU:6, one launch (start us, length us, event | category | flops | bytes accessed | tf_op | source)
XLA Modules:
  0.0 209.7 jit_solution(10637402250015136039)
XLA Ops:
  7.2 0.0 all-gather.6.cloned.1.call-start
  7.2 1.0 dynamic-slice_bitcast_fusion
  8.3 3.8 %collective-permute-start = (bf16[400,512]{1,0:T(8,128)(2,1)S(1)}, bf16[400,512]{1,0:T(8,128)(2,1)S(1)}, u32[]{:S(2)}, u32[]{:S(2)}) collective-permute-start(bf16[400,512]{1,0:T(8,128)(2,1)S(1)} %dynamic-slice_bitcast_fusion), channel_id=1, source_target_pairs={{0,4},{4,0},{1,5},{5,1},{2,6},{6,2},{3,7},{7,3},{8,12},{12,8},{9,1... | collective-permute-start | bytes 1228808 | tf_op jit(solution)/shard_map/ppermute | solution.py:224
  12.1 0.0 copy-start.1
  12.1 0.9 copy-done.1
  13.0 0.2 shard_map.77
  13.2 0.0 copy-start
  13.3 2.0 collective-permute-start.1
  15.3 0.8 copy.24.probs_ref
  16.1 0.0 copy-start.2
  16.1 0.9 copy-done.2
  17.0 0.1 shard_map.76
  17.1 6.7 %collective-permute-done.1.hidden_theirs_ref = bf16[400,128]{1,0:T(8,128)(2,1)S(1)} collective-permute-done((bf16[400,128]{1,0:T(8,128)(2,1)S(1)}, bf16[400,128]{1,0:T(8,128)(2,1)S(1)}, u32[]{:S(2)}, u32[]{:S(2)}) %collective-permute-start.1) | collective-permute-done | bytes 102432 | tf_op jit(solution)/shard_map/ppermute | solution.py:230
  23.7 0.0 copy-start.7
  23.7 0.0 collective-permute-done
  23.7 0.0 copy-start.6
  23.7 0.8 copy-done.6
  24.5 0.0 all-gather.6.cloned.1.call-update
  24.5 0.8 copy.25.ids_ref
  25.3 60.4 %all-gather = bf16[64,4096]{1,0:T(8,128)(2,1)S(1)} all-gather(bf16[16,4096]{1,0:T(8,128)(2,1)S(1)} %shard_map.76), channel_id=2, replica_groups=mesh['dp'=8,'y'=4,'zq'=4,'par'=2,'tensor'=4] {'tensor'}, dimensions={0}, use_global_device_ids=true | all-gather | bytes 655360 | tf_op jit(solution)/shard_map/all_gather | solution.py:242
  85.7 1.7 shard_map.78
  87.4 0.0 all-gather.6.cloned.1.call-done
  87.4 9.9 %all-to-all-start = ((bf16[16,8,4096]{2,1,0:T(8,128)(2,1)}), bf16[16,8,4096]{2,1,0:T(8,128)(2,1)S(1)}, u32[]{:S(2)}, u32[]{:S(2)}) async-start(bf16[16,8,4096]{2,1,0:T(8,128)(2,1)} %bitcast.4), calls=%async_computation | async-start | bytes 2097152 | tf_op jit(solution)/shard_map/all_to_all | solution.py:252
  97.3 0.0 all-gather.8.cloned.1.call-start
  97.4 0.7 pad_maximum_fusion
  98.1 0.0 all-gather.8.cloned.1.call-update
  98.1 0.1 reshape.43
  98.2 0.1 fusion.1
  98.3 0.2 reduce_window_sum.11
  98.5 0.2 select_reduce_fusion.1
  98.6 0.1 dynamic_slice.7
  98.7 29.9 %all-to-all-done = bf16[16,8,4096]{2,1,0:T(8,128)(2,1)S(1)} async-done(((bf16[16,8,4096]{2,1,0:T(8,128)(2,1)}), bf16[16,8,4096]{2,1,0:T(8,128)(2,1)S(1)}, u32[]{:S(2)}, u32[]{:S(2)}) %all-to-all-start) | async-done | bytes 1048608 | tf_op jit(solution)/shard_map/all_to_all | solution.py:252
  128.6 0.0 copy-start.4
  128.6 0.0 copy-done
  128.6 0.0 copy-done.7
  128.7 1.0 copy-done.4
  129.6 8.5 %shard_map.79 = (bf16[400,128]{1,0:T(8,128)(2,1)}, bf16[400,128]{1,0:T(8,128)(2,1)}, f32[16,128]{1,0:T(8,128)}, bf16[8,128,512]{2,1,0:T(8,128)(2,1)}) custom-call(bf16[128,4096]{1,0:T(8,128)(2,1)} %bitcast.21, bf16[400,4096]{1,0:T(8,128)(2,1)} %bitcast.22, bf16[8,400,512]{2,1,0:T(8,128)(2,1)} %bitcast.23, bf16[400,128]{1,0:T(8,128)(2,1)} %copy-done, ...), custom_call_target="tpu_custom_call" | custom-call | tf_op jit(solution)/shard_map/pallas_call | solution.py:263
  138.1 0.0 copy-start.8
  138.1 0.0 copy-start.3
  138.1 4.9 %all-to-all-start.1 = ((bf16[8,128,512]{2,1,0:T(8,128)(2,1)}), bf16[8,128,512]{2,1,0:T(8,128)(2,1)S(1)}, u32[]{:S(2)}, u32[]{:S(2)}) async-start(bf16[8,128,512]{2,1,0:T(8,128)(2,1)} %get-tuple-element.30), calls=%async_computation.1 | async-start | bytes 2097152 | tf_op jit(solution)/shard_map/all_to_all | solution.py:289
  143.1 23.8 %psum.7 = f32[16,128]{1,0:T(8,128)} all-reduce(f32[16,128]{1,0:T(8,128)} %get-tuple-element.32), channel_id=1, replica_groups=mesh['dp'=8,'y'=4,'zq'=4,'par'=2,'tensor'=4] {'tensor'}, use_global_device_ids=true, to_apply=%region_2.3 | all-reduce | flops 2048 | bytes 16384 | tf_op jit(solution)/shard_map/psum | solution.py:290
  166.9 0.0 all-gather.8.cloned.1.call-done
  166.9 0.0 all-to-all-done.1.rows_ref
  166.9 0.0 copy-start.5
  166.9 1.0 copy-done.5
  167.9 7.2 %shard_map.81 = (f32[400,512]{1,0:T(8,128)}, bf16[400,512]{1,0:T(8,128)(2,1)}) custom-call(bf16[8,2,400,128]{3,2,1,0:T(8,128)(2,1)} %bitcast.24, bf16[8,128,512]{2,1,0:T(8,128)(2,1)} %copy-done.5), custom_call_target="tpu_custom_call" | custom-call | tf_op jit(solution)/shard_map/pallas_call | solution.py:293
  175.1 6.3 %collective-permute-start.3 = (bf16[400,512]{1,0:T(8,128)(2,1)}, bf16[400,512]{1,0:T(8,128)(2,1)S(1)}, u32[]{:S(2)}, u32[]{:S(2)}) collective-permute-start(bf16[400,512]{1,0:T(8,128)(2,1)} %get-tuple-element.34), channel_id=1, source_target_pairs={{0,4},{4,0},{1,5},{5,1},{2,6},{6,2},{3,7},{7,3},{8,12},{12,8},{9,1... | collective-permute-start | bytes 1228808 | tf_op jit(solution)/shard_map/ppermute | solution.py:314
  181.4 0.1 iota_add_fusion
  181.5 0.0 copy-done.8
  181.5 1.9 collective-permute-start.2
  183.4 4.5 %all-to-all-start.2 = ((f32[16,1,128]{2,1,0:T(1,128)}), f32[16,1,128]{2,1,0:T(1,128)S(1)}, u32[]{:S(2)}, u32[]{:S(2)}) async-start(f32[16,1,128]{2,1,0:T(1,128)} %bitcast.13), calls=%async_computation.2 | async-start | bytes 16384 | tf_op jit(solution)/shard_map/all_to_all | solution.py:315
  187.9 3.8 %collective-permute-done.2.theirs_ref = bf16[400,128]{1,0:T(8,128)(2,1)S(1)} collective-permute-done((bf16[400,128]{1,0:T(8,128)(2,1)S(1)}, bf16[400,128]{1,0:T(8,128)(2,1)S(1)}, u32[]{:S(2)}, u32[]{:S(2)}) %collective-permute-start.2) | collective-permute-done | bytes 102432 | tf_op jit(solution)/shard_map/ppermute | solution.py:291
  191.7 0.0 copy-done.3
  191.7 0.9 shard_map.80
  192.6 7.0 %all-to-all-done.2 = f32[16,1,128]{2,1,0:T(1,128)S(1)} async-done(((f32[16,1,128]{2,1,0:T(1,128)}), f32[16,1,128]{2,1,0:T(1,128)S(1)}, u32[]{:S(2)}, u32[]{:S(2)}) %all-to-all-start.2) | async-done | bytes 8224 | tf_op jit(solution)/shard_map/all_to_all | solution.py:315
  199.6 0.4 select_reduce_fusion
  200.1 0.1 reshape.44
  200.2 0.7 copy.29
  200.8 0.0 collective-permute-done.3
  200.8 2.0 fusion
  (4 shorter events, 0.0 us)
Async XLA Ops:
  7.2 80.2 %all-gather.6.cloned.1.call-start = ((), (), s32[]{:S(2)}) async-start(), calls=%async_computation.3 | async-start | bytes 3686400 | tf_op jit(solution)/shard_map/all_gather | solution.py:239
  8.3 15.5 %collective-permute-start = (bf16[400,512]{1,0:T(8,128)(2,1)S(1)}, bf16[400,512]{1,0:T(8,128)(2,1)S(1)}, u32[]{:S(2)}, u32[]{:S(2)}) collective-permute-start(bf16[400,512]{1,0:T(8,128)(2,1)S(1)} %dynamic-slice_bitcast_fusion), channel_id=1, source_target_pairs={{0,4},{4,0},{1,5},{5,1},{2,6},{6,2},{3,7},{7,3},{8,12},{12,8},{9,1... | collective-permute-start | bytes 1228808 | tf_op jit(solution)/shard_map/ppermute | solution.py:224
  12.1 0.9 copy-start.1
  13.2 115.4 %copy-start = (bf16[400,128]{1,0:T(8,128)(2,1)}, bf16[400,128]{1,0:T(8,128)(2,1)S(1)}, u32[]{:S(2)}) copy-start(bf16[400,128]{1,0:T(8,128)(2,1)S(1)} %get-tuple-element.26.hidden_ref) | copy-start | bytes 307204
  13.3 10.5 %collective-permute-start.1 = (bf16[400,128]{1,0:T(8,128)(2,1)S(1)}, bf16[400,128]{1,0:T(8,128)(2,1)S(1)}, u32[]{:S(2)}, u32[]{:S(2)}) collective-permute-start(bf16[400,128]{1,0:T(8,128)(2,1)S(1)} %get-tuple-element.20), channel_id=1, source_target_pairs={{0,4},{4,0},{1,5},{5,1},{2,6},{6,2},{3,7},{7,3},{8,12},{12,8},{9,1... | collective-permute-start | bytes 307208 | tf_op jit(solution)/shard_map/ppermute | solution.py:230
  16.1 0.9 copy-start.2
  23.7 104.9 %copy-start.7 = (bf16[400,128]{1,0:T(8,128)(2,1)}, bf16[400,128]{1,0:T(8,128)(2,1)S(1)}, u32[]{:S(2)}) copy-start(bf16[400,128]{1,0:T(8,128)(2,1)S(1)} %collective-permute-done.1.hidden_theirs_ref) | copy-start | bytes 307204
  23.7 0.8 copy-start.6
  87.4 41.3 %all-to-all-start = ((bf16[16,8,4096]{2,1,0:T(8,128)(2,1)}), bf16[16,8,4096]{2,1,0:T(8,128)(2,1)S(1)}, u32[]{:S(2)}, u32[]{:S(2)}) async-start(bf16[16,8,4096]{2,1,0:T(8,128)(2,1)} %bitcast.4), calls=%async_computation | async-start | bytes 2097152 | tf_op jit(solution)/shard_map/all_to_all | solution.py:252
  97.3 69.6 %all-gather.8.cloned.1.call-start = ((), (), s32[]{:S(2)}) async-start(), calls=%async_computation.4 | async-start | bytes 1843200 | tf_op jit(solution)/shard_map/all_gather | solution.py:240
  128.6 1.0 copy-start.4
  138.1 43.3 %copy-start.8 = (bf16[400,128]{1,0:T(8,128)(2,1)S(1)}, bf16[400,128]{1,0:T(8,128)(2,1)}, u32[]{:S(2)}) copy-start(bf16[400,128]{1,0:T(8,128)(2,1)} %get-tuple-element.29) | copy-start | bytes 307204
  138.1 53.6 %copy-start.3 = (bf16[400,128]{1,0:T(8,128)(2,1)S(1)}, bf16[400,128]{1,0:T(8,128)(2,1)}, u32[]{:S(2)}) copy-start(bf16[400,128]{1,0:T(8,128)(2,1)} %get-tuple-element.28.mine_ref) | copy-start | bytes 307204
  138.1 28.8 %all-to-all-start.1 = ((bf16[8,128,512]{2,1,0:T(8,128)(2,1)}), bf16[8,128,512]{2,1,0:T(8,128)(2,1)S(1)}, u32[]{:S(2)}, u32[]{:S(2)}) async-start(bf16[8,128,512]{2,1,0:T(8,128)(2,1)} %get-tuple-element.30), calls=%async_computation.1 | async-start | bytes 2097152 | tf_op jit(solution)/shard_map/all_to_all | solution.py:289
  166.9 1.0 copy-start.5
  175.1 25.7 %collective-permute-start.3 = (bf16[400,512]{1,0:T(8,128)(2,1)}, bf16[400,512]{1,0:T(8,128)(2,1)S(1)}, u32[]{:S(2)}, u32[]{:S(2)}) collective-permute-start(bf16[400,512]{1,0:T(8,128)(2,1)} %get-tuple-element.34), channel_id=1, source_target_pairs={{0,4},{4,0},{1,5},{5,1},{2,6},{6,2},{3,7},{7,3},{8,12},{12,8},{9,1... | collective-permute-start | bytes 1228808 | tf_op jit(solution)/shard_map/ppermute | solution.py:314
  181.5 10.2 %collective-permute-start.2 = (bf16[400,128]{1,0:T(8,128)(2,1)S(1)}, bf16[400,128]{1,0:T(8,128)(2,1)S(1)}, u32[]{:S(2)}, u32[]{:S(2)}) collective-permute-start(bf16[400,128]{1,0:T(8,128)(2,1)S(1)} %copy-done.8), channel_id=1, source_target_pairs={{0,4},{4,0},{1,5},{5,1},{2,6},{6,2},{3,7},{7,3},{8,12},{12,8},{9,1... | collective-permute-start | bytes 307208 | tf_op jit(solution)/shard_map/ppermute | solution.py:291
  183.4 16.2 %all-to-all-start.2 = ((f32[16,1,128]{2,1,0:T(1,128)}), f32[16,1,128]{2,1,0:T(1,128)S(1)}, u32[]{:S(2)}, u32[]{:S(2)}) async-start(f32[16,1,128]{2,1,0:T(1,128)} %bitcast.13), calls=%async_computation.2 | async-start | bytes 16384 | tf_op jit(solution)/shard_map/all_to_all | solution.py:315
Sparse Core Ops, SparseCore 0:
  24.7 52.4 all-gather.5
  101.4 35.5 all-gather.7

commit v5 on v4

--- a/solution.py
+++ b/solution.py
@@ -24,15 +24,14 @@
     place = lax.axis_index("tensor") * PAD
     lane = lax.broadcasted_iota(jnp.int32, (own_tokens, LANES), 1)
     token = lax.broadcasted_iota(jnp.int32, (own_tokens, LANES), 0)
-    here = lane == token + place
-    probs = probs_ref[...]
+    here = (lane == token + place).astype(jnp.bfloat16)
+    parts = [
+        jnp.dot(part, here, preferred_element_type=jnp.float32).astype(jnp.bfloat16)
+        for part in split3(probs_ref[...])
+    ]
     out_ref[:own_tokens, :] = cot_ref[...]
     out_ref[own_tokens:, :] = jnp.zeros((PAD - own_tokens, cot_ref.shape[1]), jnp.bfloat16)
-    rows = []
-    for k in range(2):
-        spread = jnp.sum(jnp.where(here, probs[:, k : k + 1], 0.0), axis=0, keepdims=True)
-        rows.append(jnp.concatenate(split3(spread), axis=1))
-    out_ref[own_tokens:, : 3 * LANES] = jnp.concatenate(rows, axis=0)
+    out_ref[own_tokens:, : 3 * LANES] = jnp.concatenate(parts, axis=1)
 
 
 def fill_kernel(own_tokens, experts, capacity, gathered_ref, ids_ref, out_ref):
@@ -42,15 +41,14 @@
     lane = lax.broadcasted_iota(jnp.int32, (group, LANES), 1)
     token = lax.broadcasted_iota(jnp.int32, (group, LANES), 0)
     here = lane == token + (PAD - own_tokens) * (token // own_tokens)
-    ids = ids_ref[...]
+    moved = jnp.dot(
+        ids_ref[...].astype(jnp.float32).astype(jnp.bfloat16),
+        here.astype(jnp.bfloat16),
+        preferred_element_type=jnp.float32,
+    ).astype(jnp.int32)
     lane_row = lax.broadcasted_iota(jnp.int32, (1, LANES), 1)
     real = (lane_row < span) & (lane_row % PAD < own_tokens)
-    spread = [
-        jnp.where(
-            real, jnp.sum(jnp.where(here, ids[:, k : k + 1], 0), axis=0, keepdims=True), -1
-        )
-        for k in range(2)
-    ]
+    spread = [jnp.where(real, moved[k : k + 1], -1) for k in range(2)]
     expert = lax.broadcasted_iota(jnp.int32, (experts, LANES), 0)
     named = [(spread[k] == expert).astype(jnp.float32) for k in range(2)]
     earlier_lane = lax.broadcasted_iota(jnp.int32, (LANES, LANES), 0)
@@ -102,13 +100,6 @@
     send_ref[...] = moved[:, rows // 2 :]
 
 
-def unsort_kernel(capacity, mine_ref, theirs_ref, out_ref):
-    rows = out_ref.shape[1]
-    order = parity_order(rows, capacity, False)
-    both = jnp.concatenate([mine_ref[...], theirs_ref[...]], axis=1)
-    out_ref[...] = jnp.dot(both, order, preferred_element_type=jnp.float32).astype(jnp.bfloat16)
-
-
 def product_kernel(
     capacity,
     rows_ref,
@@ -120,65 +111,91 @@
     theirs_ref,
     partial_ref,
     by_feature_ref,
+    both,
     total,
+    sems,
 ):
-    step = pl.program_id(0)
-
-    @pl.when(step == 0)
-    def _():
-        total[...] = jnp.zeros_like(total)
-
-    rows = rows_ref[...]
-    by_feature_ref[0] = rows
+    replicas, cols, chunk = weight_theirs_ref.shape
+    stages, _, width = both.shape
+    per_stage = width // chunk
+    copies = []
+    for stage in range(stages):
+        here = [
+            pltpu.make_async_copy(
+                weight_ref.at[:, stage * width : (stage + 1) * width],
+                both.at[stage, :cols],
+                sems.at[stage, 0],
+            )
+        ]
+        for part in range(per_stage):
+            here.append(
+                pltpu.make_async_copy(
+                    weight_theirs_ref.at[stage * per_stage + part],
+                    both.at[stage, cols:, part * chunk : (part + 1) * chunk],
+                    sems.at[stage, 1 + part],
+                )
+            )
+        for copy in here:
+            copy.start()
+        copies.append(here)
+    for index in range(replicas):
+        by_feature_ref[index] = rows_ref[:, index * chunk : (index + 1) * chunk]
     contract = (((1,), (1,)), ((), ()))
-    total[0] += lax.dot_general(
-        weight_ref[...], rows, contract, preferred_element_type=jnp.float32
-    )
-    total[1] += lax.dot_general(
-        weight_theirs_ref[0], rows, contract, preferred_element_type=jnp.float32
-    )
-
-    @pl.when(step == pl.num_programs(0) - 1)
-    def _():
-        mine, theirs = total[0], total[1]
-        mine_ref[...] = mine.astype(jnp.bfloat16)
-        theirs_ref[...] = theirs.astype(jnp.bfloat16)
-        summed = jnp.sum(
-            hidden_ref[...].astype(jnp.float32) * mine
-            + hidden_theirs_ref[...].astype(jnp.float32) * theirs,
-            axis=0,
-            keepdims=True,
-        )
-        lanes = summed.shape[1]
-        experts = partial_ref.shape[0]
-        of_expert = lax.broadcasted_iota(jnp.int32, (experts, lanes), 1) // capacity
-        expert = lax.broadcasted_iota(jnp.int32, (experts, lanes), 0)
-        spread = jnp.where(of_expert == expert, summed, 0.0)
-        at = lax.broadcasted_iota(jnp.int32, (lanes, LANES), 0) % capacity
-        slot = lax.broadcasted_iota(jnp.int32, (lanes, LANES), 1)
-        partial_ref[...] = jnp.dot(
-            spread,
-            (at == slot).astype(jnp.float32),
-            precision=lax.Precision.HIGHEST,
-            preferred_element_type=jnp.float32,
-        )
-
-
-def term_kernel(hidden_ref, rows_ref, mine_ref, theirs_ref, total):
-    step = pl.program_id(0)
-
-    @pl.when(step == 0)
-    def _():
-        total[...] = jnp.zeros_like(total)
-
-    rows = rows_ref[0]
-    for half in range(2):
-        total[half] += jnp.dot(hidden_ref[0, half], rows, preferred_element_type=jnp.float32)
-
-    @pl.when(step == pl.num_programs(0) - 1)
-    def _():
-        mine_ref[...] = total[0]
-        theirs_ref[...] = total[1].astype(jnp.bfloat16)
+    for stage in range(stages):
+        for copy in copies[stage]:
+            copy.wait()
+        rows = rows_ref[:, stage * width : (stage + 1) * width]
+        added = lax.dot_general(both[stage], rows, contract, preferred_element_type=jnp.float32)
+        total[...] = added if stage == 0 else total[...] + added
+    mine, theirs = total[:cols], total[cols:]
+    mine_ref[...] = mine.astype(jnp.bfloat16)
+    theirs_ref[...] = theirs.astype(jnp.bfloat16)
+    summed = jnp.sum(
+        hidden_ref[...].astype(jnp.float32) * mine
+        + hidden_theirs_ref[...].astype(jnp.float32) * theirs,
+        axis=0,
+        keepdims=True,
+    )
+    lanes = summed.shape[1]
+    experts = partial_ref.shape[0]
+    of_expert = lax.broadcasted_iota(jnp.int32, (experts, lanes), 1) // capacity
+    expert = lax.broadcasted_iota(jnp.int32, (experts, lanes), 0)
+    spread = jnp.where(of_expert == expert, summed, 0.0)
+    at = lax.broadcasted_iota(jnp.int32, (lanes, LANES), 0) % capacity
+    slot = lax.broadcasted_iota(jnp.int32, (lanes, LANES), 1)
+    partial_ref[...] = jnp.dot(
+        spread,
+        (at == slot).astype(jnp.float32),
+        precision=lax.Precision.HIGHEST,
+        preferred_element_type=jnp.float32,
+    )
+
+
+def term_of(hidden_ref, rows_ref, half):
+    replicas, depth, chunk = rows_ref.shape
+    rows = rows_ref[...].reshape(replicas * depth, chunk)
+    hidden = jnp.concatenate([hidden_ref[p, half] for p in range(replicas)], axis=1)
+    return jnp.dot(hidden, rows, preferred_element_type=jnp.float32)
+
+
+def send_kernel(hidden_ref, rows_ref, product_ref, out_ref):
+    chunk = rows_ref.shape[2]
+    out_ref[:, :chunk] = term_of(hidden_ref, rows_ref, 1).astype(jnp.bfloat16)
+    out_ref[:, chunk:] = product_ref[...]
+
+
+def keep_kernel(hidden_ref, rows_ref, out_ref):
+    out_ref[...] = term_of(hidden_ref, rows_ref, 0)
+
+
+def finish_kernel(capacity, term_ref, product_ref, swapped_ref, weight_ref, hidden_ref):
+    chunk = term_ref.shape[1]
+    term = term_ref[...] + swapped_ref[:, :chunk].astype(jnp.float32)
+    weight_ref[...] = term.astype(jnp.bfloat16)
+    order = parity_order(hidden_ref.shape[1], capacity, False)
+    both = jnp.concatenate([product_ref[...], swapped_ref[:, chunk:]], axis=1)
+    moved = jnp.dot(both, order, preferred_element_type=jnp.float32)
+    hidden_ref[...] = moved.astype(jnp.bfloat16)
 
 
 def assign_slots(flat_ids, experts):
@@ -216,7 +233,6 @@
     chunk = model_width // n_dp
     half = experts * capacity
     swap = [(0, 1), (1, 0)]
-    large = pltpu.CompilerParams(vmem_limit_bytes=56 << 20)
     small = pltpu.CompilerParams(vmem_limit_bytes=16 << 20)
 
     weight = down_weight.T
@@ -232,10 +248,8 @@
         pack_kernel,
         out_shape=jax.ShapeDtypeStruct((PAD, model_width), jnp.bfloat16),
         compiler_params=small,
-    )(cotangent, probs)
-    packed, weight_swapped, hidden_theirs = lax.optimization_barrier(
-        (packed, weight_swapped, hidden_theirs)
-    )
+    )(cotangent, probs.T)
+    packed, weight_swapped = lax.optimization_barrier((packed, weight_swapped))
     weight_theirs = lax.all_gather(weight_swapped, "dp", axis=0)
     hidden_all = lax.all_gather(jnp.stack([hidden_mine, hidden_theirs]), "dp", axis=0)
 
@@ -244,7 +258,7 @@
         functools.partial(fill_kernel, own_tokens, experts, capacity),
         out_shape=jax.ShapeDtypeStruct((half, model_width), jnp.bfloat16),
         compiler_params=pltpu.CompilerParams(vmem_limit_bytes=24 << 20),
-    )(gathered, expert_ids)
+    )(gathered, expert_ids.T)
     buffer, weight_theirs = lax.optimization_barrier((buffer, weight_theirs))
     buffer = buffer.reshape(experts, capacity, model_width)
     groups = windows(n_dp, n_y, n_q, n_par, members)
@@ -259,64 +273,61 @@
     own_keys = lax.dynamic_slice_in_dim(keys, start_row, own_tokens * 2)
     rows, own_keys = lax.optimization_barrier((rows, own_keys))
 
-    whole = pl.BlockSpec((hidden_cols, half), lambda i: (0, 0))
+    vmem = pl.BlockSpec(memory_space=pltpu.VMEM)
+    hbm = pl.BlockSpec(memory_space=pltpu.HBM)
+    stages = 4
     product, product_theirs, partial_value, by_feature = pl.pallas_call(
         functools.partial(product_kernel, capacity),
-        grid=(n_dp,),
-        in_specs=[
-            pl.BlockSpec((half, chunk), lambda i: (0, i)),
-            pl.BlockSpec((hidden_cols, chunk), lambda i: (0, i)),
-            pl.BlockSpec((1, hidden_cols, chunk), lambda i: (i, 0, 0)),
-            whole,
-            whole,
-        ],
-        out_specs=[
-            whole,
-            whole,
-            pl.BlockSpec((experts, LANES), lambda i: (0, 0)),
-            pl.BlockSpec((1, half, chunk), lambda i: (i, 0, 0)),
-        ],
+        in_specs=[vmem, hbm, hbm, vmem, vmem],
+        out_specs=[vmem] * 4,
         out_shape=[
             jax.ShapeDtypeStruct((hidden_cols, half), jnp.bfloat16),
             jax.ShapeDtypeStruct((hidden_cols, half), jnp.bfloat16),
             jax.ShapeDtypeStruct((experts, LANES), jnp.float32),
             jax.ShapeDtypeStruct((n_dp, half, chunk), jnp.bfloat16),
         ],
-        scratch_shapes=[pltpu.VMEM((2, hidden_cols, half), jnp.float32)],
-        compiler_params=large,
+        scratch_shapes=[
+            pltpu.VMEM((stages, 2 * hidden_cols, model_width // stages), jnp.bfloat16),
+            pltpu.VMEM((2 * hidden_cols, half), jnp.float32),
+            pltpu.SemaphoreType.DMA((stages, 1 + n_dp // stages)),
+        ],
+        compiler_params=pltpu.CompilerParams(vmem_limit_bytes=50 << 20),
     )(rows, weight, weight_theirs, hidden_mine, hidden_theirs)
 
     replica_rows = lax.all_to_all(by_feature, "dp", split_axis=0, concat_axis=0, tiled=True)
     partial_value = lax.psum(partial_value, "tensor")
-    product_swapped = lax.ppermute(product_theirs, "par", swap)
-    square = pl.BlockSpec((hidden_cols, chunk), lambda i: (0, 0))
-    term, term_theirs = pl.pallas_call(
-        term_kernel,
-        grid=(n_dp,),
-        in_specs=[
-            pl.BlockSpec((1, 2, hidden_cols, half), lambda i: (i, 0, 0, 0)),
-            pl.BlockSpec((1, half, chunk), lambda i: (i, 0, 0)),
+    partial_value, replica_rows = lax.optimization_barrier((partial_value, replica_rows))
+    term_cost = pl.CostEstimate(
+        flops=2 * n_dp * half * hidden_cols * chunk,
+        bytes_accessed=2 * n_dp * half * (hidden_cols + chunk) + 4 * hidden_cols * chunk,
+        transcendentals=0,
+    )
+    medium = pltpu.CompilerParams(vmem_limit_bytes=24 << 20)
+    sent = pl.pallas_call(
+        send_kernel,
+        out_shape=jax.ShapeDtypeStruct((hidden_cols, chunk + half), jnp.bfloat16),
+        cost_estimate=term_cost,
+        compiler_params=medium,
+    )(hidden_all, replica_rows, product_theirs)
+    swapped = lax.ppermute(sent, "par", swap)
+    term = pl.pallas_call(
+        keep_kernel,
+        out_shape=jax.ShapeDtypeStruct((hidden_cols, chunk), jnp.float32),
+        cost_estimate=term_cost,
+        compiler_params=medium,
+    )(hidden_all, replica_rows)
+    weight_grad, hidden_grad = pl.pallas_call(
+        functools.partial(finish_kernel, capacity),
+        out_shape=[
+            jax.ShapeDtypeStruct((hidden_cols, chunk), jnp.bfloat16),
+            jax.ShapeDtypeStruct((hidden_cols, 2 * half), jnp.bfloat16),
         ],
-        out_specs=[square, square],
-        out_shape=[
-            jax.ShapeDtypeStruct((hidden_cols, chunk), jnp.float32),
-            jax.ShapeDtypeStruct((hidden_cols, chunk), jnp.bfloat16),
-        ],
-        scratch_shapes=[pltpu.VMEM((2, hidden_cols, chunk), jnp.float32)],
-        compiler_params=large,
-    )(hidden_all, replica_rows)
-    hidden_grad = pl.pallas_call(
-        functools.partial(unsort_kernel, capacity),
-        out_shape=jax.ShapeDtypeStruct((hidden_cols, 2 * half), jnp.bfloat16),
-        compiler_params=small,
-    )(product, product_swapped)
-    partial_value, term_theirs = lax.optimization_barrier((partial_value, term_theirs))
-    term_swapped = lax.ppermute(term_theirs, "par", swap)
+        compiler_params=medium,
+    )(term, product, swapped)
+    weight_grad, hidden_grad = weight_grad.T, hidden_grad.T
     lookup = lax.all_to_all(
         partial_value, every, split_axis=0, concat_axis=0, axis_index_groups=groups, tiled=True
     )
-    weight_grad = (term + term_swapped.astype(jnp.float32)).astype(jnp.bfloat16).T
-    hidden_grad = hidden_grad.T
 
     expert = lax.broadcasted_iota(jnp.int32, (1, experts, LANES), 1)
     slot = lax.broadcasted_iota(jnp.int32, (1, experts, LANES), 2)

time: 211 us -> 199 us (0.943)
  Pallas kernels: 18.6 us -> 12.3 us
    all_to_all x1, waiting for transfers between devices: 29.9 us -> 8.24 us  [shards(): lax.all_to_all(buffer, every, split_axis=0, concat_axis=0, axis_index_gro...]
    ppermute x1, waiting for transfers between devices: 6.67 us -> 18.9 us  [shards(): hidden_theirs = lax.ppermute(hidden_send, 'par', swap)]
    ppermute x1, waiting for transfers between devices: 0.01 us -> 7.73 us  [shards(): weight_swapped = lax.ppermute(weight_send, 'par', swap)]
    pallas_call x3 -> x4, Pallas kernels: 16.6 us -> 10.3 us  [the longest x1 6.2 us: shards(): pl.pallas_call(functools.partial(product_kernel, capacity), in_specs=[vme...]
    all_to_all x1, waiting for transfers between devices: 7.02 us -> 11.1 us  [shards(): lax.all_to_all(partial_value, every, split_axis=0, concat_axis=0, axis_in...]
    ppermute x2 -> x1, waiting for transfers between devices: 3.84 us -> 0.01 us  [shards(): swapped = lax.ppermute(sent, 'par', swap)]
    ppermute x2 -> x1, starting transfers between devices: 8.2 us -> 6.38 us  [shards(): swapped = lax.ppermute(sent, 'par', swap)]
    unnamed x21 -> x25, local copies, waits for them, and re-layouts: 6.79 us -> 6.84 us
  transfers between devices with their start and end apart: 9 -> 8, of which waited for: 4 -> 4; matrix products, arithmetic and copies ran while one was open for 2% -> 1% of each run, Pallas kernels for 5% -> 4%
where the time goes in v5:
time: 199 us; the launch traced here: 198 us
  blocking collectives  83.9 us (42%)
  waiting for transfers between devices  46 us (23%)
  starting transfers between devices  31.8 us (16%)
  between operations  14.2 us (7%)
  Pallas kernels  12.3 us (6%)
  local copies, waits for them, and re-layouts  8.2 us (4%)
    all_gather x1, blocking collectives, shards(): gathered = lax.all_gather(packed, 'tensor', axis=0)  60.4 us
    psum x1, blocking collectives, shards(): partial_value = lax.psum(partial_value, 'tensor')  23.5 us
    ppermute x1, waiting for transfers between devices, shards(): hidden_theirs = lax.ppermute(hidden_send, 'par', swap)  18.9 us
    all_to_all x1, waiting for transfers between devices, shards(): lax.all_to_all(partial_value, every, split_axis=0, concat_axis=0, axis_in...  11.1 us
    all_to_all x1, starting transfers between devices, shards(): lax.all_to_all(buffer, every, split_axis=0, concat_axis=0, axis_index_gro...  9.92 us
    all_to_all x1, waiting for transfers between devices, shards(): lax.all_to_all(buffer, every, split_axis=0, concat_axis=0, axis_index_gro...  8.24 us
    ppermute x1, waiting for transfers between devices, shards(): weight_swapped = lax.ppermute(weight_send, 'par', swap)  7.73 us
    unnamed x25, local copies, waits for them, and re-layouts  6.84 us
  transfers between devices with their start and end apart: 8, of which 4 were waited for; matrix products, arithmetic and copies ran while one was open for 1% of the time, Pallas kernels for 4%

profile of v5, /device:TPU:6, one launch (start us, length us, event | category | flops | bytes accessed | tf_op | source)
XLA Modules:
  0.0 198.1 jit_solution(11920665331038114444)
XLA Ops:
  7.2 0.0 copy-start.2
  7.2 0.0 all-gather.8.cloned.1.call-start
  7.2 0.0 copy-start.9
  7.2 1.1 dynamic-slice_bitcast_fusion
  8.3 3.8 %collective-permute-start.1 = (bf16[400,512]{1,0:T(8,128)(2,1)S(1)}, bf16[400,512]{1,0:T(8,128)(2,1)S(1)}, u32[]{:S(2)}, u32[]{:S(2)}) collective-permute-start(bf16[400,512]{1,0:T(8,128)(2,1)S(1)} %dynamic-slice_bitcast_fusion), channel_id=1, source_target_pairs={{0,4},{4,0},{1,5},{5,1},{2,6},{6,2},{3,7},{7,3},{8,12},{12,8},{9,1... | collective-permute-start | bytes 1228808 | tf_op jit(solution)/shard_map/ppermute | solution.py:240
  12.1 0.0 copy-start.3
  12.2 0.9 copy-done.3
  13.1 0.0 copy-start.6
  13.1 0.7 copy-done.6
  13.7 0.1 shard_map.77
  13.9 7.7 %collective-permute-done.1 = bf16[400,512]{1,0:T(8,128)(2,1)S(1)} collective-permute-done((bf16[400,512]{1,0:T(8,128)(2,1)S(1)}, bf16[400,512]{1,0:T(8,128)(2,1)S(1)}, u32[]{:S(2)}, u32[]{:S(2)}) %collective-permute-start.1) | collective-permute-done | bytes 409632 | tf_op jit(solution)/shard_map/ppermute | solution.py:240
  21.6 0.0 copy-start.10
  21.6 0.7 copy-done.10
  22.3 0.0 all-gather.8.cloned.1.call-update
  22.4 60.4 %all-gather.1 = bf16[64,4096]{1,0:T(8,128)(2,1)S(1)} all-gather(bf16[16,4096]{1,0:T(8,128)(2,1)S(1)} %shard_map.77), channel_id=3, replica_groups=mesh['dp'=8,'y'=4,'zq'=4,'par'=2,'tensor'=4] {'tensor'}, dimensions={0}, use_global_device_ids=true | all-gather | bytes 655360 | tf_op jit(solution)/shard_map/all_gather | solution.py:256
  82.8 0.0 copy-start.8
  82.8 0.7 copy-done.8
  83.5 1.7 shard_map.78
  85.2 0.0 all-gather.8.cloned.1.call-done
  85.2 9.9 %all-to-all-start = ((bf16[16,8,4096]{2,1,0:T(8,128)(2,1)}), bf16[16,8,4096]{2,1,0:T(8,128)(2,1)S(1)}, u32[]{:S(2)}, u32[]{:S(2)}) async-start(bf16[16,8,4096]{2,1,0:T(8,128)(2,1)} %bitcast.9), calls=%async_computation | async-start | bytes 2097152 | tf_op jit(solution)/shard_map/all_to_all | solution.py:266
  95.1 0.0 all-gather.6.cloned.1.call-start
  95.1 0.0 copy-done.2
  95.2 0.2 shard_map.76
  95.4 2.6 %collective-permute-start = (bf16[400,128]{1,0:T(8,128)(2,1)S(1)}, bf16[400,128]{1,0:T(8,128)(2,1)S(1)}, u32[]{:S(2)}, u32[]{:S(2)}) collective-permute-start(bf16[400,128]{1,0:T(8,128)(2,1)S(1)} %get-tuple-element.20), channel_id=1, source_target_pairs={{0,4},{4,0},{1,5},{5,1},{2,6},{6,2},{3,7},{7,3},{8,12},{12,8},{9,1... | collective-permute-start | bytes 307208 | tf_op jit(solution)/shard_map/ppermute | solution.py:246
  98.0 18.9 %collective-permute-done.hidden_theirs_ref = bf16[400,128]{1,0:T(8,128)(2,1)S(1)} collective-permute-done((bf16[400,128]{1,0:T(8,128)(2,1)S(1)}, bf16[400,128]{1,0:T(8,128)(2,1)S(1)}, u32[]{:S(2)}, u32[]{:S(2)}) %collective-permute-start) | collective-permute-done | bytes 102432 | tf_op jit(solution)/shard_map/ppermute | solution.py:246
  116.8 0.7 pad_maximum_fusion
  117.5 0.0 all-gather.6.cloned.1.call-update
  117.6 0.0 copy-done.9
  117.6 0.1 copy.18
  117.7 0.1 reshape.43
  117.8 0.1 fusion
  117.9 0.2 reduce_window_sum.11
  118.0 0.2 select_reduce_fusion.1
  118.2 0.1 dynamic_slice.7
  118.3 8.2 %all-to-all-done = bf16[16,8,4096]{2,1,0:T(8,128)(2,1)S(1)} async-done(((bf16[16,8,4096]{2,1,0:T(8,128)(2,1)}), bf16[16,8,4096]{2,1,0:T(8,128)(2,1)S(1)}, u32[]{:S(2)}, u32[]{:S(2)}) %all-to-all-start) | async-done | bytes 1048608 | tf_op jit(solution)/shard_map/all_to_all | solution.py:266
  126.6 6.2 %shard_map.79 = (bf16[400,128]{1,0:T(8,128)(2,1)S(1)}, bf16[400,128]{1,0:T(8,128)(2,1)S(1)}, f32[16,128]{1,0:T(8,128)S(1)}, bf16[8,128,512]{2,1,0:T(8,128)(2,1)}) custom-call(bf16[128,4096]{1,0:T(8,128)(2,1)S(1)} %bitcast.21, bf16[400,4096]{1,0:T(8,128)(2,1)} %bitcast.28, bf16[8,400,512]{2,1,0:T(8,128)(2,1)} %bitcast.29, ...), custom_call_target="tpu_custom_call" | custom-call | tf_op jit(solution)/shard_map/pallas_call | solution.py:279
  132.8 0.0 copy-start.4
  132.8 0.6 copy-done.4
  133.4 0.0 copy-start.7
  133.4 4.9 %all-to-all-start.1 = ((bf16[8,128,512]{2,1,0:T(8,128)(2,1)}), bf16[8,128,512]{2,1,0:T(8,128)(2,1)S(1)}, u32[]{:S(2)}, u32[]{:S(2)}) async-start(bf16[8,128,512]{2,1,0:T(8,128)(2,1)} %get-tuple-element.27), calls=%async_computation.1 | async-start | bytes 2097152 | tf_op jit(solution)/shard_map/all_to_all | solution.py:297
  138.3 23.5 %psum.7 = f32[16,128]{1,0:T(8,128)} all-reduce(f32[16,128]{1,0:T(8,128)S(1)} %get-tuple-element.26), channel_id=1, replica_groups=mesh['dp'=8,'y'=4,'zq'=4,'par'=2,'tensor'=4] {'tensor'}, use_global_device_ids=true, to_apply=%region_2.3 | all-reduce | flops 2048 | bytes 16384 | tf_op jit(solution)/shard_map/psum | solution.py:298
  161.8 0.0 all-to-all-done.1.rows_ref
  161.8 0.0 all-gather.6.cloned.1.call-done
  161.8 0.0 copy-start
  161.8 1.4 copy-done
  163.2 0.0 copy-start.1
  163.2 1.4 shard_map.81
  164.6 6.4 %collective-permute-start.2 = (bf16[400,640]{1,0:T(8,128)(2,1)}, bf16[400,640]{1,0:T(8,128)(2,1)}, u32[]{:S(2)}, u32[]{:S(2)}) collective-permute-start(bf16[400,640]{1,0:T(8,128)(2,1)} %shard_map.81), channel_id=1, source_target_pairs={{0,4},{4,0},{1,5},{5,1},{2,6},{6,2},{3,7},{7,3},{8,12},{12,8},{9,1... | collective-permute-start | bytes 1536008 | tf_op jit(solution)/shard_map/ppermute | solution.py:312
  171.0 0.1 iota_add_fusion
  171.1 4.1 %all-to-all-start.2 = ((f32[16,1,128]{2,1,0:T(1,128)}), f32[16,1,128]{2,1,0:T(1,128)S(1)}, u32[]{:S(2)}, u32[]{:S(2)}) async-start(f32[16,1,128]{2,1,0:T(1,128)} %bitcast.15), calls=%async_computation.2 | async-start | bytes 16384 | tf_op jit(solution)/shard_map/all_to_all | solution.py:328
  175.2 0.0 copy-done.7
  175.2 0.1 copy.20
  175.3 0.0 copy-done.1
  175.3 0.6 shard_map.80.term_ref
  175.9 11.1 %all-to-all-done.2 = f32[16,1,128]{2,1,0:T(1,128)S(1)} async-done(((f32[16,1,128]{2,1,0:T(1,128)}), f32[16,1,128]{2,1,0:T(1,128)S(1)}, u32[]{:S(2)}, u32[]{:S(2)}) %all-to-all-start.2) | async-done | bytes 8224 | tf_op jit(solution)/shard_map/all_to_all | solution.py:328
  187.0 0.4 select_reduce_fusion
  187.4 0.1 reshape.44
  187.5 0.7 copy.21
  188.2 0.0 collective-permute-done.2.swapped_ref
  188.2 0.0 copy-start.5
  188.2 0.9 copy-done.5
  189.1 2.1 %shard_map.82 = (bf16[400,512]{1,0:T(8,128)(2,1)}, bf16[400,256]{1,0:T(8,128)(2,1)}) custom-call(f32[400,512]{1,0:T(8,128)S(1)} %shard_map.80.term_ref, bf16[400,128]{1,0:T(8,128)(2,1)S(1)} %copy-done.5, bf16[400,640]{1,0:T(8,128)(2,1)} %collective-permute-done.2.swapped_ref), custom_call_target="tpu_custom_call" | custom-call | tf_op jit(solution)/shard_map/pallas_call | solution.py:319
  (4 shorter events, 0.0 us)
Async XLA Ops:
  7.2 88.0 %copy-start.2 = (bf16[256,400]{0,1:T(8,128)(2,1)S(1)}, bf16[256,400]{0,1:T(8,128)(2,1)}, u32[]{:S(2)}) copy-start(bf16[256,400]{0,1:T(8,128)(2,1)} %param.8) | copy-start | bytes 614404
  7.2 78.0 %all-gather.8.cloned.1.call-start = ((), (), s32[]{:S(2)}) async-start(), calls=%async_computation.4 | async-start | bytes 3686400 | tf_op jit(solution)/shard_map/all_gather | solution.py:253
  7.2 110.3 %copy-start.9 = (s32[56,2]{0,1:T(2,128)S(1)}, s32[56,2]{0,1:T(2,128)}, u32[]{:S(2)}) copy-start(s32[56,2]{0,1:T(2,128)} %param.7) | copy-start | bytes 1348
  8.3 13.3 %collective-permute-start.1 = (bf16[400,512]{1,0:T(8,128)(2,1)S(1)}, bf16[400,512]{1,0:T(8,128)(2,1)S(1)}, u32[]{:S(2)}, u32[]{:S(2)}) collective-permute-start(bf16[400,512]{1,0:T(8,128)(2,1)S(1)} %dynamic-slice_bitcast_fusion), channel_id=1, source_target_pairs={{0,4},{4,0},{1,5},{5,1},{2,6},{6,2},{3,7},{7,3},{8,12},{12,8},{9,1... | collective-permute-start | bytes 1228808 | tf_op jit(solution)/shard_map/ppermute | solution.py:240
  12.1 0.9 copy-start.3
  13.1 0.7 copy-start.6
  21.6 0.8 copy-start.10
  82.8 0.7 copy-start.8
  85.2 41.4 %all-to-all-start = ((bf16[16,8,4096]{2,1,0:T(8,128)(2,1)}), bf16[16,8,4096]{2,1,0:T(8,128)(2,1)S(1)}, u32[]{:S(2)}, u32[]{:S(2)}) async-start(bf16[16,8,4096]{2,1,0:T(8,128)(2,1)} %bitcast.9), calls=%async_computation | async-start | bytes 2097152 | tf_op jit(solution)/shard_map/all_to_all | solution.py:266
  95.1 66.7 %all-gather.6.cloned.1.call-start = ((), (), s32[]{:S(2)}) async-start(), calls=%async_computation.3 | async-start | bytes 1843200 | tf_op jit(solution)/shard_map/all_gather | solution.py:254
  95.4 21.4 %collective-permute-start = (bf16[400,128]{1,0:T(8,128)(2,1)S(1)}, bf16[400,128]{1,0:T(8,128)(2,1)S(1)}, u32[]{:S(2)}, u32[]{:S(2)}) collective-permute-start(bf16[400,128]{1,0:T(8,128)(2,1)S(1)} %get-tuple-element.20), channel_id=1, source_target_pairs={{0,4},{4,0},{1,5},{5,1},{2,6},{6,2},{3,7},{7,3},{8,12},{12,8},{9,1... | collective-permute-start | bytes 307208 | tf_op jit(solution)/shard_map/ppermute | solution.py:246
  132.8 0.6 copy-start.4
  133.4 41.8 %copy-start.7 = (f32[14,2]{0,1:T(2,128)S(1)}, f32[14,2]{0,1:T(2,128)}, u32[]{:S(2)}) copy-start(f32[14,2]{0,1:T(2,128)} %param.6) | copy-start | bytes 340
  133.4 28.4 %all-to-all-start.1 = ((bf16[8,128,512]{2,1,0:T(8,128)(2,1)}), bf16[8,128,512]{2,1,0:T(8,128)(2,1)S(1)}, u32[]{:S(2)}, u32[]{:S(2)}) async-start(bf16[8,128,512]{2,1,0:T(8,128)(2,1)} %get-tuple-element.27), calls=%async_computation.1 | async-start | bytes 2097152 | tf_op jit(solution)/shard_map/all_to_all | solution.py:297
  161.8 1.4 copy-start
  163.2 12.1 %copy-start.1 = (bf16[16,400,128]{2,1,0:T(8,128)(2,1)S(1)}, bf16[16,400,128]{2,1,0:T(8,128)(2,1)}, u32[]{:S(2)}) copy-start(bf16[16,400,128]{2,1,0:T(8,128)(2,1)} %all-gather.6.cloned.1.call-done) | copy-start | bytes 4915204
  164.6 23.6 %collective-permute-start.2 = (bf16[400,640]{1,0:T(8,128)(2,1)}, bf16[400,640]{1,0:T(8,128)(2,1)}, u32[]{:S(2)}, u32[]{:S(2)}) collective-permute-start(bf16[400,640]{1,0:T(8,128)(2,1)} %shard_map.81), channel_id=1, source_target_pairs={{0,4},{4,0},{1,5},{5,1},{2,6},{6,2},{3,7},{7,3},{8,12},{12,8},{9,1... | collective-permute-start | bytes 1536008 | tf_op jit(solution)/shard_map/ppermute | solution.py:312
  171.1 15.9 %all-to-all-start.2 = ((f32[16,1,128]{2,1,0:T(1,128)}), f32[16,1,128]{2,1,0:T(1,128)S(1)}, u32[]{:S(2)}, u32[]{:S(2)}) async-start(f32[16,1,128]{2,1,0:T(1,128)} %bitcast.15), calls=%async_computation.2 | async-start | bytes 16384 | tf_op jit(solution)/shard_map/all_to_all | solution.py:328
  188.2 0.9 copy-start.5
Sparse Core Ops, SparseCore 0:
  22.5 52.4 all-gather.7
  117.7 41.8 all-gather.5

commit v6 on v5

--- a/solution.py
+++ b/solution.py
@@ -7,8 +7,9 @@
 from jax.experimental.pallas import tpu as pltpu
 from jax.sharding import Mesh, PartitionSpec as P
 
-PAD = 16
 LANES = 128
+SUBLANES = 8
+PARTS = 3
 
 
 def split3(value):
@@ -20,43 +21,60 @@
 
 
 def pack_kernel(cot_ref, probs_ref, out_ref):
-    own_tokens = cot_ref.shape[0]
-    place = lax.axis_index("tensor") * PAD
+    own_tokens, width = cot_ref.shape
+    rest = own_tokens - SUBLANES
+    piece = width // (PARTS + 1)
+    out_ref[:, :width] = cot_ref[:SUBLANES, :]
+    row = lax.broadcasted_iota(jnp.int32, (SUBLANES, own_tokens), 0)
+    token = lax.broadcasted_iota(jnp.int32, (SUBLANES, own_tokens), 1)
+    body = ((row < rest) & (token == SUBLANES + row)).astype(jnp.bfloat16)
+    last = cot_ref[:, PARTS * piece :]
+    for k in range(PARTS):
+        source = SUBLANES + (row - rest) * PARTS + k
+        tail = ((row >= rest) & (token == source)).astype(jnp.bfloat16)
+        moved = jnp.dot(
+            body, cot_ref[:, k * piece : (k + 1) * piece], preferred_element_type=jnp.float32
+        ) + jnp.dot(tail, last, preferred_element_type=jnp.float32)
+        start = width + k * piece
+        out_ref[:, start : start + piece] = moved.astype(jnp.bfloat16)
+    place = lax.axis_index("tensor") * own_tokens
     lane = lax.broadcasted_iota(jnp.int32, (own_tokens, LANES), 1)
-    token = lax.broadcasted_iota(jnp.int32, (own_tokens, LANES), 0)
-    here = (lane == token + place).astype(jnp.bfloat16)
+    owner = lax.broadcasted_iota(jnp.int32, (own_tokens, LANES), 0)
+    here = (lane == owner + place).astype(jnp.bfloat16)
     parts = [
-        jnp.dot(part, here, preferred_element_type=jnp.float32).astype(jnp.bfloat16)
-        for part in split3(probs_ref[...])
+        jnp.dot(part, here, preferred_element_type=jnp.float32) for part in split3(probs_ref[...])
     ]
-    out_ref[:own_tokens, :] = cot_ref[...]
-    out_ref[own_tokens:, :] = jnp.zeros((PAD - own_tokens, cot_ref.shape[1]), jnp.bfloat16)
-    out_ref[own_tokens:, : 3 * LANES] = jnp.concatenate(parts, axis=1)
+    meta = jnp.concatenate(parts + [jnp.zeros((SUBLANES - 2 * PARTS, LANES), jnp.float32)], axis=0)
+    out_ref[:, width + PARTS * piece :] = meta.astype(jnp.bfloat16)
 
 
 def fill_kernel(own_tokens, experts, capacity, gathered_ref, ids_ref, out_ref):
     members = gathered_ref.shape[0]
+    width = out_ref.shape[1]
     group = members * own_tokens
-    span = members * PAD
+    rest = own_tokens - SUBLANES
+    piece = width // (PARTS + 1)
+    block = members * SUBLANES
     lane = lax.broadcasted_iota(jnp.int32, (group, LANES), 1)
     token = lax.broadcasted_iota(jnp.int32, (group, LANES), 0)
-    here = lane == token + (PAD - own_tokens) * (token // own_tokens)
     moved = jnp.dot(
         ids_ref[...].astype(jnp.float32).astype(jnp.bfloat16),
-        here.astype(jnp.bfloat16),
+        (lane == token).astype(jnp.bfloat16),
         preferred_element_type=jnp.float32,
     ).astype(jnp.int32)
-    lane_row = lax.broadcasted_iota(jnp.int32, (1, LANES), 1)
-    real = (lane_row < span) & (lane_row % PAD < own_tokens)
+    real = lax.broadcasted_iota(jnp.int32, (1, LANES), 1) < group
     spread = [jnp.where(real, moved[k : k + 1], -1) for k in range(2)]
     expert = lax.broadcasted_iota(jnp.int32, (experts, LANES), 0)
     named = [(spread[k] == expert).astype(jnp.float32) for k in range(2)]
-    earlier_lane = lax.broadcasted_iota(jnp.int32, (LANES, LANES), 0)
-    later_lane = lax.broadcasted_iota(jnp.int32, (LANES, LANES), 1)
-    before = (earlier_lane < later_lane).astype(jnp.bfloat16)
+    first = lax.broadcasted_iota(jnp.int32, (LANES, LANES), 0)
+    second = lax.broadcasted_iota(jnp.int32, (LANES, LANES), 1)
     earlier = jnp.dot(
-        (named[0] + named[1]).astype(jnp.bfloat16), before, preferred_element_type=jnp.float32
-    )
+        (named[0] + named[1]).astype(jnp.bfloat16),
+        (first < second).astype(jnp.bfloat16),
+        preferred_element_type=jnp.float32,
+    )
+    meta = gathered_ref[:, :, width + PARTS * piece :].astype(jnp.float32)
+    meta = jnp.sum(meta, axis=0)
     row = lax.broadcasted_iota(jnp.int32, (experts * capacity, LANES), 0)
     selector = jnp.zeros((experts * capacity, LANES), jnp.float32)
     weight = jnp.zeros((experts * capacity, LANES), jnp.float32)
@@ -64,18 +82,47 @@
         count = earlier if k == 0 else earlier + named[0]
         slot = jnp.sum(count * named[k], axis=0, keepdims=True).astype(jnp.int32)
         key = jnp.where(spread[k] >= 0, spread[k] * capacity + slot, -1)
-        parts = gathered_ref[:, own_tokens + k : own_tokens + k + 1, : 3 * LANES]
-        parts = jnp.sum(parts.astype(jnp.float32), axis=0)
-        prob = parts[:, :LANES] + parts[:, LANES : 2 * LANES] + parts[:, 2 * LANES :]
+        prob = meta[k : k + 1] + meta[2 + k : 3 + k] + meta[4 + k : 5 + k]
         match = row == key
         selector = jnp.where(match, 1.0, selector)
         weight = jnp.where(match, prob, weight)
     scale = jnp.sum(weight, axis=1, keepdims=True)
-    picked = selector[:, :span].astype(jnp.bfloat16)
+    selector = selector.astype(jnp.bfloat16)
+
+    region, within = second // block, second % SUBLANES
+    base = ((second % block) // SUBLANES) * own_tokens
+    head = jnp.where(region == 0, base + within, -1)
+    body = jnp.where((region == 1) & (within < rest), base + SUBLANES + within, head)
+    tail = base + SUBLANES + (within - rest) * PARTS + region - 1
+    tail = jnp.where((region >= 1) & (within >= rest), tail, head)
+
+    def picked(source):
+        moved = jnp.dot(
+            selector, (first == source).astype(jnp.bfloat16), preferred_element_type=jnp.float32
+        )
+        return moved.astype(jnp.bfloat16)
+
+    picked_body, picked_tail = picked(body)[:, : 2 * block], picked(tail)
+
+    def rows_at(start, step):
+        rows = gathered_ref[:, :, start : start + step].astype(jnp.float32)
+        return rows.reshape(block, step)
+
     step = 512
-    for start in range(0, gathered_ref.shape[2], step):
-        block = gathered_ref[:, :, start : start + step].reshape(span, step)
-        rows = jnp.dot(picked, block, preferred_element_type=jnp.float32)
+    for start in range(0, width, step):
+        found = [rows_at(start, step)]
+        if start < PARTS * piece:
+            found.append(rows_at(width + start, step))
+            chosen = picked_body
+        else:
+            for k in range(PARTS):
+                found.append(rows_at(width + k * piece + start - PARTS * piece, step))
+            chosen = picked_tail
+        rows = jnp.dot(
+            chosen,
+            jnp.concatenate(found, axis=0).astype(jnp.bfloat16),
+            preferred_element_type=jnp.float32,
+        )
         out_ref[:, start : start + step] = (rows * scale).astype(jnp.bfloat16)
 
 
@@ -111,43 +158,51 @@
     theirs_ref,
     partial_ref,
     by_feature_ref,
-    both,
-    total,
+    weight_buf,
+    theirs_buf,
+    turned,
     sems,
 ):
     replicas, cols, chunk = weight_theirs_ref.shape
-    stages, _, width = both.shape
-    per_stage = width // chunk
-    copies = []
-    for stage in range(stages):
-        here = [
-            pltpu.make_async_copy(
-                weight_ref.at[:, stage * width : (stage + 1) * width],
-                both.at[stage, :cols],
-                sems.at[stage, 0],
+    width = rows_ref.shape[1]
+    cuts = (0, cols // 32 * 16, cols)
+    weight_copies = [
+        pltpu.make_async_copy(
+            weight_ref.at[start:stop], weight_buf.at[start:stop], sems.at[0, index]
+        )
+        for index, (start, stop) in enumerate(zip(cuts[:-1], cuts[1:]))
+    ]
+    per = replicas // 4
+    theirs_copies = [
+        pltpu.make_async_copy(
+            weight_theirs_ref.at[index * per : (index + 1) * per],
+            theirs_buf.at[index * per : (index + 1) * per],
+            sems.at[1, index],
+        )
+        for index in range(4)
+    ]
+    for copy in theirs_copies + weight_copies:
+        copy.start()
+    for index in range(replicas):
+        rows = rows_ref[:, index * chunk : (index + 1) * chunk]
+        by_feature_ref[index] = rows
+        turned[index * chunk : (index + 1) * chunk, :] = rows.T
+    theirs = jnp.zeros(theirs_ref.shape, jnp.float32)
+    for index in range(4):
+        theirs_copies[index].wait()
+        for replica in range(index * per, (index + 1) * per):
+            theirs += jnp.dot(
+                theirs_buf[replica],
+                turned[replica * chunk : (replica + 1) * chunk, :],
+                preferred_element_type=jnp.float32,
             )
-        ]
-        for part in range(per_stage):
-            here.append(
-                pltpu.make_async_copy(
-                    weight_theirs_ref.at[stage * per_stage + part],
-                    both.at[stage, cols:, part * chunk : (part + 1) * chunk],
-                    sems.at[stage, 1 + part],
-                )
-            )
-        for copy in here:
-            copy.start()
-        copies.append(here)
-    for index in range(replicas):
-        by_feature_ref[index] = rows_ref[:, index * chunk : (index + 1) * chunk]
-    contract = (((1,), (1,)), ((), ()))
-    for stage in range(stages):
-        for copy in copies[stage]:
-            copy.wait()
-        rows = rows_ref[:, stage * width : (stage + 1) * width]
-        added = lax.dot_general(both[stage], rows, contract, preferred_element_type=jnp.float32)
-        total[...] = added if stage == 0 else total[...] + added
-    mine, theirs = total[:cols], total[cols:]
+    mine = []
+    for index, (start, stop) in enumerate(zip(cuts[:-1], cuts[1:])):
+        weight_copies[index].wait()
+        mine.append(
+            jnp.dot(weight_buf[start:stop], turned[...], preferred_element_type=jnp.float32)
+        )
+    mine = jnp.concatenate(mine, axis=0)
     mine_ref[...] = mine.astype(jnp.bfloat16)
     theirs_ref[...] = theirs.astype(jnp.bfloat16)
     summed = jnp.sum(
@@ -244,9 +299,10 @@
         compiler_params=small,
     )(saved_hidden.T)
     hidden_theirs = lax.ppermute(hidden_send, "par", swap)
+    packed_width = model_width + PARTS * model_width // (PARTS + 1) + LANES
     packed = pl.pallas_call(
         pack_kernel,
-        out_shape=jax.ShapeDtypeStruct((PAD, model_width), jnp.bfloat16),
+        out_shape=jax.ShapeDtypeStruct((SUBLANES, packed_width), jnp.bfloat16),
         compiler_params=small,
     )(cotangent, probs.T)
     packed, weight_swapped = lax.optimization_barrier((packed, weight_swapped))
@@ -275,7 +331,6 @@
 
     vmem = pl.BlockSpec(memory_space=pltpu.VMEM)
     hbm = pl.BlockSpec(memory_space=pltpu.HBM)
-    stages = 4
     product, product_theirs, partial_value, by_feature = pl.pallas_call(
         functools.partial(product_kernel, capacity),
         in_specs=[vmem, hbm, hbm, vmem, vmem],
@@ -287,9 +342,10 @@
             jax.ShapeDtypeStruct((n_dp, half, chunk), jnp.bfloat16),
         ],
         scratch_shapes=[
-            pltpu.VMEM((stages, 2 * hidden_cols, model_width // stages), jnp.bfloat16),
-            pltpu.VMEM((2 * hidden_cols, half), jnp.float32),
-            pltpu.SemaphoreType.DMA((stages, 1 + n_dp // stages)),
+            pltpu.VMEM((hidden_cols, model_width), jnp.bfloat16),
+            pltpu.VMEM((n_dp, hidden_cols, chunk), jnp.bfloat16),
+            pltpu.VMEM((model_width, half), jnp.bfloat16),
+            pltpu.SemaphoreType.DMA((2, 4)),
         ],
         compiler_params=pltpu.CompilerParams(vmem_limit_bytes=50 << 20),
     )(rows, weight, weight_theirs, hidden_mine, hidden_theirs)
@@ -302,7 +358,7 @@
         bytes_accessed=2 * n_dp * half * (hidden_cols + chunk) + 4 * hidden_cols * chunk,
         transcendentals=0,
     )
-    medium = pltpu.CompilerParams(vmem_limit_bytes=24 << 20)
+    medium = pltpu.CompilerParams(vmem_limit_bytes=50 << 20)
     sent = pl.pallas_call(
         send_kernel,
         out_shape=jax.ShapeDtypeStruct((hidden_cols, chunk + half), jnp.bfloat16),

time: 199 us -> 199 us (level)
    all_to_all x1, starting transfers between devices: 9.92 us -> 6.59 us  [shards(): lax.all_to_all(buffer, every, split_axis=0, concat_axis=0, axis_index_gro...]
  transfers between devices with their start and end apart: 8 -> 8, of which waited for: 4 -> 4; matrix products, arithmetic and copies ran while one was open for 1% -> 1% of each run, Pallas kernels for 4% -> 5%
where the time goes in v6:
time: 199 us; the launch traced here: 198 us
  blocking collectives  83.6 us (42%)
  waiting for transfers between devices  47.2 us (24%)
  starting transfers between devices  30.3 us (15%)
  between operations  14.2 us (7%)
  Pallas kernels  12.6 us (6%)
  local copies, waits for them, and re-layouts  8.2 us (4%)
    all_gather x1, blocking collectives, shards(): gathered = lax.all_gather(packed, 'tensor', axis=0)  59.6 us
    psum x1, blocking collectives, shards(): partial_value = lax.psum(partial_value, 'tensor')  24 us
    ppermute x1, waiting for transfers between devices, shards(): hidden_theirs = lax.ppermute(hidden_send, 'par', swap)  18.7 us
    all_to_all x1, waiting for transfers between devices, shards(): lax.all_to_all(partial_value, every, split_axis=0, concat_axis=0, axis_in...  11.1 us
    all_to_all x1, waiting for transfers between devices, shards(): lax.all_to_all(buffer, every, split_axis=0, concat_axis=0, axis_index_gro...  9.73 us
    ppermute x1, waiting for transfers between devices, shards(): weight_swapped = lax.ppermute(weight_send, 'par', swap)  7.66 us
    unnamed x25, local copies, waits for them, and re-layouts  6.84 us
    all_to_all x1, starting transfers between devices, shards(): lax.all_to_all(buffer, every, split_axis=0, concat_axis=0, axis_index_gro...  6.59 us
  transfers between devices with their start and end apart: 8, of which 4 were waited for; matrix products, arithmetic and copies ran while one was open for 1% of the time, Pallas kernels for 5%

profile of v6, /device:TPU:6, one launch (start us, length us, event | category | flops | bytes accessed | tf_op | source)
XLA Modules:
  0.0 197.8 jit_solution(369825344186446455)
XLA Ops:
  7.2 0.0 copy-start.9
  7.2 0.0 copy-start.2
  7.2 0.0 all-gather.8.cloned.1.call-start
  7.2 1.1 dynamic-slice_bitcast_fusion
  8.3 3.8 %collective-permute-start.1 = (bf16[400,512]{1,0:T(8,128)(2,1)S(1)}, bf16[400,512]{1,0:T(8,128)(2,1)S(1)}, u32[]{:S(2)}, u32[]{:S(2)}) collective-permute-start(bf16[400,512]{1,0:T(8,128)(2,1)S(1)} %dynamic-slice_bitcast_fusion), channel_id=1, source_target_pairs={{0,4},{4,0},{1,5},{5,1},{2,6},{6,2},{3,7},{7,3},{8,12},{12,8},{9,1... | collective-permute-start | bytes 1228808 | tf_op jit(solution)/shard_map/ppermute | solution.py:295
  12.1 0.0 copy-start.3
  12.2 0.9 copy-done.3
  13.1 0.0 copy-start.6
  13.1 0.7 copy-done.6
  13.7 0.2 shard_map.77
  13.9 7.7 %collective-permute-done.1 = bf16[400,512]{1,0:T(8,128)(2,1)S(1)} collective-permute-done((bf16[400,512]{1,0:T(8,128)(2,1)S(1)}, bf16[400,512]{1,0:T(8,128)(2,1)S(1)}, u32[]{:S(2)}, u32[]{:S(2)}) %collective-permute-start.1) | collective-permute-done | bytes 409632 | tf_op jit(solution)/shard_map/ppermute | solution.py:295
  21.6 0.0 copy-start.10
  21.6 0.7 copy-done.10
  22.3 0.0 all-gather.8.cloned.1.call-update
  22.4 59.6 %all-gather.1 = bf16[32,7296]{1,0:T(8,128)(2,1)S(1)} all-gather(bf16[8,7296]{1,0:T(8,128)(2,1)S(1)} %shard_map.77), channel_id=3, replica_groups=mesh['dp'=8,'y'=4,'zq'=4,'par'=2,'tensor'=4] {'tensor'}, dimensions={0}, use_global_device_ids=true | all-gather | bytes 583680 | tf_op jit(solution)/shard_map/all_gather | solution.py:312
  82.0 0.0 copy-start.8
  82.0 0.7 copy-done.8
  82.7 1.8 shard_map.78
  84.5 0.0 all-gather.8.cloned.1.call-done
  84.5 6.6 %all-to-all-start = ((bf16[16,8,4096]{2,1,0:T(8,128)(2,1)}), bf16[16,8,4096]{2,1,0:T(8,128)(2,1)S(1)}, u32[]{:S(2)}, u32[]{:S(2)}) async-start(bf16[16,8,4096]{2,1,0:T(8,128)(2,1)} %bitcast.9), calls=%async_computation | async-start | bytes 2097152 | tf_op jit(solution)/shard_map/all_to_all | solution.py:322
  91.1 0.0 all-gather.6.cloned.1.call-start
  91.1 0.0 copy-done.2
  91.1 0.2 shard_map.76
  91.3 4.1 %collective-permute-start = (bf16[400,128]{1,0:T(8,128)(2,1)S(1)}, bf16[400,128]{1,0:T(8,128)(2,1)S(1)}, u32[]{:S(2)}, u32[]{:S(2)}) collective-permute-start(bf16[400,128]{1,0:T(8,128)(2,1)S(1)} %get-tuple-element.20), channel_id=1, source_target_pairs={{0,4},{4,0},{1,5},{5,1},{2,6},{6,2},{3,7},{7,3},{8,12},{12,8},{9,1... | collective-permute-start | bytes 307208 | tf_op jit(solution)/shard_map/ppermute | solution.py:301
  95.4 18.7 %collective-permute-done.hidden_theirs_ref = bf16[400,128]{1,0:T(8,128)(2,1)S(1)} collective-permute-done((bf16[400,128]{1,0:T(8,128)(2,1)S(1)}, bf16[400,128]{1,0:T(8,128)(2,1)S(1)}, u32[]{:S(2)}, u32[]{:S(2)}) %collective-permute-start) | collective-permute-done | bytes 102432 | tf_op jit(solution)/shard_map/ppermute | solution.py:301
  114.2 0.7 pad_maximum_fusion
  114.9 0.0 all-gather.6.cloned.1.call-update
  114.9 0.0 copy-done.9
  114.9 0.1 copy.18
  115.0 0.1 reshape.43
  115.1 0.1 fusion
  115.2 0.2 reduce_window_sum.11
  115.4 0.2 select_reduce_fusion.1
  115.6 0.1 dynamic_slice.7
  115.6 9.7 %all-to-all-done = bf16[16,8,4096]{2,1,0:T(8,128)(2,1)S(1)} async-done(((bf16[16,8,4096]{2,1,0:T(8,128)(2,1)}), bf16[16,8,4096]{2,1,0:T(8,128)(2,1)S(1)}, u32[]{:S(2)}, u32[]{:S(2)}) %all-to-all-start) | async-done | bytes 1048608 | tf_op jit(solution)/shard_map/all_to_all | solution.py:322
  125.4 6.3 %shard_map.79 = (bf16[400,128]{1,0:T(8,128)(2,1)S(1)}, bf16[400,128]{1,0:T(8,128)(2,1)S(1)}, f32[16,128]{1,0:T(8,128)S(1)}, bf16[8,128,512]{2,1,0:T(8,128)(2,1)}) custom-call(bf16[128,4096]{1,0:T(8,128)(2,1)S(1)} %bitcast.21, bf16[400,4096]{1,0:T(8,128)(2,1)} %bitcast.28, bf16[8,400,512]{2,1,0:T(8,128)(2,1)} %bitcast.29, ...), custom_call_target="tpu_custom_call" | custom-call | tf_op jit(solution)/shard_map/pallas_call | solution.py:334
  131.7 0.0 copy-start.4
  131.7 0.6 copy-done.4
  132.4 0.0 copy-start.7
  132.4 5.6 %all-to-all-start.1 = ((bf16[8,128,512]{2,1,0:T(8,128)(2,1)}), bf16[8,128,512]{2,1,0:T(8,128)(2,1)S(1)}, u32[]{:S(2)}, u32[]{:S(2)}) async-start(bf16[8,128,512]{2,1,0:T(8,128)(2,1)} %get-tuple-element.27), calls=%async_computation.1 | async-start | bytes 2097152 | tf_op jit(solution)/shard_map/all_to_all | solution.py:353
  138.0 24.0 %psum.7 = f32[16,128]{1,0:T(8,128)} all-reduce(f32[16,128]{1,0:T(8,128)S(1)} %get-tuple-element.26), channel_id=1, replica_groups=mesh['dp'=8,'y'=4,'zq'=4,'par'=2,'tensor'=4] {'tensor'}, use_global_device_ids=true, to_apply=%region_2.3 | all-reduce | flops 2048 | bytes 16384 | tf_op jit(solution)/shard_map/psum | solution.py:354
  162.0 0.0 all-to-all-done.1.rows_ref
  162.0 0.0 all-gather.6.cloned.1.call-done
  162.0 0.0 copy-start
  162.0 1.4 copy-done
  163.4 0.0 copy-start.1
  163.4 1.4 shard_map.81
  164.8 6.2 %collective-permute-start.2 = (bf16[400,640]{1,0:T(8,128)(2,1)}, bf16[400,640]{1,0:T(8,128)(2,1)}, u32[]{:S(2)}, u32[]{:S(2)}) collective-permute-start(bf16[400,640]{1,0:T(8,128)(2,1)} %shard_map.81), channel_id=1, source_target_pairs={{0,4},{4,0},{1,5},{5,1},{2,6},{6,2},{3,7},{7,3},{8,12},{12,8},{9,1... | collective-permute-start | bytes 1536008 | tf_op jit(solution)/shard_map/ppermute | solution.py:368
  171.0 0.1 iota_add_fusion
  171.1 3.9 %all-to-all-start.2 = ((f32[16,1,128]{2,1,0:T(1,128)}), f32[16,1,128]{2,1,0:T(1,128)S(1)}, u32[]{:S(2)}, u32[]{:S(2)}) async-start(f32[16,1,128]{2,1,0:T(1,128)} %bitcast.15), calls=%async_computation.2 | async-start | bytes 16384 | tf_op jit(solution)/shard_map/all_to_all | solution.py:384
  175.0 0.0 copy-done.7
  175.0 0.1 copy.20
  175.1 0.0 copy-done.1
  175.1 0.6 shard_map.80.term_ref
  175.7 11.1 %all-to-all-done.2 = f32[16,1,128]{2,1,0:T(1,128)S(1)} async-done(((f32[16,1,128]{2,1,0:T(1,128)}), f32[16,1,128]{2,1,0:T(1,128)S(1)}, u32[]{:S(2)}, u32[]{:S(2)}) %all-to-all-start.2) | async-done | bytes 8224 | tf_op jit(solution)/shard_map/all_to_all | solution.py:384
  186.8 0.4 select_reduce_fusion
  187.2 0.1 reshape.44
  187.3 0.7 copy.21
  188.0 0.0 collective-permute-done.2.swapped_ref
  188.0 0.0 copy-start.5
  188.0 0.9 copy-done.5
  188.9 2.1 %shard_map.82 = (bf16[400,512]{1,0:T(8,128)(2,1)}, bf16[400,256]{1,0:T(8,128)(2,1)}) custom-call(f32[400,512]{1,0:T(8,128)S(1)} %shard_map.80.term_ref, bf16[400,128]{1,0:T(8,128)(2,1)S(1)} %copy-done.5, bf16[400,640]{1,0:T(8,128)(2,1)} %collective-permute-done.2.swapped_ref), custom_call_target="tpu_custom_call" | custom-call | tf_op jit(solution)/shard_map/pallas_call | solution.py:375
  (4 shorter events, 0.0 us)
Async XLA Ops:
  7.2 107.7 %copy-start.9 = (s32[56,2]{0,1:T(2,128)S(1)}, s32[56,2]{0,1:T(2,128)}, u32[]{:S(2)}) copy-start(s32[56,2]{0,1:T(2,128)} %param.7) | copy-start | bytes 1348
  7.2 83.9 %copy-start.2 = (bf16[256,400]{0,1:T(8,128)(2,1)S(1)}, bf16[256,400]{0,1:T(8,128)(2,1)}, u32[]{:S(2)}) copy-start(bf16[256,400]{0,1:T(8,128)(2,1)} %param.8) | copy-start | bytes 614404
  7.2 77.3 %all-gather.8.cloned.1.call-start = ((), (), s32[]{:S(2)}) async-start(), calls=%async_computation.4 | async-start | bytes 3686400 | tf_op jit(solution)/shard_map/all_gather | solution.py:309
  8.3 13.3 %collective-permute-start.1 = (bf16[400,512]{1,0:T(8,128)(2,1)S(1)}, bf16[400,512]{1,0:T(8,128)(2,1)S(1)}, u32[]{:S(2)}, u32[]{:S(2)}) collective-permute-start(bf16[400,512]{1,0:T(8,128)(2,1)S(1)} %dynamic-slice_bitcast_fusion), channel_id=1, source_target_pairs={{0,4},{4,0},{1,5},{5,1},{2,6},{6,2},{3,7},{7,3},{8,12},{12,8},{9,1... | collective-permute-start | bytes 1228808 | tf_op jit(solution)/shard_map/ppermute | solution.py:295
  12.1 0.9 copy-start.3
  13.1 0.7 copy-start.6
  21.6 0.8 copy-start.10
  82.0 0.7 copy-start.8
  84.5 40.9 %all-to-all-start = ((bf16[16,8,4096]{2,1,0:T(8,128)(2,1)}), bf16[16,8,4096]{2,1,0:T(8,128)(2,1)S(1)}, u32[]{:S(2)}, u32[]{:S(2)}) async-start(bf16[16,8,4096]{2,1,0:T(8,128)(2,1)} %bitcast.9), calls=%async_computation | async-start | bytes 2097152 | tf_op jit(solution)/shard_map/all_to_all | solution.py:322
  91.1 70.9 %all-gather.6.cloned.1.call-start = ((), (), s32[]{:S(2)}) async-start(), calls=%async_computation.3 | async-start | bytes 1843200 | tf_op jit(solution)/shard_map/all_gather | solution.py:310
  91.3 22.8 %collective-permute-start = (bf16[400,128]{1,0:T(8,128)(2,1)S(1)}, bf16[400,128]{1,0:T(8,128)(2,1)S(1)}, u32[]{:S(2)}, u32[]{:S(2)}) collective-permute-start(bf16[400,128]{1,0:T(8,128)(2,1)S(1)} %get-tuple-element.20), channel_id=1, source_target_pairs={{0,4},{4,0},{1,5},{5,1},{2,6},{6,2},{3,7},{7,3},{8,12},{12,8},{9,1... | collective-permute-start | bytes 307208 | tf_op jit(solution)/shard_map/ppermute | solution.py:301
  131.7 0.6 copy-start.4
  132.4 42.6 %copy-start.7 = (f32[14,2]{0,1:T(2,128)S(1)}, f32[14,2]{0,1:T(2,128)}, u32[]{:S(2)}) copy-start(f32[14,2]{0,1:T(2,128)} %param.6) | copy-start | bytes 340
  132.4 29.6 %all-to-all-start.1 = ((bf16[8,128,512]{2,1,0:T(8,128)(2,1)}), bf16[8,128,512]{2,1,0:T(8,128)(2,1)S(1)}, u32[]{:S(2)}, u32[]{:S(2)}) async-start(bf16[8,128,512]{2,1,0:T(8,128)(2,1)} %get-tuple-element.27), calls=%async_computation.1 | async-start | bytes 2097152 | tf_op jit(solution)/shard_map/all_to_all | solution.py:353
  162.0 1.4 copy-start
  163.4 11.7 %copy-start.1 = (bf16[16,400,128]{2,1,0:T(8,128)(2,1)S(1)}, bf16[16,400,128]{2,1,0:T(8,128)(2,1)}, u32[]{:S(2)}) copy-start(bf16[16,400,128]{2,1,0:T(8,128)(2,1)} %all-gather.6.cloned.1.call-done) | copy-start | bytes 4915204
  164.8 23.2 %collective-permute-start.2 = (bf16[400,640]{1,0:T(8,128)(2,1)}, bf16[400,640]{1,0:T(8,128)(2,1)}, u32[]{:S(2)}, u32[]{:S(2)}) collective-permute-start(bf16[400,640]{1,0:T(8,128)(2,1)} %shard_map.81), channel_id=1, source_target_pairs={{0,4},{4,0},{1,5},{5,1},{2,6},{6,2},{3,7},{7,3},{8,12},{12,8},{9,1... | collective-permute-start | bytes 1536008 | tf_op jit(solution)/shard_map/ppermute | solution.py:368
  171.1 15.7 %all-to-all-start.2 = ((f32[16,1,128]{2,1,0:T(1,128)}), f32[16,1,128]{2,1,0:T(1,128)S(1)}, u32[]{:S(2)}, u32[]{:S(2)}) async-start(f32[16,1,128]{2,1,0:T(1,128)} %bitcast.15), calls=%async_computation.2 | async-start | bytes 16384 | tf_op jit(solution)/shard_map/all_to_all | solution.py:384
  188.0 0.9 copy-start.5
Sparse Core Ops, SparseCore 0:
  22.5 52.4 all-gather.7
  115.0 44.4 all-gather.5

commit v7 on v6

--- a/solution.py
+++ b/solution.py
@@ -138,13 +138,20 @@
     return (natural == source).astype(jnp.bfloat16)
 
 
-def sort_kernel(capacity, hidden_ref, mine_ref, send_ref):
+def prepare_kernel(capacity, weight_ref, hidden_ref, send_ref, mine_ref, sem):
     rows = hidden_ref.shape[1]
+    chunk = send_ref.shape[1] - rows // 2
+    start = pl.multiple_of(lax.axis_index("dp") * chunk, chunk)
+    copy = pltpu.make_async_copy(
+        weight_ref.at[:, pl.ds(start, chunk)], send_ref.at[:, :chunk], sem
+    )
+    copy.start()
     order = parity_order(rows, capacity, True)
     moved = jnp.dot(hidden_ref[...], order, preferred_element_type=jnp.float32)
     moved = moved.astype(jnp.bfloat16)
     mine_ref[...] = moved[:, : rows // 2]
-    send_ref[...] = moved[:, rows // 2 :]
+    send_ref[:, chunk:] = moved[:, rows // 2 :]
+    copy.wait()
 
 
 def product_kernel(
@@ -163,8 +170,7 @@
     turned,
     sems,
 ):
-    replicas, cols, chunk = weight_theirs_ref.shape
-    width = rows_ref.shape[1]
+    replicas, cols, chunk = theirs_buf.shape
     cuts = (0, cols // 32 * 16, cols)
     weight_copies = [
         pltpu.make_async_copy(
@@ -175,7 +181,7 @@
     per = replicas // 4
     theirs_copies = [
         pltpu.make_async_copy(
-            weight_theirs_ref.at[index * per : (index + 1) * per],
+            weight_theirs_ref.at[index * per : (index + 1) * per, :, :chunk],
             theirs_buf.at[index * per : (index + 1) * per],
             sems.at[1, index],
         )
@@ -229,18 +235,19 @@
 def term_of(hidden_ref, rows_ref, half):
     replicas, depth, chunk = rows_ref.shape
     rows = rows_ref[...].reshape(replicas * depth, chunk)
-    hidden = jnp.concatenate([hidden_ref[p, half] for p in range(replicas)], axis=1)
+    lanes = slice(half * depth, (half + 1) * depth)
+    hidden = jnp.concatenate([hidden_ref[p, :, lanes] for p in range(replicas)], axis=1)
     return jnp.dot(hidden, rows, preferred_element_type=jnp.float32)
 
 
 def send_kernel(hidden_ref, rows_ref, product_ref, out_ref):
     chunk = rows_ref.shape[2]
-    out_ref[:, :chunk] = term_of(hidden_ref, rows_ref, 1).astype(jnp.bfloat16)
+    out_ref[:, :chunk] = term_of(hidden_ref, rows_ref, 0).astype(jnp.bfloat16)
     out_ref[:, chunk:] = product_ref[...]
 
 
 def keep_kernel(hidden_ref, rows_ref, out_ref):
-    out_ref[...] = term_of(hidden_ref, rows_ref, 0)
+    out_ref[...] = term_of(hidden_ref, rows_ref, 1)
 
 
 def finish_kernel(capacity, term_ref, product_ref, swapped_ref, weight_ref, hidden_ref):
@@ -288,26 +295,36 @@
     chunk = model_width // n_dp
     half = experts * capacity
     swap = [(0, 1), (1, 0)]
+    large = pltpu.CompilerParams(vmem_limit_bytes=50 << 20)
     small = pltpu.CompilerParams(vmem_limit_bytes=16 << 20)
 
     weight = down_weight.T
-    weight_send = lax.dynamic_slice_in_dim(weight, lax.axis_index("dp") * chunk, chunk, axis=1)
-    weight_swapped = lax.ppermute(weight_send, "par", swap)
-    hidden_mine, hidden_send = pl.pallas_call(
-        functools.partial(sort_kernel, capacity),
-        out_shape=[jax.ShapeDtypeStruct((hidden_cols, half), jnp.bfloat16)] * 2,
-        compiler_params=small,
-    )(saved_hidden.T)
-    hidden_theirs = lax.ppermute(hidden_send, "par", swap)
+    vmem = pl.BlockSpec(memory_space=pltpu.VMEM)
+    hbm = pl.BlockSpec(memory_space=pltpu.HBM)
+    sent, hidden_mine = pl.pallas_call(
+        functools.partial(prepare_kernel, capacity),
+        in_specs=[hbm, vmem],
+        out_specs=[vmem, vmem],
+        out_shape=[
+            jax.ShapeDtypeStruct((hidden_cols, chunk + half), jnp.bfloat16),
+            jax.ShapeDtypeStruct((hidden_cols, half), jnp.bfloat16),
+        ],
+        scratch_shapes=[pltpu.SemaphoreType.DMA],
+        compiler_params=large,
+    )(weight, saved_hidden.T)
+    swapped = lax.ppermute(sent, "par", swap)
     packed_width = model_width + PARTS * model_width // (PARTS + 1) + LANES
     packed = pl.pallas_call(
         pack_kernel,
         out_shape=jax.ShapeDtypeStruct((SUBLANES, packed_width), jnp.bfloat16),
         compiler_params=small,
     )(cotangent, probs.T)
-    packed, weight_swapped = lax.optimization_barrier((packed, weight_swapped))
-    weight_theirs = lax.all_gather(weight_swapped, "dp", axis=0)
-    hidden_all = lax.all_gather(jnp.stack([hidden_mine, hidden_theirs]), "dp", axis=0)
+    flat_ids = expert_ids.reshape(-1)
+    keys = flat_ids * capacity + assign_slots(flat_ids, experts)
+    start_row = lax.axis_index("tensor") * (own_tokens * 2)
+    own_keys = lax.dynamic_slice_in_dim(keys, start_row, own_tokens * 2)
+    packed, swapped, own_keys = lax.optimization_barrier((packed, swapped, own_keys))
+    prefetched = lax.all_gather(jnp.concatenate([swapped, hidden_mine], axis=1), "dp", axis=0)
 
     gathered = lax.all_gather(packed, "tensor", axis=0)
     buffer = pl.pallas_call(
@@ -315,7 +332,6 @@
         out_shape=jax.ShapeDtypeStruct((half, model_width), jnp.bfloat16),
         compiler_params=pltpu.CompilerParams(vmem_limit_bytes=24 << 20),
     )(gathered, expert_ids.T)
-    buffer, weight_theirs = lax.optimization_barrier((buffer, weight_theirs))
     buffer = buffer.reshape(experts, capacity, model_width)
     groups = windows(n_dp, n_y, n_q, n_par, members)
     every = ("dp", "y", "zq", "par", "tensor")
@@ -323,17 +339,16 @@
         buffer, every, split_axis=0, concat_axis=0, axis_index_groups=groups, tiled=True
     ).reshape(half, model_width)
 
-    flat_ids = expert_ids.reshape(-1)
-    keys = flat_ids * capacity + assign_slots(flat_ids, experts)
-    start_row = lax.axis_index("tensor") * (own_tokens * 2)
-    own_keys = lax.dynamic_slice_in_dim(keys, start_row, own_tokens * 2)
-    rows, own_keys = lax.optimization_barrier((rows, own_keys))
-
-    vmem = pl.BlockSpec(memory_space=pltpu.VMEM)
-    hbm = pl.BlockSpec(memory_space=pltpu.HBM)
     product, product_theirs, partial_value, by_feature = pl.pallas_call(
         functools.partial(product_kernel, capacity),
-        in_specs=[vmem, hbm, hbm, vmem, vmem],
+        grid=(1,),
+        in_specs=[
+            vmem,
+            hbm,
+            hbm,
+            vmem,
+            pl.BlockSpec((hidden_cols, half), lambda i: (0, chunk // half)),
+        ],
         out_specs=[vmem] * 4,
         out_shape=[
             jax.ShapeDtypeStruct((hidden_cols, half), jnp.bfloat16),
@@ -348,7 +363,7 @@
             pltpu.SemaphoreType.DMA((2, 4)),
         ],
         compiler_params=pltpu.CompilerParams(vmem_limit_bytes=50 << 20),
-    )(rows, weight, weight_theirs, hidden_mine, hidden_theirs)
+    )(rows, weight, prefetched, hidden_mine, swapped)
 
     replica_rows = lax.all_to_all(by_feature, "dp", split_axis=0, concat_axis=0, tiled=True)
     partial_value = lax.psum(partial_value, "tensor")
@@ -359,19 +374,24 @@
         transcendentals=0,
     )
     medium = pltpu.CompilerParams(vmem_limit_bytes=50 << 20)
+    saved = pl.BlockSpec((n_dp, hidden_cols, 2 * half), lambda i: (0, 0, chunk // (2 * half)))
     sent = pl.pallas_call(
         send_kernel,
+        grid=(1,),
+        in_specs=[saved, vmem, vmem],
         out_shape=jax.ShapeDtypeStruct((hidden_cols, chunk + half), jnp.bfloat16),
         cost_estimate=term_cost,
         compiler_params=medium,
-    )(hidden_all, replica_rows, product_theirs)
+    )(prefetched, replica_rows, product_theirs)
     swapped = lax.ppermute(sent, "par", swap)
     term = pl.pallas_call(
         keep_kernel,
+        grid=(1,),
+        in_specs=[saved, vmem],
         out_shape=jax.ShapeDtypeStruct((hidden_cols, chunk), jnp.float32),
         cost_estimate=term_cost,
         compiler_params=medium,
-    )(hidden_all, replica_rows)
+    )(prefetched, replica_rows)
     weight_grad, hidden_grad = pl.pallas_call(
         functools.partial(finish_kernel, capacity),
         out_shape=[

time: 199 us -> 194 us (0.975)
  blocking collectives: 83.6 us -> 119 us
  waiting for transfers between devices: 47.2 us -> 20.3 us
  starting transfers between devices: 30.3 us -> 21.4 us
  local copies, waits for them, and re-layouts: 8.2 us -> 4 us
    all_to_all x0 -> x1, blocking collectives: none -> 39.3 us  [shards(): lax.all_to_all(buffer, every, split_axis=0, concat_axis=0, axis_index_gro...]
    ppermute x2 -> x0, waiting for transfers between devices: 26.4 us -> none  [the longest x1 18.7 us: shards(): hidden_theirs = lax.ppermute(hidden_send, 'par', swap)]
    ppermute x1 -> x2, waiting for transfers between devices: 0.01 us -> 10.7 us  [shards(): swapped = lax.ppermute(sent, 'par', swap)]
    all_to_all x1 -> x0, waiting for transfers between devices: 9.73 us -> none  [shards(): lax.all_to_all(buffer, every, split_axis=0, concat_axis=0, axis_index_gro...]
    ppermute x2 -> x0, starting transfers between devices: 7.92 us -> none  [the longest x1 4.09 us: shards(): hidden_theirs = lax.ppermute(hidden_send, 'par', swap)]
    all_to_all x1 -> x0, starting transfers between devices: 6.59 us -> none  [shards(): lax.all_to_all(buffer, every, split_axis=0, concat_axis=0, axis_index_gro...]
    ppermute x1 -> x2, starting transfers between devices: 6.19 us -> 10.7 us  [shards(): swapped = lax.ppermute(sent, 'par', swap)]
    psum x1, blocking collectives: 24 us -> 20.4 us  [shards(): partial_value = lax.psum(partial_value, 'tensor')]
  transfers between devices with their start and end apart: 8 -> 5, of which waited for: 4 -> 2; matrix products, arithmetic and copies ran while one was open for 1% -> 1% of each run, Pallas kernels for 5% -> 2%
where the time goes in v7:
time: 194 us
  blocking collectives  119 us (61%)
  starting transfers between devices  21.4 us (11%)
  waiting for transfers between devices  20.3 us (10%)
  between operations  14.2 us (7%)
  Pallas kernels  12.7 us (7%)
  local copies, waits for them, and re-layouts  4 us (2%)
    all_gather x1, blocking collectives, shards(): gathered = lax.all_gather(packed, 'tensor', axis=0)  59.6 us
    all_to_all x1, blocking collectives, shards(): lax.all_to_all(buffer, every, split_axis=0, concat_axis=0, axis_index_gro...  39.3 us
    psum x1, blocking collectives, shards(): partial_value = lax.psum(partial_value, 'tensor')  20.4 us
    ppermute x2, starting transfers between devices, shards(): swapped = lax.ppermute(sent, 'par', swap)  10.7 us
    ppermute x2, waiting for transfers between devices, shards(): swapped = lax.ppermute(sent, 'par', swap)  10.7 us
    all_to_all x1, waiting for transfers between devices, shards(): lax.all_to_all(partial_value, every, split_axis=0, concat_axis=0, axis_in...  9.58 us
    all_to_all x1, starting transfers between devices, shards(): lax.all_to_all(by_feature, 'dp', split_axis=0, concat_axis=0, tiled=True)  6.81 us
    pallas_call x1, Pallas kernels, shards(): pl.pallas_call(functools.partial(product_kernel, capacity), grid=(1,), in...  6.32 us
  transfers between devices with their start and end apart: 5, of which 2 were waited for; matrix products, arithmetic and copies ran while one was open for 1% of the time, Pallas kernels for 2%

profile of v7, /device:TPU:6, one launch (start us, length us, event | category | flops | bytes accessed | tf_op | source)
XLA Modules:
  0.0 193.7 jit_solution(5071606018315462461)
XLA Ops:
  7.2 0.0 all-gather.4.cloned.1.call-start
  7.2 0.0 copy-start
  7.2 1.9 copy-done
  9.1 0.0 copy-start.1
  9.1 0.9 copy-done.1
  10.1 0.0 copy-start.4
  10.1 0.0 copy-start.2
  10.1 0.0 copy-start.3
  10.1 0.3 shard_map.77
  10.3 3.8 %collective-permute-start = (bf16[400,640]{1,0:T(8,128)(2,1)S(1)}, bf16[400,640]{1,0:T(8,128)(2,1)S(1)}, u32[]{:S(2)}, u32[]{:S(2)}) collective-permute-start(bf16[400,640]{1,0:T(8,128)(2,1)S(1)} %get-tuple-element.16), channel_id=1, source_target_pairs={{0,4},{4,0},{1,5},{5,1},{2,6},{6,2},{3,7},{7,3},{8,12},{12,8},{9,1... | collective-permute-start | bytes 1536008 | tf_op jit(solution)/shard_map/ppermute | solution.py:315
  14.2 0.0 copy-done.4
  14.2 0.1 copy.18
  14.3 0.1 reshape.41
  14.4 0.1 fusion
  14.5 0.2 reduce_window_sum.11
  14.7 0.2 select_reduce_fusion.1
  14.9 0.1 dynamic_slice.3
  14.9 0.0 copy-done.2
  15.0 0.0 copy-done.3
  15.0 0.2 shard_map.76
  15.2 10.7 %collective-permute-done.hidden_theirs_ref = bf16[400,640]{1,0:T(8,128)(2,1)S(1)} collective-permute-done((bf16[400,640]{1,0:T(8,128)(2,1)S(1)}, bf16[400,640]{1,0:T(8,128)(2,1)S(1)}, u32[]{:S(2)}, u32[]{:S(2)}) %collective-permute-start) | collective-permute-done | bytes 512032 | tf_op jit(solution)/shard_map/ppermute | solution.py:315
  25.8 0.9 pad_maximum_fusion
  26.7 0.0 all-gather.4.cloned.1.call-update
  26.7 59.6 %all-gather.1 = bf16[32,7296]{1,0:T(8,128)(2,1)S(1)} all-gather(bf16[8,7296]{1,0:T(8,128)(2,1)S(1)} %shard_map.76), channel_id=3, replica_groups=mesh['dp'=8,'y'=4,'zq'=4,'par'=2,'tensor'=4] {'tensor'}, dimensions={0}, use_global_device_ids=true | all-gather | bytes 583680 | tf_op jit(solution)/shard_map/all_gather | solution.py:329
  86.4 0.8 shard_map.78
  87.2 39.3 %all_to_all.19 = bf16[16,8,4096]{2,1,0:T(8,128)(2,1)S(1)} all-to-all(bf16[16,8,4096]{2,1,0:T(8,128)(2,1)S(1)} %bitcast.16), channel_id=1, replica_groups={{0,8,16,24,32,40,48,56,64,72,80,88,96,104,112,120},{1,9,17,25,33,41,49,..., dimensions={0} | all-to-all | bytes 2097152 | tf_op jit(solution)/shard_map/all_to_all | solution.py:338
  126.4 0.0 all-gather.4.cloned.1.call-done
  126.4 6.3 %shard_map.79 = (bf16[400,128]{1,0:T(8,128)(2,1)S(1)}, bf16[400,128]{1,0:T(8,128)(2,1)S(1)}, f32[16,128]{1,0:T(8,128)S(1)}, bf16[8,128,512]{2,1,0:T(8,128)(2,1)}) custom-call(bf16[128,4096]{1,0:T(8,128)(2,1)S(1)} %bitcast.17, bf16[400,4096]{1,0:T(8,128)(2,1)} %bitcast.14, bf16[8,400,768]{2,1,0:T(8,128)(2,1)} %bitcast.22, ...), custom_call_target="tpu_custom_call" | custom-call | tf_op jit(solution)/shard_map/pallas_call | solution.py:342
  132.8 6.8 %all-to-all-start.1 = ((bf16[8,128,512]{2,1,0:T(8,128)(2,1)}), bf16[8,128,512]{2,1,0:T(8,128)(2,1)S(1)}, u32[]{:S(2)}, u32[]{:S(2)}) async-start(bf16[8,128,512]{2,1,0:T(8,128)(2,1)} %get-tuple-element.21), calls=%async_computation.1 | async-start | bytes 2097152 | tf_op jit(solution)/shard_map/all_to_all | solution.py:368
  139.6 20.4 %psum.7 = f32[16,128]{1,0:T(8,128)} all-reduce(f32[16,128]{1,0:T(8,128)S(1)} %get-tuple-element.20), channel_id=1, replica_groups=mesh['dp'=8,'y'=4,'zq'=4,'par'=2,'tensor'=4] {'tensor'}, use_global_device_ids=true, to_apply=%region_2.3 | all-reduce | flops 2048 | bytes 16384 | tf_op jit(solution)/shard_map/psum | solution.py:369
  160.0 0.0 all-to-all-done.1.rows_ref
  160.0 2.0 %shard_map.81 = bf16[400,640]{1,0:T(8,128)(2,1)S(1)} custom-call(bf16[8,400,768]{2,1,0:T(8,128)(2,1)} %bitcast.23, bf16[8,128,512]{2,1,0:T(8,128)(2,1)S(1)} %all-to-all-done.1.rows_ref, bf16[400,128]{1,0:T(8,128)(2,1)S(1)} %get-tuple-element.24.product_ref), custom_call_target="tpu_custom_call" | custom-call | flops 419430400 | bytes 2686976 | tf_op jit(solution)/shard_map/pallas_call | solution.py:378
  162.1 6.9 %collective-permute-start.1 = (bf16[400,640]{1,0:T(8,128)(2,1)S(1)}, bf16[400,640]{1,0:T(8,128)(2,1)S(1)}, u32[]{:S(2)}, u32[]{:S(2)}) collective-permute-start(bf16[400,640]{1,0:T(8,128)(2,1)S(1)} %shard_map.81), channel_id=1, source_target_pairs={{0,4},{4,0},{1,5},{5,1},{2,6},{6,2},{3,7},{7,3},{8,12},{12,8},{9,1... | collective-permute-start | bytes 1536008 | tf_op jit(solution)/shard_map/ppermute | solution.py:386
  169.0 0.1 iota_add_fusion
  169.1 3.8 %all-to-all-start.2 = ((f32[16,1,128]{2,1,0:T(1,128)}), f32[16,1,128]{2,1,0:T(1,128)S(1)}, u32[]{:S(2)}, u32[]{:S(2)}) async-start(f32[16,1,128]{2,1,0:T(1,128)} %bitcast.11), calls=%async_computation.2 | async-start | bytes 16384 | tf_op jit(solution)/shard_map/all_to_all | solution.py:404
  172.9 0.1 copy.20
  172.9 2.0 %shard_map.80.term_ref = f32[400,512]{1,0:T(8,128)S(1)} custom-call(bf16[8,400,768]{2,1,0:T(8,128)(2,1)} %bitcast.24, bf16[8,128,512]{2,1,0:T(8,128)(2,1)S(1)} %all-to-all-done.1.rows_ref), custom_call_target="tpu_custom_call" | custom-call | flops 419430400 | bytes 2686976 | tf_op jit(solution)/shard_map/pallas_call | solution.py:387
  175.0 9.6 %all-to-all-done.2 = f32[16,1,128]{2,1,0:T(1,128)S(1)} async-done(((f32[16,1,128]{2,1,0:T(1,128)}), f32[16,1,128]{2,1,0:T(1,128)S(1)}, u32[]{:S(2)}, u32[]{:S(2)}) %all-to-all-start.2) | async-done | bytes 8224 | tf_op jit(solution)/shard_map/all_to_all | solution.py:404
  184.6 0.4 select_reduce_fusion
  185.0 0.1 reshape.44
  185.1 0.7 copy.21
  185.8 0.0 collective-permute-done.1.swapped_ref
  185.8 1.1 shard_map.82
  (4 shorter events, 0.0 us)
Async XLA Ops:
  7.2 119.3 %all-gather.4.cloned.1.call-start = ((), (), s32[]{:S(2)}) async-start(), calls=%async_computation.3 | async-start | bytes 5529600 | tf_op jit(solution)/shard_map/all_gather | solution.py:327
  7.2 1.9 copy-start
  9.1 0.9 copy-start.1
  10.1 4.1 %copy-start.4 = (s32[56,2]{0,1:T(2,128)S(1)}, s32[56,2]{0,1:T(2,128)}, u32[]{:S(2)}) copy-start(s32[56,2]{0,1:T(2,128)} %param.7) | copy-start | bytes 1348
  10.1 4.9 %copy-start.2 = (bf16[14,4096]{1,0:T(8,128)(2,1)S(1)}, bf16[14,4096]{1,0:T(8,128)(2,1)}, u32[]{:S(2)}) copy-start(bf16[14,4096]{1,0:T(8,128)(2,1)} %cot_ref.1) | copy-start | bytes 344068
  10.1 4.9 %copy-start.3 = (f32[14,2]{0,1:T(2,128)S(1)}, f32[14,2]{0,1:T(2,128)}, u32[]{:S(2)}) copy-start(f32[14,2]{0,1:T(2,128)} %param.6) | copy-start | bytes 340
  10.3 15.5 %collective-permute-start = (bf16[400,640]{1,0:T(8,128)(2,1)S(1)}, bf16[400,640]{1,0:T(8,128)(2,1)S(1)}, u32[]{:S(2)}, u32[]{:S(2)}) collective-permute-start(bf16[400,640]{1,0:T(8,128)(2,1)S(1)} %get-tuple-element.16), channel_id=1, source_target_pairs={{0,4},{4,0},{1,5},{5,1},{2,6},{6,2},{3,7},{7,3},{8,12},{12,8},{9,1... | collective-permute-start | bytes 1536008 | tf_op jit(solution)/shard_map/ppermute | solution.py:315
  132.8 27.3 %all-to-all-start.1 = ((bf16[8,128,512]{2,1,0:T(8,128)(2,1)}), bf16[8,128,512]{2,1,0:T(8,128)(2,1)S(1)}, u32[]{:S(2)}, u32[]{:S(2)}) async-start(bf16[8,128,512]{2,1,0:T(8,128)(2,1)} %get-tuple-element.21), calls=%async_computation.1 | async-start | bytes 2097152 | tf_op jit(solution)/shard_map/all_to_all | solution.py:368
  162.1 23.7 %collective-permute-start.1 = (bf16[400,640]{1,0:T(8,128)(2,1)S(1)}, bf16[400,640]{1,0:T(8,128)(2,1)S(1)}, u32[]{:S(2)}, u32[]{:S(2)}) collective-permute-start(bf16[400,640]{1,0:T(8,128)(2,1)S(1)} %shard_map.81), channel_id=1, source_target_pairs={{0,4},{4,0},{1,5},{5,1},{2,6},{6,2},{3,7},{7,3},{8,12},{12,8},{9,1... | collective-permute-start | bytes 1536008 | tf_op jit(solution)/shard_map/ppermute | solution.py:386
  169.1 15.5 %all-to-all-start.2 = ((f32[16,1,128]{2,1,0:T(1,128)}), f32[16,1,128]{2,1,0:T(1,128)S(1)}, u32[]{:S(2)}, u32[]{:S(2)}) async-start(f32[16,1,128]{2,1,0:T(1,128)} %bitcast.11), calls=%async_computation.2 | async-start | bytes 16384 | tf_op jit(solution)/shard_map/all_to_all | solution.py:404
Sparse Core Ops, SparseCore 0:
  26.8 58.4 all-gather.3

commit v8 on v7

--- a/solution.py
+++ b/solution.py
@@ -295,7 +295,7 @@
     chunk = model_width // n_dp
     half = experts * capacity
     swap = [(0, 1), (1, 0)]
-    large = pltpu.CompilerParams(vmem_limit_bytes=50 << 20)
+    large = pltpu.CompilerParams(vmem_limit_bytes=60 << 20)
     small = pltpu.CompilerParams(vmem_limit_bytes=16 << 20)
 
     weight = down_weight.T
@@ -400,6 +400,9 @@
         ],
         compiler_params=medium,
     )(term, product, swapped)
+    weight_grad, hidden_grad, own_keys = lax.optimization_barrier(
+        (weight_grad, hidden_grad, own_keys)
+    )
     weight_grad, hidden_grad = weight_grad.T, hidden_grad.T
     lookup = lax.all_to_all(
         partial_value, every, split_axis=0, concat_axis=0, axis_index_groups=groups, tiled=True

time: 194 us -> 194 us (level)
  starting transfers between devices: 21.4 us -> 18.3 us
  blocking collectives: 119 us -> 122 us
  local copies, waits for them, and re-layouts: 4 us -> 1.16 us
  Pallas kernels: 12.7 us -> 15.2 us
    all_to_all x1, waiting for transfers between devices: 9.58 us -> 5.95 us  [shards(): lax.all_to_all(partial_value, every, split_axis=0, concat_axis=0, axis_in...]
    psum x1, blocking collectives: 20.4 us -> 23.3 us  [shards(): partial_value = lax.psum(partial_value, 'tensor')]
    unnamed x13 -> x11, local copies, waits for them, and re-layouts: 3.71 us -> 0.87 us
    ppermute x2, waiting for transfers between devices: 10.7 us -> 13.5 us  [shards(): swapped = lax.ppermute(sent, 'par', swap)]
    ppermute x2, starting transfers between devices: 10.7 us -> 8.2 us  [shards(): swapped = lax.ppermute(sent, 'par', swap)]
    pallas_call x1, Pallas kernels: 0.26 us -> 2.8 us  [shards(): pl.pallas_call(functools.partial(prepare_kernel, capacity), in_specs=[hbm...]
    all_to_all x1, starting transfers between devices: 6.81 us -> 4.79 us  [shards(): lax.all_to_all(by_feature, 'dp', split_axis=0, concat_axis=0, tiled=True)]
  transfers between devices with their start and end apart: 5 -> 5, of which waited for: 2 -> 3; matrix products, arithmetic and copies ran while one was open for 1% -> 0% of each run, Pallas kernels for 2% -> 2%
where the time goes in v8:
time: 194 us; the launch traced here: 193 us
  blocking collectives  122 us (63%)
  waiting for transfers between devices  19.5 us (10%)
  starting transfers between devices  18.3 us (9%)
  Pallas kernels  15.2 us (8%)
  between operations  14.2 us (7%)
  other arithmetic  2.73 us (1%)
    all_gather x1, blocking collectives, shards(): gathered = lax.all_gather(packed, 'tensor', axis=0)  59.6 us
    all_to_all x1, blocking collectives, shards(): lax.all_to_all(buffer, every, split_axis=0, concat_axis=0, axis_index_gro...  39.4 us
    psum x1, blocking collectives, shards(): partial_value = lax.psum(partial_value, 'tensor')  23.3 us
    ppermute x2, waiting for transfers between devices, shards(): swapped = lax.ppermute(sent, 'par', swap)  13.5 us
    ppermute x2, starting transfers between devices, shards(): swapped = lax.ppermute(sent, 'par', swap)  8.2 us
    pallas_call x1, Pallas kernels, shards(): pl.pallas_call(functools.partial(product_kernel, capacity), grid=(1,), in...  6.32 us
    all_to_all x1, waiting for transfers between devices, shards(): lax.all_to_all(partial_value, every, split_axis=0, concat_axis=0, axis_in...  5.95 us
    all_to_all x1, starting transfers between devices, shards(): lax.all_to_all(partial_value, every, split_axis=0, concat_axis=0, axis_in...  5.27 us
  transfers between devices with their start and end apart: 5, of which 3 were waited for; matrix products, arithmetic and copies ran while one was open for 0% of the time, Pallas kernels for 2%

profile of v8, /device:TPU:6, one launch (start us, length us, event | category | flops | bytes accessed | tf_op | source)
XLA Modules:
  0.0 193.4 jit_solution(18320522650188028820)
XLA Ops:
  7.2 0.0 all-gather.4.cloned.1.call-start
  7.2 0.0 copy-start.3
  7.2 0.0 copy-start.1
  7.2 0.0 copy-start.2
  7.2 2.8 %shard_map.77 = (bf16[400,640]{1,0:T(8,128)(2,1)}, bf16[400,128]{1,0:T(8,128)(2,1)}) custom-call(bf16[400,4096]{1,0:T(8,128)(2,1)} %bitcast.22, bf16[400,256]{1,0:T(8,128)(2,1)} %bitcast.24), custom_call_target="tpu_custom_call" | custom-call | tf_op jit(solution)/shard_map/pallas_call | solution.py:304
  10.0 3.8 %collective-permute-start = (bf16[400,640]{1,0:T(8,128)(2,1)}, bf16[400,640]{1,0:T(8,128)(2,1)S(1)}, u32[]{:S(2)}, u32[]{:S(2)}) collective-permute-start(bf16[400,640]{1,0:T(8,128)(2,1)} %get-tuple-element.19), channel_id=1, source_target_pairs={{0,4},{4,0},{1,5},{5,1},{2,6},{6,2},{3,7},{7,3},{8,12},{12,8},{9,1... | collective-permute-start | bytes 1536008 | tf_op jit(solution)/shard_map/ppermute | solution.py:315
  13.9 0.0 copy-done.3
  13.9 0.1 copy.18
  14.0 0.1 reshape.41
  14.1 0.1 fusion
  14.2 0.2 reduce_window_sum.11
  14.4 0.2 select_reduce_fusion.1
  14.6 0.1 dynamic_slice.3
  14.6 0.0 copy-done.1
  14.6 0.0 copy-done.2
  14.6 0.2 shard_map.76
  14.8 10.9 %collective-permute-done.hidden_theirs_ref = bf16[400,640]{1,0:T(8,128)(2,1)S(1)} collective-permute-done((bf16[400,640]{1,0:T(8,128)(2,1)}, bf16[400,640]{1,0:T(8,128)(2,1)S(1)}, u32[]{:S(2)}, u32[]{:S(2)}) %collective-permute-start) | collective-permute-done | bytes 512032 | tf_op jit(solution)/shard_map/ppermute | solution.py:315
  25.7 1.8 pad_maximum_fusion
  27.5 0.0 all-gather.4.cloned.1.call-update
  27.5 59.6 %all-gather.1 = bf16[32,7296]{1,0:T(8,128)(2,1)S(1)} all-gather(bf16[8,7296]{1,0:T(8,128)(2,1)S(1)} %shard_map.76), channel_id=3, replica_groups=mesh['dp'=8,'y'=4,'zq'=4,'par'=2,'tensor'=4] {'tensor'}, dimensions={0}, use_global_device_ids=true | all-gather | bytes 583680 | tf_op jit(solution)/shard_map/all_gather | solution.py:329
  87.1 0.8 shard_map.78
  87.9 0.0 copy-start
  88.0 39.4 %all_to_all.19 = bf16[16,8,4096]{2,1,0:T(8,128)(2,1)S(1)} all-to-all(bf16[16,8,4096]{2,1,0:T(8,128)(2,1)S(1)} %bitcast.14), channel_id=1, replica_groups={{0,8,16,24,32,40,48,56,64,72,80,88,96,104,112,120},{1,9,17,25,33,41,49,..., dimensions={0} | all-to-all | bytes 2097152 | tf_op jit(solution)/shard_map/all_to_all | solution.py:338
  127.3 0.0 all-gather.4.cloned.1.call-done
  127.3 0.0 copy-done
  127.3 6.3 %shard_map.79 = (bf16[400,128]{1,0:T(8,128)(2,1)S(1)}, bf16[400,128]{1,0:T(8,128)(2,1)S(1)}, f32[16,128]{1,0:T(8,128)S(1)}, bf16[8,128,512]{2,1,0:T(8,128)(2,1)}) custom-call(bf16[128,4096]{1,0:T(8,128)(2,1)S(1)} %bitcast.15, bf16[400,4096]{1,0:T(8,128)(2,1)} %bitcast.23, bf16[8,400,768]{2,1,0:T(8,128)(2,1)} %bitcast.19, bf16[400,128]{1,0:T(8,128)(2,1)S(1)} %copy-done, ...), custom_call_target="tpu_custom_call" | custom-call | tf_op jit(solution)/shard_map/pallas_call | solution.py:342
  133.7 4.8 %all-to-all-start.1 = ((bf16[8,128,512]{2,1,0:T(8,128)(2,1)}), bf16[8,128,512]{2,1,0:T(8,128)(2,1)S(1)}, u32[]{:S(2)}, u32[]{:S(2)}) async-start(bf16[8,128,512]{2,1,0:T(8,128)(2,1)} %get-tuple-element.24), calls=%async_computation.1 | async-start | bytes 2097152 | tf_op jit(solution)/shard_map/all_to_all | solution.py:368
  138.5 23.3 %psum.7 = f32[16,128]{1,0:T(8,128)} all-reduce(f32[16,128]{1,0:T(8,128)S(1)} %get-tuple-element.23), channel_id=1, replica_groups=mesh['dp'=8,'y'=4,'zq'=4,'par'=2,'tensor'=4] {'tensor'}, use_global_device_ids=true, to_apply=%region_2.3 | all-reduce | flops 2048 | bytes 16384 | tf_op jit(solution)/shard_map/psum | solution.py:369
  161.8 0.0 all-to-all-done.1.rows_ref
  161.8 2.0 %shard_map.81 = bf16[400,640]{1,0:T(8,128)(2,1)S(1)} custom-call(bf16[8,400,768]{2,1,0:T(8,128)(2,1)} %bitcast.20, bf16[8,128,512]{2,1,0:T(8,128)(2,1)S(1)} %all-to-all-done.1.rows_ref, bf16[400,128]{1,0:T(8,128)(2,1)S(1)} %get-tuple-element.27.product_ref), custom_call_target="tpu_custom_call" | custom-call | flops 419430400 | bytes 2686976 | tf_op jit(solution)/shard_map/pallas_call | solution.py:378
  163.8 4.4 %collective-permute-start.1 = (bf16[400,640]{1,0:T(8,128)(2,1)S(1)}, bf16[400,640]{1,0:T(8,128)(2,1)S(1)}, u32[]{:S(2)}, u32[]{:S(2)}) collective-permute-start(bf16[400,640]{1,0:T(8,128)(2,1)S(1)} %shard_map.81), channel_id=1, source_target_pairs={{0,4},{4,0},{1,5},{5,1},{2,6},{6,2},{3,7},{7,3},{8,12},{12,8},{9,1... | collective-permute-start | bytes 1536008 | tf_op jit(solution)/shard_map/ppermute | solution.py:386
  168.2 0.1 iota_add_fusion
  168.3 5.3 %all-to-all-start.2 = ((f32[16,1,128]{2,1,0:T(1,128)}), f32[16,1,128]{2,1,0:T(1,128)S(1)}, u32[]{:S(2)}, u32[]{:S(2)}) async-start(f32[16,1,128]{2,1,0:T(1,128)} %bitcast.11), calls=%async_computation.2 | async-start | bytes 16384 | tf_op jit(solution)/shard_map/all_to_all | solution.py:407
  173.6 0.1 copy.20
  173.7 2.0 %shard_map.80.term_ref = f32[400,512]{1,0:T(8,128)S(1)} custom-call(bf16[8,400,768]{2,1,0:T(8,128)(2,1)} %bitcast.21, bf16[8,128,512]{2,1,0:T(8,128)(2,1)S(1)} %all-to-all-done.1.rows_ref), custom_call_target="tpu_custom_call" | custom-call | flops 419430400 | bytes 2686976 | tf_op jit(solution)/shard_map/pallas_call | solution.py:387
  175.7 2.6 %collective-permute-done.1.swapped_ref = bf16[400,640]{1,0:T(8,128)(2,1)S(1)} collective-permute-done((bf16[400,640]{1,0:T(8,128)(2,1)S(1)}, bf16[400,640]{1,0:T(8,128)(2,1)S(1)}, u32[]{:S(2)}, u32[]{:S(2)}) %collective-permute-start.1) | collective-permute-done | bytes 512032 | tf_op jit(solution)/shard_map/ppermute | solution.py:386
  178.3 1.1 shard_map.82
  179.4 5.9 %all-to-all-done.2 = f32[16,1,128]{2,1,0:T(1,128)S(1)} async-done(((f32[16,1,128]{2,1,0:T(1,128)}), f32[16,1,128]{2,1,0:T(1,128)S(1)}, u32[]{:S(2)}, u32[]{:S(2)}) %all-to-all-start.2) | async-done | bytes 8224 | tf_op jit(solution)/shard_map/all_to_all | solution.py:407
  185.4 0.4 select_reduce_fusion
  185.8 0.1 reshape.44
  185.9 0.7 copy.21
  (4 shorter events, 0.0 us)
Async XLA Ops:
  7.2 120.2 %all-gather.4.cloned.1.call-start = ((), (), s32[]{:S(2)}) async-start(), calls=%async_computation.3 | async-start | bytes 5529600 | tf_op jit(solution)/shard_map/all_gather | solution.py:327
  7.2 6.7 %copy-start.3 = (s32[56,2]{0,1:T(2,128)S(1)}, s32[56,2]{0,1:T(2,128)}, u32[]{:S(2)}) copy-start(s32[56,2]{0,1:T(2,128)} %param.7) | copy-start | bytes 1348
  7.2 7.4 %copy-start.1 = (bf16[14,4096]{1,0:T(8,128)(2,1)S(1)}, bf16[14,4096]{1,0:T(8,128)(2,1)}, u32[]{:S(2)}) copy-start(bf16[14,4096]{1,0:T(8,128)(2,1)} %cot_ref.1) | copy-start | bytes 344068
  7.2 7.4 %copy-start.2 = (f32[14,2]{0,1:T(2,128)S(1)}, f32[14,2]{0,1:T(2,128)}, u32[]{:S(2)}) copy-start(f32[14,2]{0,1:T(2,128)} %param.6) | copy-start | bytes 340
  10.0 15.7 %collective-permute-start = (bf16[400,640]{1,0:T(8,128)(2,1)}, bf16[400,640]{1,0:T(8,128)(2,1)S(1)}, u32[]{:S(2)}, u32[]{:S(2)}) collective-permute-start(bf16[400,640]{1,0:T(8,128)(2,1)} %get-tuple-element.19), channel_id=1, source_target_pairs={{0,4},{4,0},{1,5},{5,1},{2,6},{6,2},{3,7},{7,3},{8,12},{12,8},{9,1... | collective-permute-start | bytes 1536008 | tf_op jit(solution)/shard_map/ppermute | solution.py:315
  87.9 39.4 %copy-start = (bf16[400,128]{1,0:T(8,128)(2,1)S(1)}, bf16[400,128]{1,0:T(8,128)(2,1)}, u32[]{:S(2)}) copy-start(bf16[400,128]{1,0:T(8,128)(2,1)} %get-tuple-element.21.hidden_ref) | copy-start | bytes 307204
  133.7 28.1 %all-to-all-start.1 = ((bf16[8,128,512]{2,1,0:T(8,128)(2,1)}), bf16[8,128,512]{2,1,0:T(8,128)(2,1)S(1)}, u32[]{:S(2)}, u32[]{:S(2)}) async-start(bf16[8,128,512]{2,1,0:T(8,128)(2,1)} %get-tuple-element.24), calls=%async_computation.1 | async-start | bytes 2097152 | tf_op jit(solution)/shard_map/all_to_all | solution.py:368
  163.8 14.5 %collective-permute-start.1 = (bf16[400,640]{1,0:T(8,128)(2,1)S(1)}, bf16[400,640]{1,0:T(8,128)(2,1)S(1)}, u32[]{:S(2)}, u32[]{:S(2)}) collective-permute-start(bf16[400,640]{1,0:T(8,128)(2,1)S(1)} %shard_map.81), channel_id=1, source_target_pairs={{0,4},{4,0},{1,5},{5,1},{2,6},{6,2},{3,7},{7,3},{8,12},{12,8},{9,1... | collective-permute-start | bytes 1536008 | tf_op jit(solution)/shard_map/ppermute | solution.py:386
  168.3 17.1 %all-to-all-start.2 = ((f32[16,1,128]{2,1,0:T(1,128)}), f32[16,1,128]{2,1,0:T(1,128)S(1)}, u32[]{:S(2)}, u32[]{:S(2)}) async-start(f32[16,1,128]{2,1,0:T(1,128)} %bitcast.11), calls=%async_computation.2 | async-start | bytes 16384 | tf_op jit(solution)/shard_map/all_to_all | solution.py:407
Sparse Core Ops, SparseCore 0:
  27.7 58.4 all-gather.3

commit v9 on v8

--- a/solution.py
+++ b/solution.py
@@ -138,20 +138,15 @@
     return (natural == source).astype(jnp.bfloat16)
 
 
-def prepare_kernel(capacity, weight_ref, hidden_ref, send_ref, mine_ref, sem):
+def prepare_kernel(capacity, chunk_ref, hidden_ref, send_ref, mine_ref):
     rows = hidden_ref.shape[1]
-    chunk = send_ref.shape[1] - rows // 2
-    start = pl.multiple_of(lax.axis_index("dp") * chunk, chunk)
-    copy = pltpu.make_async_copy(
-        weight_ref.at[:, pl.ds(start, chunk)], send_ref.at[:, :chunk], sem
-    )
-    copy.start()
+    chunk = chunk_ref.shape[1]
+    send_ref[:, :chunk] = chunk_ref[...]
     order = parity_order(rows, capacity, True)
     moved = jnp.dot(hidden_ref[...], order, preferred_element_type=jnp.float32)
     moved = moved.astype(jnp.bfloat16)
     mine_ref[...] = moved[:, : rows // 2]
     send_ref[:, chunk:] = moved[:, rows // 2 :]
-    copy.wait()
 
 
 def product_kernel(
@@ -295,7 +290,6 @@
     chunk = model_width // n_dp
     half = experts * capacity
     swap = [(0, 1), (1, 0)]
-    large = pltpu.CompilerParams(vmem_limit_bytes=60 << 20)
     small = pltpu.CompilerParams(vmem_limit_bytes=16 << 20)
 
     weight = down_weight.T
@@ -303,15 +297,15 @@
     hbm = pl.BlockSpec(memory_space=pltpu.HBM)
     sent, hidden_mine = pl.pallas_call(
         functools.partial(prepare_kernel, capacity),
-        in_specs=[hbm, vmem],
-        out_specs=[vmem, vmem],
         out_shape=[
             jax.ShapeDtypeStruct((hidden_cols, chunk + half), jnp.bfloat16),
             jax.ShapeDtypeStruct((hidden_cols, half), jnp.bfloat16),
         ],
-        scratch_shapes=[pltpu.SemaphoreType.DMA],
-        compiler_params=large,
-    )(weight, saved_hidden.T)
+        compiler_params=small,
+    )(
+        lax.dynamic_slice_in_dim(weight, lax.axis_index("dp") * chunk, chunk, axis=1),
+        saved_hidden.T,
+    )
     swapped = lax.ppermute(sent, "par", swap)
     packed_width = model_width + PARTS * model_width // (PARTS + 1) + LANES
     packed = pl.pallas_call(

time: 194 us -> 192 us (0.990)
  local copies, waits for them, and re-layouts: 1.16 us -> 5.36 us
  Pallas kernels: 15.2 us -> 12.7 us
  waiting for transfers between devices: 19.5 us -> 17 us
  starting transfers between devices: 18.3 us -> 20.4 us
  blocking collectives: 122 us -> 120 us
    unnamed x11 -> x13, local copies, waits for them, and re-layouts: 0.87 us -> 4.04 us
    psum x1, blocking collectives: 23.3 us -> 20.5 us  [shards(): partial_value = lax.psum(partial_value, 'tensor')]
    pallas_call x1, Pallas kernels: 2.8 us -> 0.23 us  [shards(): pl.pallas_call(functools.partial(prepare_kernel, capacity), out_shape=[ja...]
    ppermute x2, starting transfers between devices: 8.2 us -> 10.6 us  [shards(): swapped = lax.ppermute(sent, 'par', swap)]
  transfers between devices with their start and end apart: 5 -> 5, of which waited for: 3 -> 3; matrix products, arithmetic and copies ran while one was open for 0% -> 1% of each run, Pallas kernels for 2% -> 2%
where the time goes in v9:
time: 192 us; the launch traced here: 191 us
  blocking collectives  120 us (62%)
  starting transfers between devices  20.4 us (11%)
  waiting for transfers between devices  17 us (9%)
  between operations  14.2 us (7%)
  Pallas kernels  12.7 us (7%)
  local copies, waits for them, and re-layouts  5.36 us (3%)
    all_gather x1, blocking collectives, shards(): gathered = lax.all_gather(packed, 'tensor', axis=0)  59.7 us
    all_to_all x1, blocking collectives, shards(): lax.all_to_all(buffer, every, split_axis=0, concat_axis=0, axis_index_gro...  39.9 us
    psum x1, blocking collectives, shards(): partial_value = lax.psum(partial_value, 'tensor')  20.5 us
    ppermute x2, waiting for transfers between devices, shards(): swapped = lax.ppermute(sent, 'par', swap)  12.6 us
    ppermute x2, starting transfers between devices, shards(): swapped = lax.ppermute(sent, 'par', swap)  10.6 us
    pallas_call x1, Pallas kernels, shards(): pl.pallas_call(functools.partial(product_kernel, capacity), grid=(1,), in...  6.33 us
    all_to_all x1, starting transfers between devices, shards(): lax.all_to_all(by_feature, 'dp', split_axis=0, concat_axis=0, tiled=True)  6.04 us
    all_to_all x1, waiting for transfers between devices, shards(): lax.all_to_all(partial_value, every, split_axis=0, concat_axis=0, axis_in...  4.35 us
  transfers between devices with their start and end apart: 5, of which 3 were waited for; matrix products, arithmetic and copies ran while one was open for 1% of the time, Pallas kernels for 2%

profile of v9, /device:TPU:6, one launch (start us, length us, event | category | flops | bytes accessed | tf_op | source)
XLA Modules:
  0.0 191.5 jit_solution(16644291801125788321)
XLA Ops:
  7.2 0.0 copy-start.4
  7.2 0.0 all-gather.4.cloned.1.call-start
  7.2 1.0 dynamic-slice_bitcast_fusion.chunk_ref
  8.3 0.0 copy-start
  8.3 0.9 copy-done
  9.2 0.2 shard_map.77
  9.4 3.8 %collective-permute-start = (bf16[400,640]{1,0:T(8,128)(2,1)S(1)}, bf16[400,640]{1,0:T(8,128)(2,1)S(1)}, u32[]{:S(2)}, u32[]{:S(2)}) collective-permute-start(bf16[400,640]{1,0:T(8,128)(2,1)S(1)} %get-tuple-element.19), channel_id=1, source_target_pairs={{0,4},{4,0},{1,5},{5,1},{2,6},{6,2},{3,7},{7,3},{8,12},{12,8},{9,1... | collective-permute-start | bytes 1536008 | tf_op jit(solution)/shard_map/ppermute | solution.py:309
  13.3 0.8 copy.18
  14.0 0.1 reshape.41
  14.2 0.1 fusion
  14.3 0.2 reduce_window_sum.11
  14.4 0.2 select_reduce_fusion.1
  14.6 0.1 dynamic_slice.7
  14.7 0.0 copy-start.1
  14.7 0.9 copy-done.1
  15.6 0.0 copy-start.2
  15.6 0.7 copy-done.2
  16.3 0.2 shard_map.76
  16.5 8.4 %collective-permute-done.hidden_theirs_ref = bf16[400,640]{1,0:T(8,128)(2,1)S(1)} collective-permute-done((bf16[400,640]{1,0:T(8,128)(2,1)S(1)}, bf16[400,640]{1,0:T(8,128)(2,1)S(1)}, u32[]{:S(2)}, u32[]{:S(2)}) %collective-permute-start) | collective-permute-done | bytes 512032 | tf_op jit(solution)/shard_map/ppermute | solution.py:309
  24.9 0.9 pad_maximum_fusion
  25.8 0.0 all-gather.4.cloned.1.call-update
  25.8 59.7 %all-gather.1 = bf16[32,7296]{1,0:T(8,128)(2,1)S(1)} all-gather(bf16[8,7296]{1,0:T(8,128)(2,1)S(1)} %shard_map.76), channel_id=3, replica_groups=mesh['dp'=8,'y'=4,'zq'=4,'par'=2,'tensor'=4] {'tensor'}, dimensions={0}, use_global_device_ids=true | all-gather | bytes 583680 | tf_op jit(solution)/shard_map/all_gather | solution.py:323
  85.5 0.0 copy-done.4
  85.5 0.8 shard_map.78
  86.3 39.9 %all_to_all.19 = bf16[16,8,4096]{2,1,0:T(8,128)(2,1)S(1)} all-to-all(bf16[16,8,4096]{2,1,0:T(8,128)(2,1)S(1)} %bitcast.16), channel_id=1, replica_groups={{0,8,16,24,32,40,48,56,64,72,80,88,96,104,112,120},{1,9,17,25,33,41,49,..., dimensions={0} | all-to-all | bytes 2097152 | tf_op jit(solution)/shard_map/all_to_all | solution.py:332
  126.1 0.0 all-gather.4.cloned.1.call-done
  126.1 6.3 %shard_map.79 = (bf16[400,128]{1,0:T(8,128)(2,1)S(1)}, bf16[400,128]{1,0:T(8,128)(2,1)S(1)}, f32[16,128]{1,0:T(8,128)S(1)}, bf16[8,128,512]{2,1,0:T(8,128)(2,1)}) custom-call(bf16[128,4096]{1,0:T(8,128)(2,1)S(1)} %bitcast.17, bf16[400,4096]{1,0:T(8,128)(2,1)} %bitcast.25, bf16[8,400,768]{2,1,0:T(8,128)(2,1)} %bitcast.22, ...), custom_call_target="tpu_custom_call" | custom-call | tf_op jit(solution)/shard_map/pallas_call | solution.py:336
  132.5 6.0 %all-to-all-start.1 = ((bf16[8,128,512]{2,1,0:T(8,128)(2,1)}), bf16[8,128,512]{2,1,0:T(8,128)(2,1)S(1)}, u32[]{:S(2)}, u32[]{:S(2)}) async-start(bf16[8,128,512]{2,1,0:T(8,128)(2,1)} %get-tuple-element.24), calls=%async_computation.1 | async-start | bytes 2097152 | tf_op jit(solution)/shard_map/all_to_all | solution.py:362
  138.5 20.5 %psum.7 = f32[16,128]{1,0:T(8,128)} all-reduce(f32[16,128]{1,0:T(8,128)S(1)} %get-tuple-element.23), channel_id=1, replica_groups=mesh['dp'=8,'y'=4,'zq'=4,'par'=2,'tensor'=4] {'tensor'}, use_global_device_ids=true, to_apply=%region_2.3 | all-reduce | flops 2048 | bytes 16384 | tf_op jit(solution)/shard_map/psum | solution.py:363
  159.0 0.0 all-to-all-done.1.rows_ref
  159.0 0.0 copy-start.3
  159.0 2.0 %shard_map.81 = bf16[400,640]{1,0:T(8,128)(2,1)S(1)} custom-call(bf16[8,400,768]{2,1,0:T(8,128)(2,1)} %bitcast.23, bf16[8,128,512]{2,1,0:T(8,128)(2,1)S(1)} %all-to-all-done.1.rows_ref, bf16[400,128]{1,0:T(8,128)(2,1)S(1)} %get-tuple-element.27.product_ref), custom_call_target="tpu_custom_call" | custom-call | flops 419430400 | bytes 2686976 | tf_op jit(solution)/shard_map/pallas_call | solution.py:372
  161.0 6.8 %collective-permute-start.1 = (bf16[400,640]{1,0:T(8,128)(2,1)S(1)}, bf16[400,640]{1,0:T(8,128)(2,1)S(1)}, u32[]{:S(2)}, u32[]{:S(2)}) collective-permute-start(bf16[400,640]{1,0:T(8,128)(2,1)S(1)} %shard_map.81), channel_id=1, source_target_pairs={{0,4},{4,0},{1,5},{5,1},{2,6},{6,2},{3,7},{7,3},{8,12},{12,8},{9,1... | collective-permute-start | bytes 1536008 | tf_op jit(solution)/shard_map/ppermute | solution.py:380
  167.9 0.1 iota_add_fusion
  168.0 3.7 %all-to-all-start.2 = ((f32[16,1,128]{2,1,0:T(1,128)}), f32[16,1,128]{2,1,0:T(1,128)S(1)}, u32[]{:S(2)}, u32[]{:S(2)}) async-start(f32[16,1,128]{2,1,0:T(1,128)} %bitcast.12), calls=%async_computation.2 | async-start | bytes 16384 | tf_op jit(solution)/shard_map/all_to_all | solution.py:401
  171.7 0.0 copy-done.3
  171.7 0.1 copy.20
  171.8 2.0 %shard_map.80.term_ref = f32[400,512]{1,0:T(8,128)S(1)} custom-call(bf16[8,400,768]{2,1,0:T(8,128)(2,1)} %bitcast.24, bf16[8,128,512]{2,1,0:T(8,128)(2,1)S(1)} %all-to-all-done.1.rows_ref), custom_call_target="tpu_custom_call" | custom-call | flops 419430400 | bytes 2686976 | tf_op jit(solution)/shard_map/pallas_call | solution.py:381
  173.8 4.2 %collective-permute-done.1.swapped_ref = bf16[400,640]{1,0:T(8,128)(2,1)S(1)} collective-permute-done((bf16[400,640]{1,0:T(8,128)(2,1)S(1)}, bf16[400,640]{1,0:T(8,128)(2,1)S(1)}, u32[]{:S(2)}, u32[]{:S(2)}) %collective-permute-start.1) | collective-permute-done | bytes 512032 | tf_op jit(solution)/shard_map/ppermute | solution.py:380
  178.0 1.1 shard_map.82
  179.1 4.4 %all-to-all-done.2 = f32[16,1,128]{2,1,0:T(1,128)S(1)} async-done(((f32[16,1,128]{2,1,0:T(1,128)}), f32[16,1,128]{2,1,0:T(1,128)S(1)}, u32[]{:S(2)}, u32[]{:S(2)}) %all-to-all-start.2) | async-done | bytes 8224 | tf_op jit(solution)/shard_map/all_to_all | solution.py:401
  183.4 0.4 select_reduce_fusion
  183.9 0.1 reshape.44
  184.0 0.7 copy.21
  (4 shorter events, 0.0 us)
Async XLA Ops:
  7.2 78.3 %copy-start.4 = (s32[56,2]{0,1:T(2,128)S(1)}, s32[56,2]{0,1:T(2,128)}, u32[]{:S(2)}) copy-start(s32[56,2]{0,1:T(2,128)} %param.7) | copy-start | bytes 1348
  7.2 119.0 %all-gather.4.cloned.1.call-start = ((), (), s32[]{:S(2)}) async-start(), calls=%async_computation.3 | async-start | bytes 5529600 | tf_op jit(solution)/shard_map/all_gather | solution.py:321
  8.3 0.9 copy-start
  9.4 15.5 %collective-permute-start = (bf16[400,640]{1,0:T(8,128)(2,1)S(1)}, bf16[400,640]{1,0:T(8,128)(2,1)S(1)}, u32[]{:S(2)}, u32[]{:S(2)}) collective-permute-start(bf16[400,640]{1,0:T(8,128)(2,1)S(1)} %get-tuple-element.19), channel_id=1, source_target_pairs={{0,4},{4,0},{1,5},{5,1},{2,6},{6,2},{3,7},{7,3},{8,12},{12,8},{9,1... | collective-permute-start | bytes 1536008 | tf_op jit(solution)/shard_map/ppermute | solution.py:309
  14.7 0.9 copy-start.1
  15.6 0.7 copy-start.2
  132.5 26.5 %all-to-all-start.1 = ((bf16[8,128,512]{2,1,0:T(8,128)(2,1)}), bf16[8,128,512]{2,1,0:T(8,128)(2,1)S(1)}, u32[]{:S(2)}, u32[]{:S(2)}) async-start(bf16[8,128,512]{2,1,0:T(8,128)(2,1)} %get-tuple-element.24), calls=%async_computation.1 | async-start | bytes 2097152 | tf_op jit(solution)/shard_map/all_to_all | solution.py:362
  159.0 12.7 %copy-start.3 = (f32[14,2]{0,1:T(2,128)S(1)}, f32[14,2]{0,1:T(2,128)}, u32[]{:S(2)}) copy-start(f32[14,2]{0,1:T(2,128)} %param.6) | copy-start | bytes 340
  161.0 16.9 %collective-permute-start.1 = (bf16[400,640]{1,0:T(8,128)(2,1)S(1)}, bf16[400,640]{1,0:T(8,128)(2,1)S(1)}, u32[]{:S(2)}, u32[]{:S(2)}) collective-permute-start(bf16[400,640]{1,0:T(8,128)(2,1)S(1)} %shard_map.81), channel_id=1, source_target_pairs={{0,4},{4,0},{1,5},{5,1},{2,6},{6,2},{3,7},{7,3},{8,12},{12,8},{9,1... | collective-permute-start | bytes 1536008 | tf_op jit(solution)/shard_map/ppermute | solution.py:380
  168.0 15.5 %all-to-all-start.2 = ((f32[16,1,128]{2,1,0:T(1,128)}), f32[16,1,128]{2,1,0:T(1,128)S(1)}, u32[]{:S(2)}, u32[]{:S(2)}) async-start(f32[16,1,128]{2,1,0:T(1,128)} %bitcast.12), calls=%async_computation.2 | async-start | bytes 16384 | tf_op jit(solution)/shard_map/all_to_all | solution.py:401
Sparse Core Ops, SparseCore 0:
  25.9 58.4 all-gather.3

commit v10 on v9

--- a/solution.py
+++ b/solution.py
@@ -138,15 +138,13 @@
     return (natural == source).astype(jnp.bfloat16)
 
 
-def prepare_kernel(capacity, chunk_ref, hidden_ref, send_ref, mine_ref):
+def sort_kernel(capacity, hidden_ref, mine_ref, send_ref):
     rows = hidden_ref.shape[1]
-    chunk = chunk_ref.shape[1]
-    send_ref[:, :chunk] = chunk_ref[...]
     order = parity_order(rows, capacity, True)
     moved = jnp.dot(hidden_ref[...], order, preferred_element_type=jnp.float32)
     moved = moved.astype(jnp.bfloat16)
     mine_ref[...] = moved[:, : rows // 2]
-    send_ref[:, chunk:] = moved[:, rows // 2 :]
+    send_ref[...] = moved[:, rows // 2 :]
 
 
 def product_kernel(
@@ -295,18 +293,14 @@
     weight = down_weight.T
     vmem = pl.BlockSpec(memory_space=pltpu.VMEM)
     hbm = pl.BlockSpec(memory_space=pltpu.HBM)
-    sent, hidden_mine = pl.pallas_call(
-        functools.partial(prepare_kernel, capacity),
-        out_shape=[
-            jax.ShapeDtypeStruct((hidden_cols, chunk + half), jnp.bfloat16),
-            jax.ShapeDtypeStruct((hidden_cols, half), jnp.bfloat16),
-        ],
+    weight_sent = lax.dynamic_slice_in_dim(weight, lax.axis_index("dp") * chunk, chunk, axis=1)
+    weight_swapped = lax.ppermute(weight_sent, "par", swap)
+    hidden_mine, hidden_sent = pl.pallas_call(
+        functools.partial(sort_kernel, capacity),
+        out_shape=[jax.ShapeDtypeStruct((hidden_cols, half), jnp.bfloat16)] * 2,
         compiler_params=small,
-    )(
-        lax.dynamic_slice_in_dim(weight, lax.axis_index("dp") * chunk, chunk, axis=1),
-        saved_hidden.T,
-    )
-    swapped = lax.ppermute(sent, "par", swap)
+    )(saved_hidden.T)
+    hidden_theirs = lax.ppermute(hidden_sent, "par", swap)
     packed_width = model_width + PARTS * model_width // (PARTS + 1) + LANES
     packed = pl.pallas_call(
         pack_kernel,
@@ -317,8 +311,11 @@
     keys = flat_ids * capacity + assign_slots(flat_ids, experts)
     start_row = lax.axis_index("tensor") * (own_tokens * 2)
     own_keys = lax.dynamic_slice_in_dim(keys, start_row, own_tokens * 2)
-    packed, swapped, own_keys = lax.optimization_barrier((packed, swapped, own_keys))
-    prefetched = lax.all_gather(jnp.concatenate([swapped, hidden_mine], axis=1), "dp", axis=0)
+    packed, weight_swapped, hidden_theirs, own_keys = lax.optimization_barrier(
+        (packed, weight_swapped, hidden_theirs, own_keys)
+    )
+    fetched = jnp.concatenate([weight_swapped, hidden_theirs, hidden_mine], axis=1)
+    prefetched = lax.all_gather(fetched, "dp", axis=0)
 
     gathered = lax.all_gather(packed, "tensor", axis=0)
     buffer = pl.pallas_call(
@@ -341,7 +338,7 @@
             hbm,
             hbm,
             vmem,
-            pl.BlockSpec((hidden_cols, half), lambda i: (0, chunk // half)),
+            vmem,
         ],
         out_specs=[vmem] * 4,
         out_shape=[
@@ -357,7 +354,7 @@
             pltpu.SemaphoreType.DMA((2, 4)),
         ],
         compiler_params=pltpu.CompilerParams(vmem_limit_bytes=50 << 20),
-    )(rows, weight, prefetched, hidden_mine, swapped)
+    )(rows, weight, prefetched, hidden_mine, hidden_theirs)
 
     replica_rows = lax.all_to_all(by_feature, "dp", split_axis=0, concat_axis=0, tiled=True)
     partial_value = lax.psum(partial_value, "tensor")

time: 192 us -> 191 us (level)
  blocking collectives: 120 us -> 122 us
    ppermute x2 -> x1, waiting for transfers between devices: 12.6 us -> 2.59 us  [shards(): swapped = lax.ppermute(sent, 'par', swap)]
    ppermute x0 -> x2, waiting for transfers between devices: none -> 6.82 us  [the longest x1 6.81 us: shards(): hidden_theirs = lax.ppermute(hidden_sent, 'par', swap)]
    ppermute x2 -> x1, starting transfers between devices: 10.6 us -> 4.37 us  [shards(): swapped = lax.ppermute(sent, 'par', swap)]
    ppermute x0 -> x2, starting transfers between devices: none -> 5.85 us  [the longest x1 3.83 us: shards(): weight_swapped = lax.ppermute(weight_sent, 'par', swap)]
    psum x1, blocking collectives: 20.5 us -> 23.4 us  [shards(): partial_value = lax.psum(partial_value, 'tensor')]
    unnamed x13 -> x11, local copies, waits for them, and re-layouts: 4.04 us -> 2.46 us
  transfers between devices with their start and end apart: 5 -> 6, of which waited for: 3 -> 3; matrix products, arithmetic and copies ran while one was open for 1% -> 1% of each run, Pallas kernels for 2% -> 2%
where the time goes in v10:
time: 191 us; the launch traced here: 190 us
  blocking collectives  122 us (64%)
  starting transfers between devices  20.3 us (11%)
  waiting for transfers between devices  15.4 us (8%)
  between operations  14.2 us (7%)
  Pallas kernels  12.7 us (7%)
  local copies, waits for them, and re-layouts  3.81 us (2%)
    all_gather x1, blocking collectives, shards(): gathered = lax.all_gather(packed, 'tensor', axis=0)  59.6 us
    all_to_all x1, blocking collectives, shards(): lax.all_to_all(buffer, every, split_axis=0, concat_axis=0, axis_index_gro...  39.3 us
    psum x1, blocking collectives, shards(): partial_value = lax.psum(partial_value, 'tensor')  23.4 us
    ppermute x1, waiting for transfers between devices, shards(): hidden_theirs = lax.ppermute(hidden_sent, 'par', swap)  6.81 us
    pallas_call x1, Pallas kernels, shards(): pl.pallas_call(functools.partial(product_kernel, capacity), grid=(1,), in...  6.32 us
    all_to_all x1, waiting for transfers between devices, shards(): lax.all_to_all(partial_value, every, split_axis=0, concat_axis=0, axis_in...  5.98 us
    all_to_all x1, starting transfers between devices, shards(): lax.all_to_all(partial_value, every, split_axis=0, concat_axis=0, axis_in...  5.31 us
    all_to_all x1, starting transfers between devices, shards(): lax.all_to_all(by_feature, 'dp', split_axis=0, concat_axis=0, tiled=True)  4.77 us
  transfers between devices with their start and end apart: 6, of which 3 were waited for; matrix products, arithmetic and copies ran while one was open for 1% of the time, Pallas kernels for 2%

profile of v10, /device:TPU:6, one launch (start us, length us, event | category | flops | bytes accessed | tf_op | source)
XLA Modules:
  0.0 190.5 jit_solution(15958010737325648522)
XLA Ops:
  7.2 0.0 copy-start.2
  7.2 0.0 copy-start.1
  7.2 0.0 all-gather.4.cloned.1.call-start
  7.2 1.1 dynamic-slice_bitcast_fusion
  8.3 3.8 %collective-permute-start = (bf16[400,512]{1,0:T(8,128)(2,1)S(1)}, bf16[400,512]{1,0:T(8,128)(2,1)S(1)}, u32[]{:S(2)}, u32[]{:S(2)}) collective-permute-start(bf16[400,512]{1,0:T(8,128)(2,1)S(1)} %dynamic-slice_bitcast_fusion), channel_id=1, source_target_pairs={{0,4},{4,0},{1,5},{5,1},{2,6},{6,2},{3,7},{7,3},{8,12},{12,8},{9,1... | collective-permute-start | bytes 1228808 | tf_op jit(solution)/shard_map/ppermute | solution.py:297
  12.1 0.0 copy-start
  12.1 0.9 copy-done
  13.1 0.2 shard_map.77
  13.3 2.0 %collective-permute-start.1 = (bf16[400,128]{1,0:T(8,128)(2,1)S(1)}, bf16[400,128]{1,0:T(8,128)(2,1)S(1)}, u32[]{:S(2)}, u32[]{:S(2)}) collective-permute-start(bf16[400,128]{1,0:T(8,128)(2,1)S(1)} %get-tuple-element.20), channel_id=1, source_target_pairs={{0,4},{4,0},{1,5},{5,1},{2,6},{6,2},{3,7},{7,3},{8,12},{12,8},{9,1... | collective-permute-start | bytes 307208 | tf_op jit(solution)/shard_map/ppermute | solution.py:303
  15.3 0.8 copy.18
  16.1 0.1 reshape.41
  16.2 0.1 fusion
  16.3 0.2 reduce_window_sum.11
  16.5 0.2 select_reduce_fusion.1
  16.7 0.1 dynamic_slice.7
  16.7 0.0 copy-done.2
  16.7 0.0 copy-done.1
  16.8 0.2 shard_map.76
  17.0 0.0 copy-start.3
  17.0 6.8 %collective-permute-done.1.hidden_theirs_ref = bf16[400,128]{1,0:T(8,128)(2,1)S(1)} collective-permute-done((bf16[400,128]{1,0:T(8,128)(2,1)S(1)}, bf16[400,128]{1,0:T(8,128)(2,1)S(1)}, u32[]{:S(2)}, u32[]{:S(2)}) %collective-permute-start.1) | collective-permute-done | bytes 102432 | tf_op jit(solution)/shard_map/ppermute | solution.py:303
  23.8 0.0 collective-permute-done
  23.8 0.9 pad_maximum_fusion
  24.6 0.0 all-gather.4.cloned.1.call-update
  24.7 59.6 %all-gather.1 = bf16[32,7296]{1,0:T(8,128)(2,1)S(1)} all-gather(bf16[8,7296]{1,0:T(8,128)(2,1)S(1)} %shard_map.76), channel_id=3, replica_groups=mesh['dp'=8,'y'=4,'zq'=4,'par'=2,'tensor'=4] {'tensor'}, dimensions={0}, use_global_device_ids=true | all-gather | bytes 583680 | tf_op jit(solution)/shard_map/all_gather | solution.py:320
  84.3 0.0 copy-done.3
  84.3 0.8 shard_map.78
  85.1 39.3 %all_to_all.19 = bf16[16,8,4096]{2,1,0:T(8,128)(2,1)S(1)} all-to-all(bf16[16,8,4096]{2,1,0:T(8,128)(2,1)S(1)} %bitcast.16), channel_id=1, replica_groups={{0,8,16,24,32,40,48,56,64,72,80,88,96,104,112,120},{1,9,17,25,33,41,49,..., dimensions={0} | all-to-all | bytes 2097152 | tf_op jit(solution)/shard_map/all_to_all | solution.py:329
  124.3 0.0 all-gather.4.cloned.1.call-done
  124.3 6.3 %shard_map.79 = (bf16[400,128]{1,0:T(8,128)(2,1)S(1)}, bf16[400,128]{1,0:T(8,128)(2,1)S(1)}, f32[16,128]{1,0:T(8,128)S(1)}, bf16[8,128,512]{2,1,0:T(8,128)(2,1)}) custom-call(bf16[128,4096]{1,0:T(8,128)(2,1)S(1)} %bitcast.17, bf16[400,4096]{1,0:T(8,128)(2,1)} %bitcast.25, bf16[8,400,768]{2,1,0:T(8,128)(2,1)} %bitcast.22, ...), custom_call_target="tpu_custom_call" | custom-call | tf_op jit(solution)/shard_map/pallas_call | solution.py:333
  130.7 4.8 %all-to-all-start.1 = ((bf16[8,128,512]{2,1,0:T(8,128)(2,1)}), bf16[8,128,512]{2,1,0:T(8,128)(2,1)S(1)}, u32[]{:S(2)}, u32[]{:S(2)}) async-start(bf16[8,128,512]{2,1,0:T(8,128)(2,1)} %get-tuple-element.26), calls=%async_computation.1 | async-start | bytes 2097152 | tf_op jit(solution)/shard_map/all_to_all | solution.py:359
  135.4 23.4 %psum.7 = f32[16,128]{1,0:T(8,128)} all-reduce(f32[16,128]{1,0:T(8,128)S(1)} %get-tuple-element.25), channel_id=1, replica_groups=mesh['dp'=8,'y'=4,'zq'=4,'par'=2,'tensor'=4] {'tensor'}, use_global_device_ids=true, to_apply=%region_2.3 | all-reduce | flops 2048 | bytes 16384 | tf_op jit(solution)/shard_map/psum | solution.py:360
  158.8 0.0 all-to-all-done.1.rows_ref
  158.8 2.0 %shard_map.81 = bf16[400,640]{1,0:T(8,128)(2,1)S(1)} custom-call(bf16[8,400,768]{2,1,0:T(8,128)(2,1)} %bitcast.23, bf16[8,128,512]{2,1,0:T(8,128)(2,1)S(1)} %all-to-all-done.1.rows_ref, bf16[400,128]{1,0:T(8,128)(2,1)S(1)} %get-tuple-element.29.product_ref), custom_call_target="tpu_custom_call" | custom-call | flops 419430400 | bytes 2686976 | tf_op jit(solution)/shard_map/pallas_call | solution.py:369
  160.8 4.4 %collective-permute-start.2 = (bf16[400,640]{1,0:T(8,128)(2,1)S(1)}, bf16[400,640]{1,0:T(8,128)(2,1)S(1)}, u32[]{:S(2)}, u32[]{:S(2)}) collective-permute-start(bf16[400,640]{1,0:T(8,128)(2,1)S(1)} %shard_map.81), channel_id=1, source_target_pairs={{0,4},{4,0},{1,5},{5,1},{2,6},{6,2},{3,7},{7,3},{8,12},{12,8},{9,1... | collective-permute-start | bytes 1536008 | tf_op jit(solution)/shard_map/ppermute | solution.py:377
  165.2 0.1 iota_add_fusion
  165.3 5.3 %all-to-all-start.2 = ((f32[16,1,128]{2,1,0:T(1,128)}), f32[16,1,128]{2,1,0:T(1,128)S(1)}, u32[]{:S(2)}, u32[]{:S(2)}) async-start(f32[16,1,128]{2,1,0:T(1,128)} %bitcast.12), calls=%async_computation.2 | async-start | bytes 16384 | tf_op jit(solution)/shard_map/all_to_all | solution.py:398
  170.6 0.1 copy.20
  170.7 2.0 %shard_map.80.term_ref = f32[400,512]{1,0:T(8,128)S(1)} custom-call(bf16[8,400,768]{2,1,0:T(8,128)(2,1)} %bitcast.24, bf16[8,128,512]{2,1,0:T(8,128)(2,1)S(1)} %all-to-all-done.1.rows_ref), custom_call_target="tpu_custom_call" | custom-call | flops 419430400 | bytes 2686976 | tf_op jit(solution)/shard_map/pallas_call | solution.py:378
  172.8 2.6 %collective-permute-done.2.swapped_ref = bf16[400,640]{1,0:T(8,128)(2,1)S(1)} collective-permute-done((bf16[400,640]{1,0:T(8,128)(2,1)S(1)}, bf16[400,640]{1,0:T(8,128)(2,1)S(1)}, u32[]{:S(2)}, u32[]{:S(2)}) %collective-permute-start.2) | collective-permute-done | bytes 512032 | tf_op jit(solution)/shard_map/ppermute | solution.py:377
  175.3 1.1 shard_map.82
  176.4 6.0 %all-to-all-done.2 = f32[16,1,128]{2,1,0:T(1,128)S(1)} async-done(((f32[16,1,128]{2,1,0:T(1,128)}), f32[16,1,128]{2,1,0:T(1,128)S(1)}, u32[]{:S(2)}, u32[]{:S(2)}) %all-to-all-start.2) | async-done | bytes 8224 | tf_op jit(solution)/shard_map/all_to_all | solution.py:398
  182.4 0.4 select_reduce_fusion
  182.9 0.1 reshape.44
  183.0 0.7 copy.21
  (4 shorter events, 0.0 us)
Async XLA Ops:
  7.2 9.6 %copy-start.2 = (f32[14,2]{0,1:T(2,128)S(1)}, f32[14,2]{0,1:T(2,128)}, u32[]{:S(2)}) copy-start(f32[14,2]{0,1:T(2,128)} %param.6) | copy-start | bytes 340
  7.2 9.6 %copy-start.1 = (bf16[14,4096]{1,0:T(8,128)(2,1)S(1)}, bf16[14,4096]{1,0:T(8,128)(2,1)}, u32[]{:S(2)}) copy-start(bf16[14,4096]{1,0:T(8,128)(2,1)} %cot_ref.1) | copy-start | bytes 344068
  7.2 117.2 %all-gather.4.cloned.1.call-start = ((), (), s32[]{:S(2)}) async-start(), calls=%async_computation.3 | async-start | bytes 5529600 | tf_op jit(solution)/shard_map/all_gather | solution.py:318
  8.3 15.5 %collective-permute-start = (bf16[400,512]{1,0:T(8,128)(2,1)S(1)}, bf16[400,512]{1,0:T(8,128)(2,1)S(1)}, u32[]{:S(2)}, u32[]{:S(2)}) collective-permute-start(bf16[400,512]{1,0:T(8,128)(2,1)S(1)} %dynamic-slice_bitcast_fusion), channel_id=1, source_target_pairs={{0,4},{4,0},{1,5},{5,1},{2,6},{6,2},{3,7},{7,3},{8,12},{12,8},{9,1... | collective-permute-start | bytes 1228808 | tf_op jit(solution)/shard_map/ppermute | solution.py:297
  12.1 0.9 copy-start
  13.3 10.5 %collective-permute-start.1 = (bf16[400,128]{1,0:T(8,128)(2,1)S(1)}, bf16[400,128]{1,0:T(8,128)(2,1)S(1)}, u32[]{:S(2)}, u32[]{:S(2)}) collective-permute-start(bf16[400,128]{1,0:T(8,128)(2,1)S(1)} %get-tuple-element.20), channel_id=1, source_target_pairs={{0,4},{4,0},{1,5},{5,1},{2,6},{6,2},{3,7},{7,3},{8,12},{12,8},{9,1... | collective-permute-start | bytes 307208 | tf_op jit(solution)/shard_map/ppermute | solution.py:303
  17.0 67.3 %copy-start.3 = (s32[56,2]{0,1:T(2,128)S(1)}, s32[56,2]{0,1:T(2,128)}, u32[]{:S(2)}) copy-start(s32[56,2]{0,1:T(2,128)} %param.7) | copy-start | bytes 1348
  130.7 28.1 %all-to-all-start.1 = ((bf16[8,128,512]{2,1,0:T(8,128)(2,1)}), bf16[8,128,512]{2,1,0:T(8,128)(2,1)S(1)}, u32[]{:S(2)}, u32[]{:S(2)}) async-start(bf16[8,128,512]{2,1,0:T(8,128)(2,1)} %get-tuple-element.26), calls=%async_computation.1 | async-start | bytes 2097152 | tf_op jit(solution)/shard_map/all_to_all | solution.py:359
  160.8 14.5 %collective-permute-start.2 = (bf16[400,640]{1,0:T(8,128)(2,1)S(1)}, bf16[400,640]{1,0:T(8,128)(2,1)S(1)}, u32[]{:S(2)}, u32[]{:S(2)}) collective-permute-start(bf16[400,640]{1,0:T(8,128)(2,1)S(1)} %shard_map.81), channel_id=1, source_target_pairs={{0,4},{4,0},{1,5},{5,1},{2,6},{6,2},{3,7},{7,3},{8,12},{12,8},{9,1... | collective-permute-start | bytes 1536008 | tf_op jit(solution)/shard_map/ppermute | solution.py:377
  165.3 17.1 %all-to-all-start.2 = ((f32[16,1,128]{2,1,0:T(1,128)}), f32[16,1,128]{2,1,0:T(1,128)S(1)}, u32[]{:S(2)}, u32[]{:S(2)}) async-start(f32[16,1,128]{2,1,0:T(1,128)} %bitcast.12), calls=%async_computation.2 | async-start | bytes 16384 | tf_op jit(solution)/shard_map/all_to_all | solution.py:398
Sparse Core Ops, SparseCore 0:
  24.8 58.4 all-gather.3
